TPU v7x, 256 devices: a whole 4x4x8 slice. The times are simulated.
256 devices in a mesh: ctx: 16 (over z_hi, x, core), tp: 16 (over y, z_lo).
Axes of the slice: x: 4, y: 4, z: 8 (z_hi: 2, z_lo: 4; z = z_hi * 4 + z_lo), core: 2. Of those that a mesh axis runs over, the one named last changes fastest.
Arguments:
- hidden: bfloat16 [8192, 8192], P('ctx'), may hold values from -8 to 8
- norm_gain: bfloat16 [8192], replicated, may hold values from 0.099609375 to 1.8984375
- trainer_query: bfloat16 [16, 8192, 256], P('tp', 'ctx'), may hold values from -1 to 1
- trainer_query_bias: bfloat16 [16, 256], P('tp'), may hold values from -3 to 3
- trainer_kv: bfloat16 [4, 8192, 256], P(None, 'ctx'), may hold values from -1 to 1
- trainer_kv_bias: bfloat16 [4, 256], replicated, may hold values from -3 to 3
- matching: int32 [16], replicated, may hold values from 0 to 15, as said below
- block_lists: int32 [32, 17], P('ctx'), may hold values from -1 to 31, as said below
- completion_lengths: int32 [16], replicated, may hold values from 1 to 256, as said below
Outputs:
- attended: bfloat16 [8192, 4096], P('ctx', 'tp')
Inputs may be any that keep to these rules, and one draw needn't show every extreme that they name: `matching`: each number of 0 to 15 once. `block_lists`: row b < 16 lists blocks 0 to b; row 16 + c lists prefix blocks 0 to k - 1 for some k of 1 to 16, then block 16 + c; entries rise, the rest is -1; some row has 17 entries. `completion_lengths`: some completion has 256 live tokens.
All inputs are finite; a program needn't handle non-finite values.
Results may differ from a plain program's by a relative error of at most 0.0087.
Values may be sent and summed in bfloat16 or wider, within the bound.
No kernel may reach another device: no remote copies, remote signals or barrier semaphores. Data moves between devices by JAX's collectives and lax.ppermute only.
A program may use at most 64 MiB of HBM per device.

v0:
```python
import functools
import math

import jax
import jax.numpy as jnp
from jax import lax
from jax.experimental import pallas as pl
from jax.experimental.pallas import tpu as pltpu
from jax.sharding import Mesh, PartitionSpec as P

BLK = 256
THETA = 1000000.0
EPSILON = 1e-06
BF = jnp.bfloat16
F32 = jnp.float32
ZH, X, CORE, Y, ZL = "zh", "x", "core", "y", "zl"


def full(shape):
    zeros = (0,) * len(shape)
    return pl.BlockSpec(shape, lambda *_: zeros)


CHEAP = pl.CostEstimate(flops=0, bytes_accessed=0, transcendentals=0)
SIX_US = pl.CostEstimate(flops=0, bytes_accessed=20 << 20, transcendentals=0)
HBM = pl.BlockSpec(memory_space=pltpu.HBM)
VMEM_LIMIT = 40 << 20
VMEM_MOST = 60 << 20


THREE_US = pl.CostEstimate(flops=0, bytes_accessed=10 << 20, transcendentals=0)


def norm_kernel(order, h_ref, g_ref, near_ref, far_ref):
    parts, step, width = near_ref.shape

    def square(k, total):
        piece = h_ref[:, pl.ds(pl.multiple_of(k * width, width), width)].astype(F32)
        return total + piece * piece

    total = lax.fori_loop(0, 2 * parts, square, jnp.zeros((step, width), F32), unroll=4)
    mean = jnp.sum(total, axis=1, keepdims=True) * (1.0 / (2 * parts * width))
    rs = lax.rsqrt(mean + EPSILON)
    for half, o_ref in ((0, near_ref), (parts, far_ref)):

        def scale(k, carry):
            off = pl.multiple_of(order[half + k] * width, width)
            piece = h_ref[:, pl.ds(off, width)].astype(F32)
            gain = g_ref[:, pl.ds(off, width)].astype(F32)
            o_ref[k] = (piece * rs * gain).astype(BF)
            return carry

        lax.fori_loop(0, parts, scale, 0, unroll=4)


def norm(hidden, gain, order):
    rows, d = hidden.shape
    parts = 8
    width = d // parts // 2
    step = 64
    block = pl.BlockSpec((parts, step, width), lambda i, o: (0, i, 0))
    return pl.pallas_call(
        norm_kernel,
        grid_spec=pltpu.PrefetchScalarGridSpec(
            num_scalar_prefetch=1,
            grid=(rows // step,),
            in_specs=[
                pl.BlockSpec((step, d), lambda i, o: (i, 0)),
                pl.BlockSpec((1, d), lambda i, o: (0, 0)),
            ],
            out_specs=[block, block],
        ),
        out_shape=[jax.ShapeDtypeStruct((parts, rows, width), BF)] * 2,
        compiler_params=pltpu.CompilerParams(vmem_limit_bytes=VMEM_LIMIT),
        cost_estimate=SIX_US,
        name="norm",
    )(order, hidden, gain.reshape(1, d))


def fetch(n_refs, ks, nbuf, nsem, w_refs, wbuf, wsem):
    per = len(ks) // len(w_refs)
    for i, w_ref in enumerate(w_refs):
        pltpu.make_async_copy(w_ref, wbuf.at[i], wsem.at[i]).start()
        for j in range(i * per, (i + 1) * per):
            for t, n_ref in enumerate(n_refs):
                pltpu.make_async_copy(n_ref.at[ks[j]], nbuf.at[t, j], nsem.at[t, j]).start()


def kv_kernel(near_ref, far_ref, *refs):
    w_refs = refs[:4]
    own_ref, other_ref, nbuf, wbuf, left, right, nsem, wsem = refs[4:]
    fetch((near_ref, far_ref), (0, 4, 1, 5, 2, 6, 3, 7), nbuf, nsem, w_refs, wbuf, wsem)
    left[...] = jnp.zeros_like(left)
    right[...] = jnp.zeros_like(right)

    def step(i, carry):
        pltpu.make_async_copy(w_refs[0], wbuf.at[i], wsem.at[i]).wait()
        w0, w1 = wbuf[i, :256, :], wbuf[i, 256:, :]
        for t in range(2):
            for r in range(2):
                pltpu.make_async_copy(near_ref.at[0], nbuf.at[t, 2 * i + r], nsem.at[t, 2 * i + r]).wait()
            n0, n1 = nbuf.at[t, 2 * i], nbuf.at[t, 2 * i + 1]
            left[t] += jnp.dot(n0[:, :256], w0, preferred_element_type=F32) + jnp.dot(
                n1[:, :256], w1, preferred_element_type=F32
            )
            right[t] += jnp.dot(n0[:, 256:], w0, preferred_element_type=F32) + jnp.dot(
                n1[:, 256:], w1, preferred_element_type=F32
            )
        return carry

    lax.fori_loop(0, 4, step, 0)
    for t, o_ref in ((0, own_ref), (1, other_ref)):
        o_ref[...] = left[t].T[:64] + right[t].T[64:]


def kv_project(near, far, pieces):
    parts, rows, width = near.shape
    return pl.pallas_call(
        kv_kernel,
        in_specs=[HBM] * 6,
        out_specs=[full((64, rows))] * 2,
        out_shape=[jax.ShapeDtypeStruct((64, rows), F32)] * 2,
        scratch_shapes=[
            pltpu.VMEM((2, parts, rows, width), BF),
            pltpu.VMEM((4, 512, 128), BF),
            pltpu.VMEM((2, rows, 128), F32),
            pltpu.VMEM((2, rows, 128), F32),
            pltpu.SemaphoreType.DMA((2, 8)),
            pltpu.SemaphoreType.DMA((4,)),
        ],
        compiler_params=pltpu.CompilerParams(vmem_limit_bytes=VMEM_MOST),
        cost_estimate=SIX_US,
        name="kv_project",
    )(near, far, *pieces)


def kv_finish_kernel(one_ref, two_ref, bias_ref, cos_ref, sin_ref, o_ref):
    kv = one_ref[...] + two_ref[...] + bias_ref[:, :1]
    first, second = kv[:16], kv[16:32]
    cos, sin = cos_ref[...], sin_ref[...]
    o_ref[0:16] = (first * cos - second * sin).astype(BF)
    o_ref[16:32] = (second * cos + first * sin).astype(BF)
    o_ref[32:64] = kv[32:64].astype(BF)


def kv_finish(one, two, bias, cos, sin):
    inputs = [one, two, bias, cos, sin]
    return pl.pallas_call(
        kv_finish_kernel,
        in_specs=[full(v.shape) for v in inputs],
        out_specs=full(one.shape),
        out_shape=jax.ShapeDtypeStruct(one.shape, BF),
        compiler_params=pltpu.CompilerParams(vmem_limit_bytes=8 << 20),
        cost_estimate=CHEAP,
        name="kv_finish",
    )(*inputs)


def q_kernel(first, near_ref, far_ref, *refs):
    w_refs, refs = refs[:4], refs[4:]
    if first:
        so_far, refs = refs[:2], refs[2:]
    own_ref, other_ref, nbuf, wbuf, nsem, wsem = refs
    fetch((near_ref, far_ref), range(first, first + 4), nbuf, nsem, w_refs, wbuf, wsem)
    for t, o_ref in ((0, own_ref), (1, other_ref)):
        o_ref[...] = so_far[t][...] if first else jnp.zeros_like(o_ref)

    def step(i, carry):
        for r in range(2):
            pltpu.make_async_copy(w_refs[0], wbuf.at[2 * i + r], wsem.at[2 * i + r]).wait()
        for t, o_ref in ((0, own_ref), (1, other_ref)):
            out = None
            for r in range(2):
                k = 2 * i + r
                pltpu.make_async_copy(near_ref.at[0], nbuf.at[t, k], nsem.at[t, k]).wait()
                part = jnp.dot(nbuf[t, k], wbuf[k], preferred_element_type=F32)
                out = part if out is None else out + part
            o_ref[...] += out
        return carry

    lax.fori_loop(0, 2, step, 0)


def q_project(first, near, far, pieces, so_far):
    parts, rows, width = near.shape
    shape = jax.ShapeDtypeStruct((rows, 256), F32)
    return pl.pallas_call(
        functools.partial(q_kernel, first),
        in_specs=[HBM] * 6 + [full(shape.shape)] * len(so_far),
        out_specs=[full(shape.shape)] * 2,
        out_shape=[shape] * 2,
        scratch_shapes=[
            pltpu.VMEM((2, 4, rows, width), BF),
            pltpu.VMEM((4, 512, 256), BF),
            pltpu.SemaphoreType.DMA((2, 4)),
            pltpu.SemaphoreType.DMA((4,)),
        ],
        compiler_params=pltpu.CompilerParams(vmem_limit_bytes=VMEM_MOST),
        cost_estimate=THREE_US,
        name="q_project",
    )(near, far, *pieces, *so_far)


def choose_kernel(tab, *refs):
    sources, outs = refs[:4], refs[4:]
    for e in range(4):
        for d in range(4):

            @pl.when(tab[e] == d)
            def _():
                outs[e][...] = sources[d][...]


def choose(tab, sources):
    shape = sources[0].shape
    return pl.pallas_call(
        choose_kernel,
        grid_spec=pltpu.PrefetchScalarGridSpec(
            num_scalar_prefetch=1,
            grid=(1,),
            in_specs=[full(shape)] * 4,
            out_specs=[full(shape)] * 4,
        ),
        out_shape=[jax.ShapeDtypeStruct(shape, BF)] * 4,
        compiler_params=pltpu.CompilerParams(vmem_limit_bytes=8 << 20),
        cost_estimate=CHEAP,
        name="choose",
    )(tab, *sources)


def settle_kernel(tab, *refs):
    w_ref, bias_ref = refs[4:]
    for d in range(4):

        @pl.when(tab[0] == d)
        def _():
            w_ref[...] = refs[d][:512, :]
            bias_ref[...] = refs[d][512:, :].astype(F32)


def settle(tab, candidates):
    outs = [jax.ShapeDtypeStruct((512, 256), BF), jax.ShapeDtypeStruct((16, 256), F32)]
    return pl.pallas_call(
        settle_kernel,
        grid_spec=pltpu.PrefetchScalarGridSpec(
            num_scalar_prefetch=1,
            grid=(1,),
            in_specs=[full(candidates[0].shape)] * 4,
            out_specs=[full(o.shape) for o in outs],
        ),
        out_shape=outs,
        compiler_params=pltpu.CompilerParams(vmem_limit_bytes=8 << 20),
        cost_estimate=CHEAP,
        name="settle",
    )(tab, *candidates)


def place(ref_piece, j, kt, vt, col):
    krow = pl.multiple_of(j * 16, 16)
    vrow = pl.multiple_of(j * 32, 32)
    kt[pl.ds(krow, 16), pl.ds(col, 512)] = ref_piece[0:16, :]
    kt[pl.ds(krow + 64, 16), pl.ds(col, 512)] = ref_piece[16:32, :]
    vt[pl.ds(vrow, 32), pl.ds(col, 512)] = ref_piece[32:64, :]


def assemble_kernel(tab, *refs):
    o_ref = refs[4]
    for a in range(4):
        col = pl.multiple_of(tab[8 + a] * 512, 512)

        def one(d, carry):
            place(refs[a].at[d], tab[16 + d], o_ref.at[0], o_ref.at[1], col)
            return carry

        lax.fori_loop(0, 4, one, 0)


def assemble(tab, base):
    shape = jax.ShapeDtypeStruct((2, 128, 2048), BF)
    return pl.pallas_call(
        assemble_kernel,
        grid_spec=pltpu.PrefetchScalarGridSpec(
            num_scalar_prefetch=1,
            grid=(1,),
            in_specs=[full(a.shape) for a in base],
            out_specs=full(shape.shape),
        ),
        out_shape=shape,
        compiler_params=pltpu.CompilerParams(vmem_limit_bytes=8 << 20),
        cost_estimate=CHEAP,
        name="assemble",
    )(tab, *base)


def attention_kernel(
    tab, one_ref, two_ref, bias_ref, cos_ref, sin_ref, own_ref, near_ref, far_ref, o_ref, qs, kv, own_kt, own_vt, sems
):
    core = tab[24]
    copies = [
        pltpu.make_async_copy(ref, kv.at[place_at], sems.at[i])
        for i, (ref, place_at) in enumerate(((near_ref, core), (far_ref, 1 - core)))
    ]
    for copy in copies:
        copy.start()
    for d in range(4):
        place(own_ref.at[d], tab[20 + d], own_kt, own_vt, 0)
    for blk in range(2):
        rows = slice(blk * 256, (blk + 1) * 256)
        for h in range(2):
            cols = slice(h * 128, (h + 1) * 128)
            u = one_ref[rows, cols] + two_ref[rows, cols] + bias_ref[0:1, cols]
            turned = u * cos_ref[rows, :] + pltpu.roll(u, 64, 1) * sin_ref[rows, :]
            qs[blk, h * 256 : (h + 1) * 256, :] = turned.astype(BF)

    factor = (128 ** -0.5) * math.log2(math.e)

    def lanes(p):
        total = p[:, :128]
        for i in range(1, p.shape[1] // 128):
            total = total + p[:, i * 128 : (i + 1) * 128]
        return total

    def pv(p, v):
        return lax.dot_general(p.astype(BF), v, (((1,), (1,)), ((), ())), preferred_element_type=F32)

    def first(blk):
        live = tab[2 + blk]
        c0 = blk * 256
        s = jnp.dot(qs[blk], own_kt[:, c0 : c0 + 256], preferred_element_type=F32) * factor
        row = lax.broadcasted_iota(jnp.int32, (512, 256), 0)
        row = jnp.where(row >= 256, row - 256, row)
        column = lax.broadcasted_iota(jnp.int32, (512, 256), 1)
        mask = (column <= row) & (column < live)
        s = jnp.where(mask, s, -1e30)
        top = jnp.max(s, axis=1, keepdims=True)
        p = jnp.where(mask, jnp.exp2(s - top), 0.0)
        return (top, lanes(p), pv(p, own_vt[:, c0 : c0 + 256]))

    def step(blk, c, width, state):
        top, total, acc = state
        side = lax.rem(c, 2)
        keys = pl.ds(pl.multiple_of(c // 2 * 512, 512), width)
        s = jnp.dot(qs[blk], kv[side, 0, :, keys], preferred_element_type=F32) * factor
        new = jnp.maximum(top, jnp.max(s, axis=1, keepdims=True))
        p = jnp.exp2(s - new)
        decay = jnp.exp2(top - new)
        return (new, total * decay + lanes(p), acc * decay + pv(p, kv[side, 1, :, keys]))

    states = [first(0), first(1)]
    for copy in copies:
        copy.wait()
    for blk in range(2):
        n = tab[blk]
        state = lax.fori_loop(0, n // 2, lambda c, st: step(blk, c, 512, st), states[blk])
        state = lax.fori_loop(0, lax.rem(n, 2), lambda i, st: step(blk, n // 2, 256, st), state)
        top, total, acc = state
        result = (acc / jnp.sum(total, axis=1, keepdims=True)).astype(BF)
        for h in range(2):
            o_ref[blk * 256 : (blk + 1) * 256, h * 128 : (h + 1) * 128] = result[h * 256 : (h + 1) * 256]


def attention(tab, one, two, bias, cos, sin, own, near, far):
    inputs = [one, two, bias, cos, sin, own]
    return pl.pallas_call(
        attention_kernel,
        grid_spec=pltpu.PrefetchScalarGridSpec(
            num_scalar_prefetch=1,
            grid=(1,),
            in_specs=[full(a.shape) for a in inputs] + [HBM] * 2,
            out_specs=full((512, 256)),
            scratch_shapes=[
                pltpu.VMEM((2, 512, 128), BF),
                pltpu.VMEM((2, 2, 128, 2048), BF),
                pltpu.VMEM((128, 512), BF),
                pltpu.VMEM((128, 512), BF),
                pltpu.SemaphoreType.DMA((2,)),
            ],
        ),
        out_shape=jax.ShapeDtypeStruct((512, 256), BF),
        compiler_params=pltpu.CompilerParams(vmem_limit_bytes=VMEM_LIMIT),
        cost_estimate=CHEAP,
        name="attention",
    )(tab, *inputs, near, far)


def shift(v, axis, by):
    n = lax.axis_size(axis)
    return lax.ppermute(v, axis, [(i, (i + by) % n) for i in range(n)])


def flip(v, axis, bits):
    n = lax.axis_size(axis)
    return lax.ppermute(v, axis, [(i, i ^ bits) for i in range(n)])


def after(value, *others):
    return lax.optimization_barrier((value, *others))[0]


def each(fn, values, *others):
    return [fn(after(v, *others) if others else v) for v in values]


def local(
    hidden,
    norm_gain,
    trainer_query,
    trainer_query_bias,
    trainer_kv,
    trainer_kv_bias,
    matching,
    block_lists,
    completion_lengths,
):
    zh, x, core, y, zl = (lax.axis_index(a).astype(jnp.int32) for a in (ZH, X, CORE, Y, ZL))
    rows = hidden.shape[0]
    ctx = (zh * 4 + x) * 2 + core
    four = jnp.arange(4, dtype=jnp.int32)

    ks = jnp.arange(16, dtype=jnp.int32)
    order = ((zh ^ ((ks >> 2) & 1)) * 4 + (x ^ (ks & 3))) * 2 + (core ^ (ks >> 3))
    near, far_out = norm(hidden, norm_gain, order)

    head = lax.dynamic_index_in_dim(trainer_kv, y, 0, keepdims=False)
    out_col = jnp.arange(128, dtype=jnp.int32) % 64
    wanted = jnp.where(
        out_col < 16,
        zl * 16 + out_col,
        jnp.where(out_col < 32, 64 + zl * 16 + out_col - 16, 128 + zl * 32 + out_col - 32),
    )
    side = jnp.arange(128, dtype=jnp.int32) // 64
    pick = jnp.arange(256, dtype=jnp.int32)[:, None] == wanted[None, :]
    pick_l = (pick & (side == 0)[None, :]).astype(BF)
    pick_r = (pick & (side == 1)[None, :]).astype(BF)
    packed = (
        jnp.dot(head[:256], pick_l, preferred_element_type=F32)
        + jnp.dot(head[256:], pick_r, preferred_element_type=F32)
    ).astype(BF)
    head_bias = lax.dynamic_index_in_dim(trainer_kv_bias, y, 0, keepdims=False).astype(F32)
    own_bias = jnp.sum(jnp.where(pick[:, :64], head_bias[:, None], 0.0), axis=0)
    own_bias = jnp.broadcast_to(own_bias[:, None], (64, 128))

    source = lambda tz: jnp.sum(
        jnp.where(matching[None, :] == (y * 4 + tz)[:, None], jnp.arange(16, dtype=jnp.int32)[None, :], 0), axis=1
    )
    src = source(zl ^ four)
    bias_rows = jnp.broadcast_to(trainer_query_bias, (16, 256))
    block = jnp.concatenate([trainer_query[0], bias_rows], axis=0)
    gathered = [block] + [flip(block, Y, e) for e in (1, 2, 3)]
    both = jnp.concatenate([packed, flip(packed, ZH, 1)], axis=0)
    tab_1 = ((src // 4) ^ y).astype(jnp.int32)
    sent = choose(after(tab_1, near, both), gathered)
    both = after(both, sent[0])
    p_near = [both] + [flip(both, X, d) for d in (1, 2, 3)]
    far = flip(after(far_out, sent[0]), CORE, 1)
    candidates = [sent[0]] + [flip(sent[f], ZL, f) for f in (1, 2, 3)]

    counts = jnp.sum((block_lists >= 0).astype(jnp.int32), axis=1)
    token = jnp.arange(rows, dtype=jnp.int32)
    positions = (jnp.where(token < BLK, counts[0], counts[1]) - 1) * BLK + token % BLK
    freqs = THETA ** (-2.0 * jnp.arange(64, dtype=F32) / 128)
    angles = positions.astype(F32)[:, None] * freqs[None, :]
    cosine, sine = jnp.cos(angles), jnp.sin(angles)
    cos2 = jnp.concatenate([cosine, cosine], axis=1)
    sin2 = jnp.concatenate([-sine, sine], axis=1)
    own_freqs = lax.dynamic_slice_in_dim(freqs, zl * 16, 16, 0)
    own_angles = own_freqs[:, None] * positions.astype(F32)[None, :]
    cos_t, sin_t = jnp.cos(own_angles), jnp.sin(own_angles)

    tab_2 = ((src[:1] % 4) ^ zl).astype(jnp.int32)
    s0, bias = settle(after(tab_2, far, *p_near), candidates)
    z0 = flip(s0, ZH, 1)
    s_near = [s0] + [flip(s0, X, d) for d in (1, 2, 3)]

    kv_own, kv_other = kv_project(after(near, s0), far, p_near)
    kv_other, z0, *s_near = lax.optimization_barrier((kv_other, z0, *s_near))
    z_near = [z0] + [flip(z0, X, d) for d in (1, 2, 3)]
    piece = kv_finish(kv_own, flip(kv_other, CORE, 1), own_bias, cos_t, sin_t)
    over = lax.ppermute(piece, (ZH, ZL), [(i, 4 + (3 - i)) for i in range(4)])
    start = jnp.where(zh == 0, piece, over)
    pair = jnp.stack([start, piece])
    pairs = [pair] + [flip(pair, ZL, d) for d in (1, 2, 3)]
    base0 = jnp.stack([p[0] for p in pairs])
    own = jnp.stack([p[1] for p in pairs])
    q_half = list(q_project(0, near, far, s_near, []))
    base0, q_half[0], *z_near = lax.optimization_barrier((base0, q_half[0], *z_near))
    base_near = [base0] + [flip(base0, X, d) for d in (1, 2, 3)]
    q_own, q_other = q_project(4, near, far, z_near, q_half)
    q_two = flip(q_other, CORE, 1)
    base_near[0] = after(base_near[0], q_own)

    blocks = ctx * 2 + jnp.arange(2, dtype=jnp.int32)
    slots = jnp.arange(16, dtype=jnp.int32)
    lengths = jnp.sum(
        jnp.where((blocks[:, None] - 16) == slots[None, :], completion_lengths[None, :], 0), axis=1
    )
    live = jnp.where(blocks < 16, BLK, lengths)
    tab = jnp.concatenate(
        [
            counts - 1,
            live,
            jnp.zeros((4,), jnp.int32),
            x ^ four,
            jnp.zeros((4,), jnp.int32),
            zl ^ four ^ (3 * zh),
            zl ^ four,
            core[None],
        ]
    ).astype(jnp.int32)
    whole = assemble(tab, base_near)
    return attention(tab, q_own, q_two, bias, cos2, sin2, own, whole, flip(whole, CORE, 1))


def solution(mesh):
    fine = Mesh(mesh.devices.reshape(2, 4, 2, 4, 4), (ZH, X, CORE, Y, ZL))
    ctx = (ZH, X, CORE)
    tp = (Y, ZL)
    in_specs = (
        P(ctx, None),
        P(),
        P(tp, ctx, None),
        P(tp, None),
        P(None, ctx, None),
        P(),
        P(),
        P(ctx, None),
        P(),
    )
    return jax.shard_map(local, mesh=fine, in_specs=in_specs, out_specs=P(ctx, tp), check_vma=False)
```

profile of v0, /device:TPU:39, one launch (start us, length us, event | category | flops | bytes accessed | tf_op | source)
XLA Modules:
  0.0 142.5 jit_solution(15945821739753515852)
XLA Ops:
  0.0 0.8 reduce
  0.8 1.0 pad_maximum_fusion.refs_0_
  1.8 1.4 collective-permute-start.1
  3.2 2.6 %collective-permute-start.2 = (bf16[528,256]{1,0:T(8,128)(2,1)S(1)}, bf16[528,256]{1,0:T(8,128)(2,1)S(1)}, u32[]{:S(2)}, u32[]{:S(2)}) collective-permute-start(bf16[528,256]{1,0:T(8,128)(2,1)S(1)} %pad_maximum_fusion.refs_0_), channel_id=1, source_target_pairs={{0,8},{4,12},{8,0},{12,4},{1,9},{5,13},{9,1},{13,5},{2,10},{6,14},... | collective-permute-start | bytes 811016 | tf_op jit(solution)/shard_map/ppermute | solution.py:393
  6.3 6.1 %collective-permute-start = (bf16[256,128]{1,0:T(8,128)(2,1)S(1)}, bf16[256,128]{1,0:T(8,128)(2,1)S(1)}, u32[]{:S(2)}, u32[]{:S(2)}) collective-permute-start(bf16[256,128]{1,0:T(8,128)(2,1)S(1)} %fusion), channel_id=1, source_target_pairs={{0,128},{128,0},{1,129},{129,1},{2,130},{130,2},{3,131},{131,3},{4... | collective-permute-start | bytes 196616 | tf_op jit(solution)/shard_map/ppermute | solution.py:393
  12.4 0.8 select_reduce_fusion.1
  13.3 0.7 reshape.101.g_ref
  14.1 9.3 %norm.1 = (bf16[8,512,512]{2,1,0:T(8,128)(2,1)S(1)}, bf16[8,512,512]{2,1,0:T(8,128)(2,1)S(1)}) custom-call(s32[16]{0:T(128)S(1)} %xor_add_fusion.order, bf16[512,8192]{1,0:T(8,128)(2,1)} %h_ref.1, bf16[1,8192]{1,0:T(2,128)(2,1)S(1)} %reshape.101.g_ref), custom_call_target="tpu_custom_call" | custom-call | bytes 20971520 | tf_op jit(solution)/shard_map/norm/pallas_call | solution.py:62
  23.3 1.9 %copy-done.1 = bf16[8,512,512]{2,1,0:T(8,128)(2,1)} copy-done((bf16[8,512,512]{2,1,0:T(8,128)(2,1)}, bf16[8,512,512]{2,1,0:T(8,128)(2,1)S(1)}, u32[]{:S(2)}) %copy-start.1) | copy-done | bytes 4194328
  25.4 0.7 choose.1
  26.1 1.8 %collective-permute-start.4 = (bf16[8,512,512]{2,1,0:T(8,128)(2,1)S(1)}, bf16[8,512,512]{2,1,0:T(8,128)(2,1)S(1)}, u32[]{:S(2)}, u32[]{:S(2)}) collective-permute-start(bf16[8,512,512]{2,1,0:T(8,128)(2,1)S(1)} %get-tuple-element.41), channel_id=1, source_target_pairs={{0,16},{16,0},{1,17},{17,1},{2,18},{18,2},{3,19},{19,3},{4,20},{20... | collective-permute-start | bytes 12582920 | tf_op jit(solution)/shard_map/ppermute | solution.py:393
  28.5 0.8 collective-permute-start.6
  29.4 0.8 collective-permute-start.10
  30.2 1.6 %collective-permute-start.8 = (bf16[528,256]{1,0:T(8,128)(2,1)S(1)}, bf16[528,256]{1,0:T(8,128)(2,1)S(1)}, u32[]{:S(2)}, u32[]{:S(2)}) collective-permute-start(bf16[528,256]{1,0:T(8,128)(2,1)S(1)} %get-tuple-element.44), channel_id=1, source_target_pairs={{0,1},{1,0},{2,3},{3,2},{4,5},{5,4},{6,7},{7,6},{8,9},{9,8},{10,11... | collective-permute-start | bytes 811016 | tf_op jit(solution)/shard_map/ppermute | solution.py:393
  31.9 1.1 collective-permute-done.5.refs_1_
  33.0 1.2 collective-permute-start.9
  34.3 1.4 collective-permute-done.6.refs_2_
  35.7 2.5 %collective-permute-start.7 = (bf16[512,128]{1,0:T(8,128)(2,1)S(1)}, bf16[512,128]{1,0:T(8,128)(2,1)S(1)}, u32[]{:S(2)}, u32[]{:S(2)}) collective-permute-start(bf16[512,128]{1,0:T(8,128)(2,1)S(1)} %pad_maximum_fusion.5.refs_0_), channel_id=1, source_target_pairs={{0,96},{32,64},{64,32},{96,0},{1,97},{33,65},{65,33},{97,1},{2,98}... | collective-permute-start | bytes 393224 | tf_op jit(solution)/shard_map/ppermute | solution.py:393
  38.9 1.3 fusion.10
  40.3 0.8 collective-permute-done.7.refs_3_
  41.1 1.6 %collective-permute-done.10.refs_3_ = bf16[528,256]{1,0:T(8,128)(2,1)S(1)} collective-permute-done((bf16[528,256]{1,0:T(8,128)(2,1)S(1)}, bf16[528,256]{1,0:T(8,128)(2,1)S(1)}, u32[]{:S(2)}, u32[]{:S(2)}) %collective-permute-start.10) | collective-permute-done | bytes 270368 | tf_op jit(solution)/shard_map/ppermute | solution.py:393
  42.7 1.9 %collective-permute-done.8.refs_1_ = bf16[528,256]{1,0:T(8,128)(2,1)S(1)} collective-permute-done((bf16[528,256]{1,0:T(8,128)(2,1)S(1)}, bf16[528,256]{1,0:T(8,128)(2,1)S(1)}, u32[]{:S(2)}, u32[]{:S(2)}) %collective-permute-start.8) | collective-permute-done | bytes 270368 | tf_op jit(solution)/shard_map/ppermute | solution.py:393
  44.5 8.3 %collective-permute-done.9.refs_2_ = bf16[528,256]{1,0:T(8,128)(2,1)S(1)} collective-permute-done((bf16[528,256]{1,0:T(8,128)(2,1)S(1)}, bf16[528,256]{1,0:T(8,128)(2,1)S(1)}, u32[]{:S(2)}, u32[]{:S(2)}) %collective-permute-start.9) | collective-permute-done | bytes 270368 | tf_op jit(solution)/shard_map/ppermute | solution.py:393
  54.1 3.1 %collective-permute-start.13 = (bf16[512,256]{1,0:T(8,128)(2,1)S(1)}, bf16[512,256]{1,0:T(8,128)(2,1)S(1)}, u32[]{:S(2)}, u32[]{:S(2)}) collective-permute-start(bf16[512,256]{1,0:T(8,128)(2,1)S(1)} %get-tuple-element.52.refs_0_), channel_id=1, source_target_pairs={{0,64},{32,96},{64,0},{96,32},{1,65},{33,97},{65,1},{97,33},{2,66}... | collective-permute-start | bytes 786440 | tf_op jit(solution)/shard_map/ppermute | solution.py:393
  57.7 7.5 %kv_project.1 = (f32[64,512]{1,0:T(8,128)}, f32[64,512]{1,0:T(8,128)}) custom-call(bf16[8,512,512]{2,1,0:T(8,128)(2,1)} %copy-done.1, bf16[8,512,512]{2,1,0:T(8,128)(2,1)} %copy-done.5, bf16[512,128]{1,0:T(8,128)(2,1)} %copy-done.6, bf16[512,128]{1,0:T(8,128)(2,1)} %copy-done.14, bf16[512,128]{1,0:T(8,128)(2,1)} %copy-done.15, bf16[512,128]{1,0:T(8,128)(2,1)} %copy-done.16), custom_call_target="tpu_custom_call" | custom-call | bytes 20971520 | tf_op jit(solution)/shard_map/kv_project/pallas_call | solution.py:118
  65.3 2.1 %collective-permute-done.13.refs_2_ = bf16[512,256]{1,0:T(8,128)(2,1)S(1)} collective-permute-done((bf16[512,256]{1,0:T(8,128)(2,1)S(1)}, bf16[512,256]{1,0:T(8,128)(2,1)S(1)}, u32[]{:S(2)}, u32[]{:S(2)}) %collective-permute-start.13) | collective-permute-done | bytes 262176 | tf_op jit(solution)/shard_map/ppermute | solution.py:393
  67.4 3.2 %collective-permute-done.14.refs_3_ = bf16[512,256]{1,0:T(8,128)(2,1)S(1)} collective-permute-done((bf16[512,256]{1,0:T(8,128)(2,1)S(1)}, bf16[512,256]{1,0:T(8,128)(2,1)S(1)}, u32[]{:S(2)}, u32[]{:S(2)}) %collective-permute-start.14) | collective-permute-done | bytes 262176 | tf_op jit(solution)/shard_map/ppermute | solution.py:393
  70.6 2.2 %collective-permute-start.15 = (f32[64,512]{1,0:T(8,128)}, f32[64,512]{1,0:T(8,128)S(1)}, u32[]{:S(2)}, u32[]{:S(2)}) collective-permute-start(f32[64,512]{1,0:T(8,128)} %get-tuple-element.51), channel_id=1, source_target_pairs={{0,16},{16,0},{1,17},{17,1},{2,18},{18,2},{3,19},{19,3},{4,20},{20... | collective-permute-start | bytes 393224 | tf_op jit(solution)/shard_map/ppermute | solution.py:393
  72.9 1.1 collective-permute-done.15.two_ref
  74.0 0.9 copy-done.4
  75.0 6.2 %collective-permute-start.16 = (bf16[64,512]{1,0:T(8,128)(2,1)S(1)}, bf16[64,512]{1,0:T(8,128)(2,1)S(1)}, u32[]{:S(2)}, u32[]{:S(2)}) collective-permute-start(bf16[64,512]{1,0:T(8,128)(2,1)S(1)} %kv_finish.1), channel_id=1, source_target_pairs={{0,131},{1,130},{2,129},{3,128},{4,135},{5,134},{6,133},{7,132},{8... | collective-permute-start | bytes 196616 | tf_op jit(solution)/shard_map/ppermute | solution.py:479
  81.2 1.3 collective-permute-done.16
  82.6 3.1 %collective-permute-start.17 = (bf16[2,64,512]{2,1,0:T(8,128)(2,1)S(1)}, bf16[2,64,512]{2,1,0:T(8,128)(2,1)S(1)}, u32[]{:S(2)}, u32[]{:S(2)}) collective-permute-start(bf16[2,64,512]{2,1,0:T(8,128)(2,1)S(1)} %pad_maximum_fusion.6), channel_id=1, source_target_pairs={{0,1},{1,0},{2,3},{3,2},{4,5},{5,4},{6,7},{7,6},{8,9},{9,8},{10,11... | collective-permute-start | bytes 393224 | tf_op jit(solution)/shard_map/ppermute | solution.py:393
  86.0 1.4 collective-permute-start.21
  87.4 2.5 %collective-permute-start.22 = (bf16[512,256]{1,0:T(8,128)(2,1)S(1)}, bf16[512,256]{1,0:T(8,128)(2,1)S(1)}, u32[]{:S(2)}, u32[]{:S(2)}) collective-permute-start(bf16[512,256]{1,0:T(8,128)(2,1)S(1)} %collective-permute-done.11.refs_0_), channel_id=1, source_target_pairs={{0,96},{32,64},{64,32},{96,0},{1,97},{33,65},{65,33},{97,1},{2,98}... | collective-permute-start | bytes 786440 | tf_op jit(solution)/shard_map/ppermute | solution.py:393
  89.8 5.7 %q_project.2 = (f32[512,256]{1,0:T(8,128)}, f32[512,256]{1,0:T(8,128)}) custom-call(bf16[8,512,512]{2,1,0:T(8,128)(2,1)} %copy-done.1, bf16[8,512,512]{2,1,0:T(8,128)(2,1)} %copy-done.5, bf16[512,256]{1,0:T(8,128)(2,1)} %copy-done.3, bf16[512,256]{1,0:T(8,128)(2,1)} %copy-done.8, bf16[512,256]{1,0:T(8,128)(2,1)} %copy-done.9, bf16[512,256]{1,0:T(8,128)(2,1)} %copy-done.10), custom_call_target="tpu_custom_call" | custom-call | bytes 10485760 | tf_op jit(solution)/shard_map/q_project/pallas_call | solution.py:187
  96.9 3.8 %collective-permute-done.18 = bf16[2,64,512]{2,1,0:T(8,128)(2,1)S(1)} collective-permute-done((bf16[2,64,512]{2,1,0:T(8,128)(2,1)S(1)}, bf16[2,64,512]{2,1,0:T(8,128)(2,1)S(1)}, u32[]{:S(2)}, u32[]{:S(2)}) %collective-permute-start.18) | collective-permute-done | bytes 131104 | tf_op jit(solution)/shard_map/ppermute | solution.py:393
  100.7 7.3 %collective-permute-done.19 = bf16[2,64,512]{2,1,0:T(8,128)(2,1)S(1)} collective-permute-done((bf16[2,64,512]{2,1,0:T(8,128)(2,1)S(1)}, bf16[2,64,512]{2,1,0:T(8,128)(2,1)S(1)}, u32[]{:S(2)}, u32[]{:S(2)}) %collective-permute-start.19) | collective-permute-done | bytes 131104 | tf_op jit(solution)/shard_map/ppermute | solution.py:393
  108.2 1.4 collective-permute-start.25
  109.6 2.5 %collective-permute-start.26 = (bf16[4,64,512]{2,1,0:T(8,128)(2,1)S(1)}, bf16[4,64,512]{2,1,0:T(8,128)(2,1)S(1)}, u32[]{:S(2)}, u32[]{:S(2)}) collective-permute-start(bf16[4,64,512]{2,1,0:T(8,128)(2,1)S(1)} %pad_maximum_fusion.1.refs_0_), channel_id=1, source_target_pairs={{0,96},{32,64},{64,32},{96,0},{1,97},{33,65},{65,33},{97,1},{2,98}... | collective-permute-start | bytes 786440 | tf_op jit(solution)/shard_map/ppermute | solution.py:393
  112.2 6.9 %q_project.3 = (f32[512,256]{1,0:T(8,128)}, f32[512,256]{1,0:T(8,128)}) custom-call(bf16[8,512,512]{2,1,0:T(8,128)(2,1)} %copy-done.1, bf16[8,512,512]{2,1,0:T(8,128)(2,1)} %copy-done.5, bf16[512,256]{1,0:T(8,128)(2,1)} %copy-done.7, bf16[512,256]{1,0:T(8,128)(2,1)} %copy-done.11, bf16[512,256]{1,0:T(8,128)(2,1)} %copy-done.12, bf16[512,256]{1,0:T(8,128)(2,1)} %copy-done.13, ...), custom_call_target="tpu_custom_call" | custom-call | bytes 10485760 | tf_op jit(solution)/shard_map/q_project/pallas_call | solution.py:187
  119.1 0.8 collective-permute-done.25.refs_2_
  119.9 3.1 %collective-permute-done.26.refs_3_ = bf16[4,64,512]{2,1,0:T(8,128)(2,1)S(1)} collective-permute-done((bf16[4,64,512]{2,1,0:T(8,128)(2,1)S(1)}, bf16[4,64,512]{2,1,0:T(8,128)(2,1)S(1)}, u32[]{:S(2)}, u32[]{:S(2)}) %collective-permute-start.26) | collective-permute-done | bytes 262176 | tf_op jit(solution)/shard_map/ppermute | solution.py:393
  123.0 0.7 assemble.1.near_ref
  123.7 2.3 %collective-permute-start.27 = (bf16[2,128,2048]{2,1,0:T(8,128)(2,1)S(1)}, bf16[2,128,2048]{2,1,0:T(8,128)(2,1)S(1)}, u32[]{:S(2)}, u32[]{:S(2)}) collective-permute-start(bf16[2,128,2048]{2,1,0:T(8,128)(2,1)S(1)} %assemble.1.near_ref), channel_id=1, source_target_pairs={{0,16},{16,0},{1,17},{17,1},{2,18},{18,2},{3,19},{19,3},{4,20},{20... | collective-permute-start | bytes 3145736 | tf_op jit(solution)/shard_map/ppermute | solution.py:393
  126.1 1.0 fusion.4
  127.3 1.9 %collective-permute-done.23.two_ref = f32[512,256]{1,0:T(8,128)S(1)} collective-permute-done((f32[512,256]{1,0:T(8,128)}, f32[512,256]{1,0:T(8,128)S(1)}, u32[]{:S(2)}, u32[]{:S(2)}) %collective-permute-start.23) | collective-permute-done | bytes 524320 | tf_op jit(solution)/shard_map/ppermute | solution.py:393
  129.2 13.1 %attention.1 = bf16[512,256]{1,0:T(8,128)(2,1)} custom-call(s32[25]{0:T(128)S(1)} %concatenate.15.tab, f32[512,256]{1,0:T(8,128)S(1)} %copy-done.2, f32[512,256]{1,0:T(8,128)S(1)} %collective-permute-done.23.two_ref, f32[16,256]{1,0:T(8,128)S(1)} %get-tuple-element.66.bias_ref, f32[512,128]{1,0:T(8,128)S(1)} %get-tuple-element.88.cos_ref, ...), custom_call_target="tpu_custom_call" | custom-call | tf_op jit(solution)/shard_map/attention/pallas_call | solution.py:364
  (96 shorter events, 6.4 us)
Async XLA Ops:
  0.0 5.8 %copy-start = (bf16[4,512,256]{2,1,0:T(8,128)(2,1)S(1)}, bf16[4,512,256]{2,1,0:T(8,128)(2,1)}, u32[]{:S(2)}) copy-start(bf16[4,512,256]{2,1,0:T(8,128)(2,1)} %param.13) | copy-start | bytes 3145732
  1.8 23.6 %collective-permute-start.1 = (bf16[528,256]{1,0:T(8,128)(2,1)S(1)}, bf16[528,256]{1,0:T(8,128)(2,1)S(1)}, u32[]{:S(2)}, u32[]{:S(2)}) collective-permute-start(bf16[528,256]{1,0:T(8,128)(2,1)S(1)} %pad_maximum_fusion.refs_0_), channel_id=1, source_target_pairs={{0,4},{4,0},{8,12},{12,8},{1,5},{5,1},{9,13},{13,9},{2,6},{6,2},{1... | collective-permute-start | bytes 811016 | tf_op jit(solution)/shard_map/ppermute | solution.py:393
  3.2 22.2 %collective-permute-start.2 = (bf16[528,256]{1,0:T(8,128)(2,1)S(1)}, bf16[528,256]{1,0:T(8,128)(2,1)S(1)}, u32[]{:S(2)}, u32[]{:S(2)}) collective-permute-start(bf16[528,256]{1,0:T(8,128)(2,1)S(1)} %pad_maximum_fusion.refs_0_), channel_id=1, source_target_pairs={{0,8},{4,12},{8,0},{12,4},{1,9},{5,13},{9,1},{13,5},{2,10},{6,14},... | collective-permute-start | bytes 811016 | tf_op jit(solution)/shard_map/ppermute | solution.py:393
  5.8 19.6 %collective-permute-start.3 = (bf16[528,256]{1,0:T(8,128)(2,1)S(1)}, bf16[528,256]{1,0:T(8,128)(2,1)S(1)}, u32[]{:S(2)}, u32[]{:S(2)}) collective-permute-start(bf16[528,256]{1,0:T(8,128)(2,1)S(1)} %pad_maximum_fusion.refs_0_), channel_id=1, source_target_pairs={{0,12},{4,8},{8,4},{12,0},{1,13},{5,9},{9,5},{13,1},{2,14},{6,10},... | collective-permute-start | bytes 811016 | tf_op jit(solution)/shard_map/ppermute | solution.py:393
  6.3 19.0 %collective-permute-start = (bf16[256,128]{1,0:T(8,128)(2,1)S(1)}, bf16[256,128]{1,0:T(8,128)(2,1)S(1)}, u32[]{:S(2)}, u32[]{:S(2)}) collective-permute-start(bf16[256,128]{1,0:T(8,128)(2,1)S(1)} %fusion), channel_id=1, source_target_pairs={{0,128},{128,0},{1,129},{129,1},{2,130},{130,2},{3,131},{131,3},{4... | collective-permute-start | bytes 196616 | tf_op jit(solution)/shard_map/ppermute | solution.py:393
  14.0 20.1 %copy-start.18 = (s32[2,17]{1,0:T(2,128)S(1)}, s32[2,17]{1,0:T(2,128)}, u32[]{:S(2)}) copy-start(s32[2,17]{1,0:T(2,128)} %param.16) | copy-start | bytes 412
  23.3 2.0 %copy-start.1 = (bf16[8,512,512]{2,1,0:T(8,128)(2,1)}, bf16[8,512,512]{2,1,0:T(8,128)(2,1)S(1)}, u32[]{:S(2)}) copy-start(bf16[8,512,512]{2,1,0:T(8,128)(2,1)S(1)} %get-tuple-element.48.near_ref) | copy-start | bytes 12582916
  25.3 32.4 %copy-start.6 = (bf16[512,128]{1,0:T(8,128)(2,1)}, bf16[512,128]{1,0:T(8,128)(2,1)S(1)}, u32[]{:S(2)}) copy-start(bf16[512,128]{1,0:T(8,128)(2,1)S(1)} %pad_maximum_fusion.5.refs_0_) | copy-start | bytes 393220
  26.1 15.0 %collective-permute-start.4 = (bf16[8,512,512]{2,1,0:T(8,128)(2,1)S(1)}, bf16[8,512,512]{2,1,0:T(8,128)(2,1)S(1)}, u32[]{:S(2)}, u32[]{:S(2)}) collective-permute-start(bf16[8,512,512]{2,1,0:T(8,128)(2,1)S(1)} %get-tuple-element.41), channel_id=1, source_target_pairs={{0,16},{16,0},{1,17},{17,1},{2,18},{18,2},{3,19},{19,3},{4,20},{20... | collective-permute-start | bytes 12582920 | tf_op jit(solution)/shard_map/ppermute | solution.py:393
  27.9 5.1 %collective-permute-start.5 = (bf16[512,128]{1,0:T(8,128)(2,1)S(1)}, bf16[512,128]{1,0:T(8,128)(2,1)S(1)}, u32[]{:S(2)}, u32[]{:S(2)}) collective-permute-start(bf16[512,128]{1,0:T(8,128)(2,1)S(1)} %pad_maximum_fusion.5.refs_0_), channel_id=1, source_target_pairs={{0,32},{32,0},{64,96},{96,64},{1,33},{33,1},{65,97},{97,65},{2,34}... | collective-permute-start | bytes 393224 | tf_op jit(solution)/shard_map/ppermute | solution.py:393
  28.5 7.2 %collective-permute-start.6 = (bf16[512,128]{1,0:T(8,128)(2,1)S(1)}, bf16[512,128]{1,0:T(8,128)(2,1)S(1)}, u32[]{:S(2)}, u32[]{:S(2)}) collective-permute-start(bf16[512,128]{1,0:T(8,128)(2,1)S(1)} %pad_maximum_fusion.5.refs_0_), channel_id=1, source_target_pairs={{0,64},{32,96},{64,0},{96,32},{1,65},{33,97},{65,1},{97,33},{2,66}... | collective-permute-start | bytes 393224 | tf_op jit(solution)/shard_map/ppermute | solution.py:393
  29.4 13.3 %collective-permute-start.10 = (bf16[528,256]{1,0:T(8,128)(2,1)S(1)}, bf16[528,256]{1,0:T(8,128)(2,1)S(1)}, u32[]{:S(2)}, u32[]{:S(2)}) collective-permute-start(bf16[528,256]{1,0:T(8,128)(2,1)S(1)} %get-tuple-element.46), channel_id=1, source_target_pairs={{0,3},{1,2},{2,1},{3,0},{4,7},{5,6},{6,5},{7,4},{8,11},{9,10},{10,... | collective-permute-start | bytes 811016 | tf_op jit(solution)/shard_map/ppermute | solution.py:393
  30.2 14.3 %collective-permute-start.8 = (bf16[528,256]{1,0:T(8,128)(2,1)S(1)}, bf16[528,256]{1,0:T(8,128)(2,1)S(1)}, u32[]{:S(2)}, u32[]{:S(2)}) collective-permute-start(bf16[528,256]{1,0:T(8,128)(2,1)S(1)} %get-tuple-element.44), channel_id=1, source_target_pairs={{0,1},{1,0},{2,3},{3,2},{4,5},{5,4},{6,7},{7,6},{8,9},{9,8},{10,11... | collective-permute-start | bytes 811016 | tf_op jit(solution)/shard_map/ppermute | solution.py:393
  33.0 24.7 %copy-start.14 = (bf16[512,128]{1,0:T(8,128)(2,1)}, bf16[512,128]{1,0:T(8,128)(2,1)S(1)}, u32[]{:S(2)}) copy-start(bf16[512,128]{1,0:T(8,128)(2,1)S(1)} %collective-permute-done.5.refs_1_) | copy-start | bytes 393220
  33.0 19.8 %collective-permute-start.9 = (bf16[528,256]{1,0:T(8,128)(2,1)S(1)}, bf16[528,256]{1,0:T(8,128)(2,1)S(1)}, u32[]{:S(2)}, u32[]{:S(2)}) collective-permute-start(bf16[528,256]{1,0:T(8,128)(2,1)S(1)} %get-tuple-element.45), channel_id=1, source_target_pairs={{0,2},{1,3},{2,0},{3,1},{4,6},{5,7},{6,4},{7,5},{8,10},{9,11},{10,... | collective-permute-start | bytes 811016 | tf_op jit(solution)/shard_map/ppermute | solution.py:393
  35.7 22.0 %copy-start.15 = (bf16[512,128]{1,0:T(8,128)(2,1)}, bf16[512,128]{1,0:T(8,128)(2,1)S(1)}, u32[]{:S(2)}) copy-start(bf16[512,128]{1,0:T(8,128)(2,1)S(1)} %collective-permute-done.6.refs_2_) | copy-start | bytes 393220
  35.7 5.4 %collective-permute-start.7 = (bf16[512,128]{1,0:T(8,128)(2,1)S(1)}, bf16[512,128]{1,0:T(8,128)(2,1)S(1)}, u32[]{:S(2)}, u32[]{:S(2)}) collective-permute-start(bf16[512,128]{1,0:T(8,128)(2,1)S(1)} %pad_maximum_fusion.5.refs_0_), channel_id=1, source_target_pairs={{0,96},{32,64},{64,32},{96,0},{1,97},{33,65},{65,33},{97,1},{2,98}... | collective-permute-start | bytes 393224 | tf_op jit(solution)/shard_map/ppermute | solution.py:393
  41.0 16.7 %copy-start.16 = (bf16[512,128]{1,0:T(8,128)(2,1)}, bf16[512,128]{1,0:T(8,128)(2,1)S(1)}, u32[]{:S(2)}) copy-start(bf16[512,128]{1,0:T(8,128)(2,1)S(1)} %collective-permute-done.7.refs_3_) | copy-start | bytes 393220
  41.1 13.1 %copy-start.5 = (bf16[8,512,512]{2,1,0:T(8,128)(2,1)}, bf16[8,512,512]{2,1,0:T(8,128)(2,1)S(1)}, u32[]{:S(2)}) copy-start(bf16[8,512,512]{2,1,0:T(8,128)(2,1)S(1)} %collective-permute-done.4.far_ref) | copy-start | bytes 12582916
  52.8 12.4 %copy-start.3 = (bf16[512,256]{1,0:T(8,128)(2,1)}, bf16[512,256]{1,0:T(8,128)(2,1)S(1)}, u32[]{:S(2)}) copy-start(bf16[512,256]{1,0:T(8,128)(2,1)S(1)} %get-tuple-element.52.refs_0_) | copy-start | bytes 786436
  52.8 12.4 %collective-permute-start.11 = (bf16[512,256]{1,0:T(8,128)(2,1)S(1)}, bf16[512,256]{1,0:T(8,128)(2,1)S(1)}, u32[]{:S(2)}, u32[]{:S(2)}) collective-permute-start(bf16[512,256]{1,0:T(8,128)(2,1)S(1)} %get-tuple-element.52.refs_0_), channel_id=1, source_target_pairs={{0,128},{128,0},{1,129},{129,1},{2,130},{130,2},{3,131},{131,3},{4... | collective-permute-start | bytes 786440 | tf_op jit(solution)/shard_map/ppermute | solution.py:393
  53.5 11.8 %collective-permute-start.12 = (bf16[512,256]{1,0:T(8,128)(2,1)S(1)}, bf16[512,256]{1,0:T(8,128)(2,1)S(1)}, u32[]{:S(2)}, u32[]{:S(2)}) collective-permute-start(bf16[512,256]{1,0:T(8,128)(2,1)S(1)} %get-tuple-element.52.refs_0_), channel_id=1, source_target_pairs={{0,32},{32,0},{64,96},{96,64},{1,33},{33,1},{65,97},{97,65},{2,34}... | collective-permute-start | bytes 786440 | tf_op jit(solution)/shard_map/ppermute | solution.py:393
  54.1 13.3 %collective-permute-start.13 = (bf16[512,256]{1,0:T(8,128)(2,1)S(1)}, bf16[512,256]{1,0:T(8,128)(2,1)S(1)}, u32[]{:S(2)}, u32[]{:S(2)}) collective-permute-start(bf16[512,256]{1,0:T(8,128)(2,1)S(1)} %get-tuple-element.52.refs_0_), channel_id=1, source_target_pairs={{0,64},{32,96},{64,0},{96,32},{1,65},{33,97},{65,1},{97,33},{2,66}... | collective-permute-start | bytes 786440 | tf_op jit(solution)/shard_map/ppermute | solution.py:393
  57.2 13.4 %collective-permute-start.14 = (bf16[512,256]{1,0:T(8,128)(2,1)S(1)}, bf16[512,256]{1,0:T(8,128)(2,1)S(1)}, u32[]{:S(2)}, u32[]{:S(2)}) collective-permute-start(bf16[512,256]{1,0:T(8,128)(2,1)S(1)} %get-tuple-element.52.refs_0_), channel_id=1, source_target_pairs={{0,96},{32,64},{64,32},{96,0},{1,97},{33,65},{65,33},{97,1},{2,98}... | collective-permute-start | bytes 786440 | tf_op jit(solution)/shard_map/ppermute | solution.py:393
  57.7 15.0 %copy-start.17 = (bf16[4,256]{1,0:T(4,128)(2,1)S(1)}, bf16[4,256]{1,0:T(4,128)(2,1)}, u32[]{:S(2)}) copy-start(bf16[4,256]{1,0:T(4,128)(2,1)} %param.14) | copy-start | bytes 6148
  57.7 28.0 %copy-start.19 = (s32[16]{0:T(128)S(1)}, s32[16]{0:T(128)}, u32[]{:S(2)}) copy-start(s32[16]{0:T(128)} %param.17) | copy-start | bytes 196
  65.3 30.3 %copy-start.7 = (bf16[512,256]{1,0:T(8,128)(2,1)}, bf16[512,256]{1,0:T(8,128)(2,1)S(1)}, u32[]{:S(2)}) copy-start(bf16[512,256]{1,0:T(8,128)(2,1)S(1)} %collective-permute-done.11.refs_0_) | copy-start | bytes 786436
  65.3 24.5 %copy-start.8 = (bf16[512,256]{1,0:T(8,128)(2,1)}, bf16[512,256]{1,0:T(8,128)(2,1)S(1)}, u32[]{:S(2)}) copy-start(bf16[512,256]{1,0:T(8,128)(2,1)S(1)} %collective-permute-done.12.refs_1_) | copy-start | bytes 786436
  67.4 22.4 %copy-start.9 = (bf16[512,256]{1,0:T(8,128)(2,1)}, bf16[512,256]{1,0:T(8,128)(2,1)S(1)}, u32[]{:S(2)}) copy-start(bf16[512,256]{1,0:T(8,128)(2,1)S(1)} %collective-permute-done.13.refs_2_) | copy-start | bytes 786436
  70.6 19.3 %copy-start.10 = (bf16[512,256]{1,0:T(8,128)(2,1)}, bf16[512,256]{1,0:T(8,128)(2,1)S(1)}, u32[]{:S(2)}) copy-start(bf16[512,256]{1,0:T(8,128)(2,1)S(1)} %collective-permute-done.14.refs_3_) | copy-start | bytes 786436
  70.6 3.4 %collective-permute-start.15 = (f32[64,512]{1,0:T(8,128)}, f32[64,512]{1,0:T(8,128)S(1)}, u32[]{:S(2)}, u32[]{:S(2)}) collective-permute-start(f32[64,512]{1,0:T(8,128)} %get-tuple-element.51), channel_id=1, source_target_pairs={{0,16},{16,0},{1,17},{17,1},{2,18},{18,2},{3,19},{19,3},{4,20},{20... | collective-permute-start | bytes 393224 | tf_op jit(solution)/shard_map/ppermute | solution.py:393
  74.0 0.9 copy-start.4
  75.0 7.5 %collective-permute-start.16 = (bf16[64,512]{1,0:T(8,128)(2,1)S(1)}, bf16[64,512]{1,0:T(8,128)(2,1)S(1)}, u32[]{:S(2)}, u32[]{:S(2)}) collective-permute-start(bf16[64,512]{1,0:T(8,128)(2,1)S(1)} %kv_finish.1), channel_id=1, source_target_pairs={{0,131},{1,130},{2,129},{3,128},{4,135},{5,134},{6,133},{7,132},{8... | collective-permute-start | bytes 196616 | tf_op jit(solution)/shard_map/ppermute | solution.py:479
  82.6 13.6 %collective-permute-start.17 = (bf16[2,64,512]{2,1,0:T(8,128)(2,1)S(1)}, bf16[2,64,512]{2,1,0:T(8,128)(2,1)S(1)}, u32[]{:S(2)}, u32[]{:S(2)}) collective-permute-start(bf16[2,64,512]{2,1,0:T(8,128)(2,1)S(1)} %pad_maximum_fusion.6), channel_id=1, source_target_pairs={{0,1},{1,0},{2,3},{3,2},{4,5},{5,4},{6,7},{7,6},{8,9},{9,8},{10,11... | collective-permute-start | bytes 393224 | tf_op jit(solution)/shard_map/ppermute | solution.py:393
  85.9 22.2 %collective-permute-start.20 = (bf16[512,256]{1,0:T(8,128)(2,1)S(1)}, bf16[512,256]{1,0:T(8,128)(2,1)S(1)}, u32[]{:S(2)}, u32[]{:S(2)}) collective-permute-start(bf16[512,256]{1,0:T(8,128)(2,1)S(1)} %collective-permute-done.11.refs_0_), channel_id=1, source_target_pairs={{0,32},{32,0},{64,96},{96,64},{1,33},{33,1},{65,97},{97,65},{2,34}... | collective-permute-start | bytes 786440 | tf_op jit(solution)/shard_map/ppermute | solution.py:393
  86.0 22.1 %collective-permute-start.21 = (bf16[512,256]{1,0:T(8,128)(2,1)S(1)}, bf16[512,256]{1,0:T(8,128)(2,1)S(1)}, u32[]{:S(2)}, u32[]{:S(2)}) collective-permute-start(bf16[512,256]{1,0:T(8,128)(2,1)S(1)} %collective-permute-done.11.refs_0_), channel_id=1, source_target_pairs={{0,64},{32,96},{64,0},{96,32},{1,65},{33,97},{65,1},{97,33},{2,66}... | collective-permute-start | bytes 786440 | tf_op jit(solution)/shard_map/ppermute | solution.py:393
  87.4 20.8 %collective-permute-start.22 = (bf16[512,256]{1,0:T(8,128)(2,1)S(1)}, bf16[512,256]{1,0:T(8,128)(2,1)S(1)}, u32[]{:S(2)}, u32[]{:S(2)}) collective-permute-start(bf16[512,256]{1,0:T(8,128)(2,1)S(1)} %collective-permute-done.11.refs_0_), channel_id=1, source_target_pairs={{0,96},{32,64},{64,32},{96,0},{1,97},{33,65},{65,33},{97,1},{2,98}... | collective-permute-start | bytes 786440 | tf_op jit(solution)/shard_map/ppermute | solution.py:393
  95.6 5.1 %collective-permute-start.18 = (bf16[2,64,512]{2,1,0:T(8,128)(2,1)S(1)}, bf16[2,64,512]{2,1,0:T(8,128)(2,1)S(1)}, u32[]{:S(2)}, u32[]{:S(2)}) collective-permute-start(bf16[2,64,512]{2,1,0:T(8,128)(2,1)S(1)} %pad_maximum_fusion.6), channel_id=1, source_target_pairs={{0,2},{1,3},{2,0},{3,1},{4,6},{5,7},{6,4},{7,5},{8,10},{9,11},{10,... | collective-permute-start | bytes 393224 | tf_op jit(solution)/shard_map/ppermute | solution.py:393
  96.2 11.9 %collective-permute-start.19 = (bf16[2,64,512]{2,1,0:T(8,128)(2,1)S(1)}, bf16[2,64,512]{2,1,0:T(8,128)(2,1)S(1)}, u32[]{:S(2)}, u32[]{:S(2)}) collective-permute-start(bf16[2,64,512]{2,1,0:T(8,128)(2,1)S(1)} %pad_maximum_fusion.6), channel_id=1, source_target_pairs={{0,3},{1,2},{2,1},{3,0},{4,7},{5,6},{6,5},{7,4},{8,11},{9,10},{10,... | collective-permute-start | bytes 393224 | tf_op jit(solution)/shard_map/ppermute | solution.py:393
  108.1 4.1 %copy-start.11 = (bf16[512,256]{1,0:T(8,128)(2,1)}, bf16[512,256]{1,0:T(8,128)(2,1)S(1)}, u32[]{:S(2)}) copy-start(bf16[512,256]{1,0:T(8,128)(2,1)S(1)} %collective-permute-done.20.refs_1_) | copy-start | bytes 786436
  108.1 4.1 %copy-start.12 = (bf16[512,256]{1,0:T(8,128)(2,1)}, bf16[512,256]{1,0:T(8,128)(2,1)S(1)}, u32[]{:S(2)}) copy-start(bf16[512,256]{1,0:T(8,128)(2,1)S(1)} %collective-permute-done.21.refs_2_) | copy-start | bytes 786436
  108.1 4.0 %copy-start.13 = (bf16[512,256]{1,0:T(8,128)(2,1)}, bf16[512,256]{1,0:T(8,128)(2,1)S(1)}, u32[]{:S(2)}) copy-start(bf16[512,256]{1,0:T(8,128)(2,1)S(1)} %collective-permute-done.22.refs_3_) | copy-start | bytes 786436
  108.1 11.0 %collective-permute-start.24 = (bf16[4,64,512]{2,1,0:T(8,128)(2,1)S(1)}, bf16[4,64,512]{2,1,0:T(8,128)(2,1)S(1)}, u32[]{:S(2)}, u32[]{:S(2)}) collective-permute-start(bf16[4,64,512]{2,1,0:T(8,128)(2,1)S(1)} %pad_maximum_fusion.1.refs_0_), channel_id=1, source_target_pairs={{0,32},{32,0},{64,96},{96,64},{1,33},{33,1},{65,97},{97,65},{2,34}... | collective-permute-start | bytes 786440 | tf_op jit(solution)/shard_map/ppermute | solution.py:393
  108.2 11.6 %collective-permute-start.25 = (bf16[4,64,512]{2,1,0:T(8,128)(2,1)S(1)}, bf16[4,64,512]{2,1,0:T(8,128)(2,1)S(1)}, u32[]{:S(2)}, u32[]{:S(2)}) collective-permute-start(bf16[4,64,512]{2,1,0:T(8,128)(2,1)S(1)} %pad_maximum_fusion.1.refs_0_), channel_id=1, source_target_pairs={{0,64},{32,96},{64,0},{96,32},{1,65},{33,97},{65,1},{97,33},{2,66}... | collective-permute-start | bytes 786440 | tf_op jit(solution)/shard_map/ppermute | solution.py:393
  109.6 13.4 %collective-permute-start.26 = (bf16[4,64,512]{2,1,0:T(8,128)(2,1)S(1)}, bf16[4,64,512]{2,1,0:T(8,128)(2,1)S(1)}, u32[]{:S(2)}, u32[]{:S(2)}) collective-permute-start(bf16[4,64,512]{2,1,0:T(8,128)(2,1)S(1)} %pad_maximum_fusion.1.refs_0_), channel_id=1, source_target_pairs={{0,96},{32,64},{64,32},{96,0},{1,97},{33,65},{65,33},{97,1},{2,98}... | collective-permute-start | bytes 786440 | tf_op jit(solution)/shard_map/ppermute | solution.py:393
  119.1 10.1 %copy-start.2 = (f32[512,256]{1,0:T(8,128)S(1)}, f32[512,256]{1,0:T(8,128)}, u32[]{:S(2)}) copy-start(f32[512,256]{1,0:T(8,128)} %get-tuple-element.64.one_ref) | copy-start | bytes 1572868
  123.7 5.5 %collective-permute-start.27 = (bf16[2,128,2048]{2,1,0:T(8,128)(2,1)S(1)}, bf16[2,128,2048]{2,1,0:T(8,128)(2,1)S(1)}, u32[]{:S(2)}, u32[]{:S(2)}) collective-permute-start(bf16[2,128,2048]{2,1,0:T(8,128)(2,1)S(1)} %assemble.1.near_ref), channel_id=1, source_target_pairs={{0,16},{16,0},{1,17},{17,1},{2,18},{18,2},{3,19},{19,3},{4,20},{20... | collective-permute-start | bytes 3145736 | tf_op jit(solution)/shard_map/ppermute | solution.py:393
  126.0 3.2 %collective-permute-start.23 = (f32[512,256]{1,0:T(8,128)}, f32[512,256]{1,0:T(8,128)S(1)}, u32[]{:S(2)}, u32[]{:S(2)}) collective-permute-start(f32[512,256]{1,0:T(8,128)} %get-tuple-element.65), channel_id=1, source_target_pairs={{0,16},{16,0},{1,17},{17,1},{2,18},{18,2},{3,19},{19,3},{4,20},{20... | collective-permute-start | bytes 1572872 | tf_op jit(solution)/shard_map/ppermute | solution.py:393
where the time goes:
time: 143 us
  starting transfers between devices  47 us (33%)
  Pallas kernels  44.1 us (31%)
  waiting for transfers between devices  39.6 us (28%)
  other arithmetic  5.98 us (4%)
  local copies, waits for them, and re-layouts  4.61 us (3%)
    ppermute x27, starting transfers between devices, flip(): return lax.ppermute(v, axis, [(i, i ^ bits) for i in range(n)])  40.8 us
    ppermute x27, waiting for transfers between devices, flip(): return lax.ppermute(v, axis, [(i, i ^ bits) for i in range(n)])  38.3 us
    pallas_call x1, Pallas kernels, attention(): pl.pallas_call(attention_kernel, grid_spec=pltpu.PrefetchScalarGridSpec(n...  13.1 us
    pallas_call x2, Pallas kernels, q_project(): pl.pallas_call(functools.partial(q_kernel, first), in_specs=[HBM] * 6 + [...  12.6 us
    pallas_call x1, Pallas kernels, norm(): pl.pallas_call(norm_kernel, grid_spec=pltpu.PrefetchScalarGridSpec(num_sc...  9.27 us
    pallas_call x1, Pallas kernels, kv_project(): pl.pallas_call(kv_kernel, in_specs=[HBM] * 6, out_specs=[full((64, rows))...  7.52 us
    ppermute x1, starting transfers between devices, local(): over = lax.ppermute(piece, (ZH, ZL), [(i, 4 + (3 - i)) for i in range(4)])  6.22 us
    unnamed x40, local copies, waits for them, and re-layouts  2.94 us
  transfers between devices with their start and end apart: 28, of which 15 were waited for; matrix products, arithmetic and copies ran while one was open for 4% of the time, Pallas kernels for 21%

commit v1 on v0

--- a/solution.py
+++ b/solution.py
@@ -88,29 +88,25 @@
 
 def kv_kernel(near_ref, far_ref, *refs):
     w_refs = refs[:4]
-    own_ref, other_ref, nbuf, wbuf, left, right, nsem, wsem = refs[4:]
+    own_ref, other_ref, nbuf, wbuf, acc, nsem, wsem = refs[4:]
     fetch((near_ref, far_ref), (0, 4, 1, 5, 2, 6, 3, 7), nbuf, nsem, w_refs, wbuf, wsem)
-    left[...] = jnp.zeros_like(left)
-    right[...] = jnp.zeros_like(right)
+    acc[...] = jnp.zeros_like(acc)
 
     def step(i, carry):
         pltpu.make_async_copy(w_refs[0], wbuf.at[i], wsem.at[i]).wait()
-        w0, w1 = wbuf[i, :256, :], wbuf[i, 256:, :]
         for t in range(2):
+            out = None
             for r in range(2):
-                pltpu.make_async_copy(near_ref.at[0], nbuf.at[t, 2 * i + r], nsem.at[t, 2 * i + r]).wait()
-            n0, n1 = nbuf.at[t, 2 * i], nbuf.at[t, 2 * i + 1]
-            left[t] += jnp.dot(n0[:, :256], w0, preferred_element_type=F32) + jnp.dot(
-                n1[:, :256], w1, preferred_element_type=F32
-            )
-            right[t] += jnp.dot(n0[:, 256:], w0, preferred_element_type=F32) + jnp.dot(
-                n1[:, 256:], w1, preferred_element_type=F32
-            )
+                k = 2 * i + r
+                pltpu.make_async_copy(near_ref.at[0], nbuf.at[t, k], nsem.at[t, k]).wait()
+                part = jnp.dot(nbuf[t, k], wbuf[i, r], preferred_element_type=F32)
+                out = part if out is None else out + part
+            acc[t] += out
         return carry
 
     lax.fori_loop(0, 4, step, 0)
     for t, o_ref in ((0, own_ref), (1, other_ref)):
-        o_ref[...] = left[t].T[:64] + right[t].T[64:]
+        o_ref[...] = acc[t].T
 
 
 def kv_project(near, far, pieces):
@@ -118,12 +114,11 @@
     return pl.pallas_call(
         kv_kernel,
         in_specs=[HBM] * 6,
-        out_specs=[full((64, rows))] * 2,
-        out_shape=[jax.ShapeDtypeStruct((64, rows), F32)] * 2,
+        out_specs=[full((128, rows))] * 2,
+        out_shape=[jax.ShapeDtypeStruct((128, rows), F32)] * 2,
         scratch_shapes=[
             pltpu.VMEM((2, parts, rows, width), BF),
-            pltpu.VMEM((4, 512, 128), BF),
-            pltpu.VMEM((2, rows, 128), F32),
+            pltpu.VMEM((4, 2, 512, 128), BF),
             pltpu.VMEM((2, rows, 128), F32),
             pltpu.SemaphoreType.DMA((2, 8)),
             pltpu.SemaphoreType.DMA((4,)),
@@ -136,11 +131,10 @@
 
 def kv_finish_kernel(one_ref, two_ref, bias_ref, cos_ref, sin_ref, o_ref):
     kv = one_ref[...] + two_ref[...] + bias_ref[:, :1]
-    first, second = kv[:16], kv[16:32]
+    first, second = kv[:64], kv[64:]
     cos, sin = cos_ref[...], sin_ref[...]
-    o_ref[0:16] = (first * cos - second * sin).astype(BF)
-    o_ref[16:32] = (second * cos + first * sin).astype(BF)
-    o_ref[32:64] = kv[32:64].astype(BF)
+    o_ref[0:64] = (first * cos - second * sin).astype(BF)
+    o_ref[64:128] = (second * cos + first * sin).astype(BF)
 
 
 def kv_finish(one, two, bias, cos, sin):
@@ -201,78 +195,65 @@
     )(near, far, *pieces, *so_far)
 
 
-def choose_kernel(tab, *refs):
+def choose_kernel(row_tab, col_tab, *refs):
     sources, outs = refs[:4], refs[4:]
-    for e in range(4):
-        for d in range(4):
-
-            @pl.when(tab[e] == d)
+    for f in range(4):
+        for e in range(4):
+
+            @pl.when(row_tab[f] == e)
             def _():
-                outs[e][...] = sources[d][...]
-
-
-def choose(tab, sources):
+                outs[f][...] = sources[e][col_tab[f]]
+
+
+def choose(row_tab, col_tab, sources):
     shape = sources[0].shape
     return pl.pallas_call(
         choose_kernel,
+        grid_spec=pltpu.PrefetchScalarGridSpec(
+            num_scalar_prefetch=2,
+            grid=(1,),
+            in_specs=[full(shape)] * 4,
+            out_specs=[full(shape[1:])] * 4,
+        ),
+        out_shape=[jax.ShapeDtypeStruct(shape[1:], BF)] * 4,
+        compiler_params=pltpu.CompilerParams(vmem_limit_bytes=8 << 20),
+        cost_estimate=CHEAP,
+        name="choose",
+    )(row_tab, col_tab, *sources)
+
+
+def q_finish_kernel(order, one_ref, two_ref, bias_ref, cos_ref, sin_ref, *outs):
+    for d, o_ref in enumerate(outs):
+        rows = pl.ds(pl.multiple_of(order[d] * 128, 128), 128)
+        for h in range(2):
+            cols = slice(h * 128, (h + 1) * 128)
+            u = one_ref[rows, cols] + two_ref[rows, cols] + bias_ref[0:1, cols].astype(F32)
+            o_ref[:, cols] = (u * cos_ref[rows, :] + pltpu.roll(u, 64, 1) * sin_ref[rows, :]).astype(BF)
+
+
+def q_finish(order, one, two, bias, cos, sin):
+    inputs = [one, two, bias, cos, sin]
+    return pl.pallas_call(
+        q_finish_kernel,
         grid_spec=pltpu.PrefetchScalarGridSpec(
             num_scalar_prefetch=1,
             grid=(1,),
-            in_specs=[full(shape)] * 4,
-            out_specs=[full(shape)] * 4,
+            in_specs=[full(v.shape) for v in inputs],
+            out_specs=[full((128, 256))] * 4,
         ),
-        out_shape=[jax.ShapeDtypeStruct(shape, BF)] * 4,
+        out_shape=[jax.ShapeDtypeStruct((128, 256), BF)] * 4,
         compiler_params=pltpu.CompilerParams(vmem_limit_bytes=8 << 20),
         cost_estimate=CHEAP,
-        name="choose",
-    )(tab, *sources)
-
-
-def settle_kernel(tab, *refs):
-    w_ref, bias_ref = refs[4:]
-    for d in range(4):
-
-        @pl.when(tab[0] == d)
-        def _():
-            w_ref[...] = refs[d][:512, :]
-            bias_ref[...] = refs[d][512:, :].astype(F32)
-
-
-def settle(tab, candidates):
-    outs = [jax.ShapeDtypeStruct((512, 256), BF), jax.ShapeDtypeStruct((16, 256), F32)]
-    return pl.pallas_call(
-        settle_kernel,
-        grid_spec=pltpu.PrefetchScalarGridSpec(
-            num_scalar_prefetch=1,
-            grid=(1,),
-            in_specs=[full(candidates[0].shape)] * 4,
-            out_specs=[full(o.shape) for o in outs],
-        ),
-        out_shape=outs,
-        compiler_params=pltpu.CompilerParams(vmem_limit_bytes=8 << 20),
-        cost_estimate=CHEAP,
-        name="settle",
-    )(tab, *candidates)
-
-
-def place(ref_piece, j, kt, vt, col):
-    krow = pl.multiple_of(j * 16, 16)
-    vrow = pl.multiple_of(j * 32, 32)
-    kt[pl.ds(krow, 16), pl.ds(col, 512)] = ref_piece[0:16, :]
-    kt[pl.ds(krow + 64, 16), pl.ds(col, 512)] = ref_piece[16:32, :]
-    vt[pl.ds(vrow, 32), pl.ds(col, 512)] = ref_piece[32:64, :]
+        name="q_finish",
+    )(order, *inputs)
 
 
 def assemble_kernel(tab, *refs):
     o_ref = refs[4]
     for a in range(4):
         col = pl.multiple_of(tab[8 + a] * 512, 512)
-
-        def one(d, carry):
-            place(refs[a].at[d], tab[16 + d], o_ref.at[0], o_ref.at[1], col)
-            return carry
-
-        lax.fori_loop(0, 4, one, 0)
+        for i in range(2):
+            o_ref[i, :, pl.ds(col, 512)] = refs[a][tab[5] ^ i]
 
 
 def assemble(tab, base):
@@ -292,25 +273,21 @@
     )(tab, *base)
 
 
-def attention_kernel(
-    tab, one_ref, two_ref, bias_ref, cos_ref, sin_ref, own_ref, near_ref, far_ref, o_ref, qs, kv, own_kt, own_vt, sems
-):
-    core = tab[24]
+def attention_kernel(tab, q0, q1, q2, q3, own_ref, near_ref, far_ref, o_ref, qs, kv, sems):
+    core, value_side = tab[4], tab[5]
     copies = [
         pltpu.make_async_copy(ref, kv.at[place_at], sems.at[i])
         for i, (ref, place_at) in enumerate(((near_ref, core), (far_ref, 1 - core)))
     ]
     for copy in copies:
         copy.start()
-    for d in range(4):
-        place(own_ref.at[d], tab[20 + d], own_kt, own_vt, 0)
-    for blk in range(2):
-        rows = slice(blk * 256, (blk + 1) * 256)
+    own_kt = own_ref.at[value_side]
+    own_vt = own_ref.at[value_side ^ 1]
+    for f, q_ref in enumerate((q0, q1, q2, q3)):
+        where = tab[12 + f]
+        off = pl.multiple_of(lax.rem(where, 2) * 128, 128)
         for h in range(2):
-            cols = slice(h * 128, (h + 1) * 128)
-            u = one_ref[rows, cols] + two_ref[rows, cols] + bias_ref[0:1, cols]
-            turned = u * cos_ref[rows, :] + pltpu.roll(u, 64, 1) * sin_ref[rows, :]
-            qs[blk, h * 256 : (h + 1) * 256, :] = turned.astype(BF)
+            qs[where // 2, pl.ds(h * 256 + off, 128), :] = q_ref[:, h * 128 : (h + 1) * 128]
 
     factor = (128 ** -0.5) * math.log2(math.e)
 
@@ -336,6 +313,16 @@
         p = jnp.where(mask, jnp.exp2(s - top), 0.0)
         return (top, lanes(p), pv(p, own_vt[:, c0 : c0 + 256]))
 
+    def wide(blk, i, state):
+        top, total, acc = state
+        keys = pl.ds(pl.multiple_of(i * 512, 512), 512)
+        ss = [jnp.dot(qs[blk], kv[side, 0, :, keys], preferred_element_type=F32) * factor for side in range(2)]
+        new = jnp.maximum(top, jnp.max(jnp.maximum(ss[0], ss[1]), axis=1, keepdims=True))
+        ps = [jnp.exp2(s - new) for s in ss]
+        decay = jnp.exp2(top - new)
+        total = total * decay + (lanes(ps[0]) + lanes(ps[1]))
+        return (new, total, acc * decay + (pv(ps[0], kv[0, 1, :, keys]) + pv(ps[1], kv[1, 1, :, keys])))
+
     def step(blk, c, width, state):
         top, total, acc = state
         side = lax.rem(c, 2)
@@ -351,7 +338,8 @@
         copy.wait()
     for blk in range(2):
         n = tab[blk]
-        state = lax.fori_loop(0, n // 2, lambda c, st: step(blk, c, 512, st), states[blk])
+        state = lax.fori_loop(0, n // 4, lambda i, st: wide(blk, i, st), states[blk])
+        state = lax.fori_loop(n // 4 * 2, n // 2, lambda c, st: step(blk, c, 512, st), state)
         state = lax.fori_loop(0, lax.rem(n, 2), lambda i, st: step(blk, n // 2, 256, st), state)
         top, total, acc = state
         result = (acc / jnp.sum(total, axis=1, keepdims=True)).astype(BF)
@@ -359,8 +347,8 @@
             o_ref[blk * 256 : (blk + 1) * 256, h * 128 : (h + 1) * 128] = result[h * 256 : (h + 1) * 256]
 
 
-def attention(tab, one, two, bias, cos, sin, own, near, far):
-    inputs = [one, two, bias, cos, sin, own]
+def attention(tab, candidates, own, near, far):
+    inputs = [*candidates, own]
     return pl.pallas_call(
         attention_kernel,
         grid_spec=pltpu.PrefetchScalarGridSpec(
@@ -371,8 +359,6 @@
             scratch_shapes=[
                 pltpu.VMEM((2, 512, 128), BF),
                 pltpu.VMEM((2, 2, 128, 2048), BF),
-                pltpu.VMEM((128, 512), BF),
-                pltpu.VMEM((128, 512), BF),
                 pltpu.SemaphoreType.DMA((2,)),
             ],
         ),
@@ -421,39 +407,22 @@
     order = ((zh ^ ((ks >> 2) & 1)) * 4 + (x ^ (ks & 3))) * 2 + (core ^ (ks >> 3))
     near, far_out = norm(hidden, norm_gain, order)
 
-    head = lax.dynamic_index_in_dim(trainer_kv, y, 0, keepdims=False)
-    out_col = jnp.arange(128, dtype=jnp.int32) % 64
-    wanted = jnp.where(
-        out_col < 16,
-        zl * 16 + out_col,
-        jnp.where(out_col < 32, 64 + zl * 16 + out_col - 16, 128 + zl * 32 + out_col - 32),
+    value_side = zl & 1
+    half_at = lambda v: lax.dynamic_slice_in_dim(
+        lax.dynamic_index_in_dim(v, y, 0, keepdims=False), value_side * 128, 128, v.ndim - 2
     )
-    side = jnp.arange(128, dtype=jnp.int32) // 64
-    pick = jnp.arange(256, dtype=jnp.int32)[:, None] == wanted[None, :]
-    pick_l = (pick & (side == 0)[None, :]).astype(BF)
-    pick_r = (pick & (side == 1)[None, :]).astype(BF)
-    packed = (
-        jnp.dot(head[:256], pick_l, preferred_element_type=F32)
-        + jnp.dot(head[256:], pick_r, preferred_element_type=F32)
-    ).astype(BF)
-    head_bias = lax.dynamic_index_in_dim(trainer_kv_bias, y, 0, keepdims=False).astype(F32)
-    own_bias = jnp.sum(jnp.where(pick[:, :64], head_bias[:, None], 0.0), axis=0)
-    own_bias = jnp.broadcast_to(own_bias[:, None], (64, 128))
-
-    source = lambda tz: jnp.sum(
-        jnp.where(matching[None, :] == (y * 4 + tz)[:, None], jnp.arange(16, dtype=jnp.int32)[None, :], 0), axis=1
-    )
-    src = source(zl ^ four)
-    bias_rows = jnp.broadcast_to(trainer_query_bias, (16, 256))
-    block = jnp.concatenate([trainer_query[0], bias_rows], axis=0)
-    gathered = [block] + [flip(block, Y, e) for e in (1, 2, 3)]
-    both = jnp.concatenate([packed, flip(packed, ZH, 1)], axis=0)
-    tab_1 = ((src // 4) ^ y).astype(jnp.int32)
-    sent = choose(after(tab_1, near, both), gathered)
-    both = after(both, sent[0])
+    packed = half_at(trainer_kv)
+    own_bias = jnp.broadcast_to(half_at(trainer_kv_bias).astype(F32)[:, None], (128, 128))
+
+    s0 = trainer_query[0]
+    z0 = flip(s0, ZH, 1)
+    both = jnp.stack([packed, flip(packed, ZH, 1)])
+    s_near = [s0] + [flip(s0, X, d) for d in (1, 2, 3)]
+    near, far_out, z0, both, *s_near = lax.optimization_barrier((near, far_out, z0, both, *s_near))
+    far = flip(far_out, CORE, 1)
     p_near = [both] + [flip(both, X, d) for d in (1, 2, 3)]
-    far = flip(after(far_out, sent[0]), CORE, 1)
-    candidates = [sent[0]] + [flip(sent[f], ZL, f) for f in (1, 2, 3)]
+    z0 = after(z0, p_near[1])
+    z_near = [z0] + [flip(z0, X, d) for d in (1, 2, 3)]
 
     counts = jnp.sum((block_lists >= 0).astype(jnp.int32), axis=1)
     token = jnp.arange(rows, dtype=jnp.int32)
@@ -463,31 +432,35 @@
     cosine, sine = jnp.cos(angles), jnp.sin(angles)
     cos2 = jnp.concatenate([cosine, cosine], axis=1)
     sin2 = jnp.concatenate([-sine, sine], axis=1)
-    own_freqs = lax.dynamic_slice_in_dim(freqs, zl * 16, 16, 0)
-    own_angles = own_freqs[:, None] * positions.astype(F32)[None, :]
-    cos_t, sin_t = jnp.cos(own_angles), jnp.sin(own_angles)
-
-    tab_2 = ((src[:1] % 4) ^ zl).astype(jnp.int32)
-    s0, bias = settle(after(tab_2, far, *p_near), candidates)
-    z0 = flip(s0, ZH, 1)
-    s_near = [s0] + [flip(s0, X, d) for d in (1, 2, 3)]
-
-    kv_own, kv_other = kv_project(after(near, s0), far, p_near)
-    kv_other, z0, *s_near = lax.optimization_barrier((kv_other, z0, *s_near))
-    z_near = [z0] + [flip(z0, X, d) for d in (1, 2, 3)]
+    cos_t = jnp.where(value_side == 0, cosine.T, 1.0)
+    sin_t = jnp.where(value_side == 0, sine.T, 0.0)
+
+    q_half = list(q_project(0, near, far, s_near, []))
+    kv_own, kv_other = kv_project(after(near, q_half[0]), far, p_near)
+    kv_other, q_half[0], *z_near = lax.optimization_barrier((kv_other, q_half[0], *z_near))
     piece = kv_finish(kv_own, flip(kv_other, CORE, 1), own_bias, cos_t, sin_t)
-    over = lax.ppermute(piece, (ZH, ZL), [(i, 4 + (3 - i)) for i in range(4)])
+    over = flip(piece, ZH, 1)
     start = jnp.where(zh == 0, piece, over)
     pair = jnp.stack([start, piece])
-    pairs = [pair] + [flip(pair, ZL, d) for d in (1, 2, 3)]
-    base0 = jnp.stack([p[0] for p in pairs])
-    own = jnp.stack([p[1] for p in pairs])
-    q_half = list(q_project(0, near, far, s_near, []))
-    base0, q_half[0], *z_near = lax.optimization_barrier((base0, q_half[0], *z_near))
+    mate = flip(pair, ZL, 1)
+    base0 = jnp.stack([pair[0], mate[0]])
+    own = jnp.stack([pair[1], mate[1]])
+
+    q_own, q_other = q_project(4, near, far, z_near, q_half)
+    parts = q_finish(zl ^ four, q_own, flip(q_other, CORE, 1), trainer_query_bias, cos2, sin2)
+    mine = jnp.stack([parts[0]] + [flip(parts[d], ZL, d) for d in (1, 2, 3)])
+    mine, base0 = lax.optimization_barrier((mine, base0))
+    gathered = [mine] + [flip(mine, Y, e) for e in (1, 2, 3)]
     base_near = [base0] + [flip(base0, X, d) for d in (1, 2, 3)]
-    q_own, q_other = q_project(4, near, far, z_near, q_half)
-    q_two = flip(q_other, CORE, 1)
-    base_near[0] = after(base_near[0], q_own)
+    target = y * 4 + (zl ^ four)
+    src = jnp.sum(
+        jnp.where(matching[None, :] == target[:, None], jnp.arange(16, dtype=jnp.int32)[None, :], 0), axis=1
+    )
+    tab_1 = ((src // 4) ^ y).astype(jnp.int32)
+    tab_1, *base_near = lax.optimization_barrier((tab_1, *base_near))
+    sent = choose(tab_1, ((src % 4) ^ zl).astype(jnp.int32), gathered)
+    base_near[0] = after(base_near[0], sent[0])
+    candidates = [sent[0]] + [flip(sent[f], ZL, f) for f in (1, 2, 3)]
 
     blocks = ctx * 2 + jnp.arange(2, dtype=jnp.int32)
     slots = jnp.arange(16, dtype=jnp.int32)
@@ -499,16 +472,15 @@
         [
             counts - 1,
             live,
-            jnp.zeros((4,), jnp.int32),
+            core[None],
+            value_side[None],
+            jnp.zeros((2,), jnp.int32),
             x ^ four,
-            jnp.zeros((4,), jnp.int32),
-            zl ^ four ^ (3 * zh),
             zl ^ four,
-            core[None],
         ]
     ).astype(jnp.int32)
     whole = assemble(tab, base_near)
-    return attention(tab, q_own, q_two, bias, cos2, sin2, own, whole, flip(whole, CORE, 1))
+    return attention(tab, candidates, own, whole, flip(whole, CORE, 1))
 
 
 def solution(mesh):

time: 143 us -> 130 us (0.909)
  waiting for transfers between devices: 39.6 us -> 31.2 us
  starting transfers between devices: 47 us -> 44.1 us
  other arithmetic: 5.98 us -> 4.5 us
    ppermute x27 -> x29, waiting for transfers between devices: 38.3 us -> 31.2 us  [flip(): return lax.ppermute(v, axis, [(i, i ^ bits) for i in range(n)])]
    ppermute x1 -> x0, starting transfers between devices: 6.22 us -> none  [local(): over = lax.ppermute(piece, (ZH, ZL), [(i, 4 + (3 - i)) for i in range(4)])]
    ppermute x27 -> x29, starting transfers between devices: 40.8 us -> 44.1 us  [flip(): return lax.ppermute(v, axis, [(i, i ^ bits) for i in range(n)])]
    pallas_call x1, Pallas kernels: 13.1 us -> 11.4 us  [attention(): pl.pallas_call(attention_kernel, grid_spec=pltpu.PrefetchScalarGridSpec(n...]
    unnamed x40 -> x36, local copies, waits for them, and re-layouts: 2.94 us -> 4.03 us
  transfers between devices with their start and end apart: 28 -> 29, of which waited for: 15 -> 15; matrix products, arithmetic and copies ran while one was open for 4% -> 5% of each run, Pallas kernels for 21% -> 23%
where the time goes in v1:
time: 130 us
  starting transfers between devices  44.1 us (34%)
  Pallas kernels  43.3 us (33%)
  waiting for transfers between devices  31.2 us (24%)
  local copies, waits for them, and re-layouts  5.83 us (4%)
  other arithmetic  4.5 us (3%)
    ppermute x29, starting transfers between devices, flip(): return lax.ppermute(v, axis, [(i, i ^ bits) for i in range(n)])  44.1 us
    ppermute x29, waiting for transfers between devices, flip(): return lax.ppermute(v, axis, [(i, i ^ bits) for i in range(n)])  31.2 us
    pallas_call x2, Pallas kernels, q_project(): pl.pallas_call(functools.partial(q_kernel, first), in_specs=[HBM] * 6 + [...  12.6 us
    pallas_call x1, Pallas kernels, attention(): pl.pallas_call(attention_kernel, grid_spec=pltpu.PrefetchScalarGridSpec(n...  11.4 us
    pallas_call x1, Pallas kernels, norm(): pl.pallas_call(norm_kernel, grid_spec=pltpu.PrefetchScalarGridSpec(num_sc...  9.27 us
    pallas_call x1, Pallas kernels, kv_project(): pl.pallas_call(kv_kernel, in_specs=[HBM] * 6, out_specs=[full((128, rows)...  7.85 us
    unnamed x36, local copies, waits for them, and re-layouts  4.03 us
  transfers between devices with their start and end apart: 29, of which 15 were waited for; matrix products, arithmetic and copies ran while one was open for 5% of the time, Pallas kernels for 23%

profile of v1, /device:TPU:39, one launch (start us, length us, event | category | flops | bytes accessed | tf_op | source)
XLA Modules:
  0.0 129.6 jit_solution(5670047457912568866)
XLA Ops:
  0.0 6.0 %collective-permute-start = (bf16[512,256]{1,0:T(8,128)(2,1)}, bf16[512,256]{1,0:T(8,128)(2,1)S(1)}, u32[]{:S(2)}, u32[]{:S(2)}) collective-permute-start(bf16[512,256]{1,0:T(8,128)(2,1)} %bitcast.21), channel_id=1, source_target_pairs={{0,128},{128,0},{1,129},{129,1},{2,130},{130,2},{3,131},{131,3},{4... | collective-permute-start | bytes 786440 | tf_op jit(solution)/shard_map/ppermute | solution.py:379
  6.6 0.8 collective-permute-start.3
  7.4 2.5 %collective-permute-start.4 = (bf16[512,256]{1,0:T(8,128)(2,1)}, bf16[512,256]{1,0:T(8,128)(2,1)S(1)}, u32[]{:S(2)}, u32[]{:S(2)}) collective-permute-start(bf16[512,256]{1,0:T(8,128)(2,1)} %bitcast.24), channel_id=1, source_target_pairs={{0,96},{32,64},{64,32},{96,0},{1,97},{33,65},{65,33},{97,1},{2,98}... | collective-permute-start | bytes 786440 | tf_op jit(solution)/shard_map/ppermute | solution.py:379
  10.2 0.7 reshape.47.g_ref
  10.9 9.3 %norm.1 = (bf16[8,512,512]{2,1,0:T(8,128)(2,1)S(1)}, bf16[8,512,512]{2,1,0:T(8,128)(2,1)S(1)}) custom-call(s32[16]{0:T(128)S(1)} %xor_add_fusion.order, bf16[512,8192]{1,0:T(8,128)(2,1)} %h_ref.1, bf16[1,8192]{1,0:T(2,128)(2,1)S(1)} %reshape.47.g_ref), custom_call_target="tpu_custom_call" | custom-call | bytes 20971520 | tf_op jit(solution)/shard_map/norm/pallas_call | solution.py:62
  20.2 2.0 %copy-done.1 = bf16[8,512,512]{2,1,0:T(8,128)(2,1)} copy-done((bf16[8,512,512]{2,1,0:T(8,128)(2,1)}, bf16[8,512,512]{2,1,0:T(8,128)(2,1)S(1)}, u32[]{:S(2)}) %copy-start.1) | copy-done | bytes 4194328
  22.3 1.2 collective-permute-done.1
  23.6 1.4 %collective-permute-start.5 = (bf16[8,512,512]{2,1,0:T(8,128)(2,1)S(1)}, bf16[8,512,512]{2,1,0:T(8,128)(2,1)S(1)}, u32[]{:S(2)}, u32[]{:S(2)}) collective-permute-start(bf16[8,512,512]{2,1,0:T(8,128)(2,1)S(1)} %get-tuple-element.48), channel_id=1, source_target_pairs={{0,16},{16,0},{1,17},{17,1},{2,18},{18,2},{3,19},{19,3},{4,20},{20... | collective-permute-start | bytes 12582920 | tf_op jit(solution)/shard_map/ppermute | solution.py:379
  25.8 0.7 fusion.14
  26.4 1.3 %fusion.4 = f32[512]{0:T(512)S(1)} fusion(s32[]{:T(128)} %bitcast.6, s32[]{:T(128)} %bitcast.5), kind=kLoop, calls=%fused_computation.17 | loop fusion | flops 6144 | bytes 2056 | tf_op jit(solution)/shard_map/convert_element_type | solution.py:431
  27.8 1.3 %collective-permute-start.7 = (bf16[2,512,128]{2,1,0:T(8,128)(2,1)S(1)}, bf16[2,512,128]{2,1,0:T(8,128)(2,1)}, u32[]{:S(2)}, u32[]{:S(2)}) collective-permute-start(bf16[2,512,128]{2,1,0:T(8,128)(2,1)S(1)} %pad_maximum_fusion.2.refs_0_), channel_id=1, source_target_pairs={{0,64},{32,96},{64,0},{96,32},{1,65},{33,97},{65,1},{97,33},{2,66}... | collective-permute-start | bytes 786440 | tf_op jit(solution)/shard_map/ppermute | solution.py:379
  29.1 2.0 %collective-permute-start.8 = (bf16[2,512,128]{2,1,0:T(8,128)(2,1)S(1)}, bf16[2,512,128]{2,1,0:T(8,128)(2,1)}, u32[]{:S(2)}, u32[]{:S(2)}) collective-permute-start(bf16[2,512,128]{2,1,0:T(8,128)(2,1)S(1)} %pad_maximum_fusion.2.refs_0_), channel_id=1, source_target_pairs={{0,96},{32,64},{64,32},{96,0},{1,97},{33,65},{65,33},{97,1},{2,98}... | collective-permute-start | bytes 786440 | tf_op jit(solution)/shard_map/ppermute | solution.py:379
  31.2 2.0 %collective-permute-done.6.refs_1_ = bf16[2,512,128]{2,1,0:T(8,128)(2,1)S(1)} collective-permute-done((bf16[2,512,128]{2,1,0:T(8,128)(2,1)S(1)}, bf16[2,512,128]{2,1,0:T(8,128)(2,1)S(1)}, u32[]{:S(2)}, u32[]{:S(2)}) %collective-permute-start.6) | collective-permute-done | bytes 262176 | tf_op jit(solution)/shard_map/ppermute | solution.py:379
  33.8 1.2 collective-permute-start.10
  35.0 2.1 %collective-permute-start.11 = (bf16[512,256]{1,0:T(8,128)(2,1)S(1)}, bf16[512,256]{1,0:T(8,128)(2,1)S(1)}, u32[]{:S(2)}, u32[]{:S(2)}) collective-permute-start(bf16[512,256]{1,0:T(8,128)(2,1)S(1)} %collective-permute-done.refs_0_), channel_id=1, source_target_pairs={{0,96},{32,64},{64,32},{96,0},{1,97},{33,65},{65,33},{97,1},{2,98}... | collective-permute-start | bytes 786440 | tf_op jit(solution)/shard_map/ppermute | solution.py:379
  37.1 1.0 fusion.2
  38.3 5.7 %q_project.2 = (f32[512,256]{1,0:T(8,128)}, f32[512,256]{1,0:T(8,128)}) custom-call(bf16[8,512,512]{2,1,0:T(8,128)(2,1)} %copy-done.1, bf16[8,512,512]{2,1,0:T(8,128)(2,1)} %copy-done.5, bf16[512,256]{1,0:T(8,128)(2,1)} %bitcast.25, bf16[512,256]{1,0:T(8,128)(2,1)} %copy-done.8, bf16[512,256]{1,0:T(8,128)(2,1)} %copy-done.9, bf16[512,256]{1,0:T(8,128)(2,1)} %copy-done.10), custom_call_target="tpu_custom_call" | custom-call | bytes 10485760 | tf_op jit(solution)/shard_map/q_project/pallas_call | solution.py:181
  44.1 7.8 %kv_project.1 = (f32[128,512]{1,0:T(8,128)}, f32[128,512]{1,0:T(8,128)}) custom-call(bf16[8,512,512]{2,1,0:T(8,128)(2,1)} %copy-done.1, bf16[8,512,512]{2,1,0:T(8,128)(2,1)} %copy-done.5, bf16[2,512,128]{2,1,0:T(8,128)(2,1)} %copy-done.6, bf16[2,512,128]{2,1,0:T(8,128)(2,1)} %copy-done.14, bf16[2,512,128]{2,1,0:T(8,128)(2,1)} %collective-permute-done.7.refs_2_, ...), custom_call_target="tpu_custom_call" | custom-call | bytes 20971520 | tf_op jit(solution)/shard_map/kv_project/pallas_call | solution.py:114
  52.0 2.8 %collective-permute-done.11.refs_3_ = bf16[512,256]{1,0:T(8,128)(2,1)S(1)} collective-permute-done((bf16[512,256]{1,0:T(8,128)(2,1)S(1)}, bf16[512,256]{1,0:T(8,128)(2,1)S(1)}, u32[]{:S(2)}, u32[]{:S(2)}) %collective-permute-start.11) | collective-permute-done | bytes 262176 | tf_op jit(solution)/shard_map/ppermute | solution.py:379
  54.8 1.1 collective-permute-start.16
  55.9 0.8 bitcast_convert_fusion
  57.4 1.0 copy-done.3
  58.4 5.1 %collective-permute-start.17 = (bf16[128,512]{1,0:T(8,128)(2,1)S(1)}, bf16[128,512]{1,0:T(8,128)(2,1)S(1)}, u32[]{:S(2)}, u32[]{:S(2)}) collective-permute-start(bf16[128,512]{1,0:T(8,128)(2,1)S(1)} %kv_finish.1), channel_id=1, source_target_pairs={{0,128},{128,0},{1,129},{129,1},{2,130},{130,2},{3,131},{131,3},{4... | collective-permute-start | bytes 393224 | tf_op jit(solution)/shard_map/ppermute | solution.py:379
  63.6 6.9 %q_project.3 = (f32[512,256]{1,0:T(8,128)}, f32[512,256]{1,0:T(8,128)}) custom-call(bf16[8,512,512]{2,1,0:T(8,128)(2,1)} %copy-done.1, bf16[8,512,512]{2,1,0:T(8,128)(2,1)} %copy-done.5, bf16[512,256]{1,0:T(8,128)(2,1)} %copy-done.7, bf16[512,256]{1,0:T(8,128)(2,1)} %copy-done.11, bf16[512,256]{1,0:T(8,128)(2,1)} %copy-done.12, bf16[512,256]{1,0:T(8,128)(2,1)} %copy-done.13, ...), custom_call_target="tpu_custom_call" | custom-call | bytes 10485760 | tf_op jit(solution)/shard_map/q_project/pallas_call | solution.py:181
  70.5 0.7 collective-permute-start.12
  71.9 1.1 collective-permute-done.12.two_ref
  73.0 1.0 copy-done.2
  74.0 0.7 q_finish.1
  75.2 2.0 %collective-permute-start.14 = (bf16[128,256]{1,0:T(8,128)(2,1)S(1)}, bf16[128,256]{1,0:T(8,128)(2,1)S(1)}, u32[]{:S(2)}, u32[]{:S(2)}) collective-permute-start(bf16[128,256]{1,0:T(8,128)(2,1)S(1)} %get-tuple-element.69), channel_id=1, source_target_pairs={{0,2},{1,3},{2,0},{3,1},{4,6},{5,7},{6,4},{7,5},{8,10},{9,11},{10,... | collective-permute-start | bytes 196616 | tf_op jit(solution)/shard_map/ppermute | solution.py:379
  77.5 0.8 collective-permute-done.15
  78.3 3.4 %collective-permute-done.14 = bf16[128,256]{1,0:T(8,128)(2,1)S(1)} collective-permute-done((bf16[128,256]{1,0:T(8,128)(2,1)S(1)}, bf16[128,256]{1,0:T(8,128)(2,1)S(1)}, u32[]{:S(2)}, u32[]{:S(2)}) %collective-permute-start.14) | collective-permute-done | bytes 65568 | tf_op jit(solution)/shard_map/ppermute | solution.py:379
  81.7 2.0 %collective-permute-done.13 = bf16[128,256]{1,0:T(8,128)(2,1)S(1)} collective-permute-done((bf16[128,256]{1,0:T(8,128)(2,1)S(1)}, bf16[128,256]{1,0:T(8,128)(2,1)S(1)}, u32[]{:S(2)}, u32[]{:S(2)}) %collective-permute-start.13) | collective-permute-done | bytes 65568 | tf_op jit(solution)/shard_map/ppermute | solution.py:379
  84.2 3.7 %collective-permute-start.20 = (bf16[2,128,512]{2,1,0:T(8,128)(2,1)S(1)}, bf16[2,128,512]{2,1,0:T(8,128)(2,1)S(1)}, u32[]{:S(2)}, u32[]{:S(2)}) collective-permute-start(bf16[2,128,512]{2,1,0:T(8,128)(2,1)S(1)} %pad_maximum_fusion.1.refs_0_), channel_id=1, source_target_pairs={{0,64},{32,96},{64,0},{96,32},{1,65},{33,97},{65,1},{97,33},{2,66}... | collective-permute-start | bytes 786440 | tf_op jit(solution)/shard_map/ppermute | solution.py:379
  88.1 1.3 %collective-permute-start.22 = (bf16[4,128,256]{2,1,0:T(8,128)(2,1)S(1)}, bf16[4,128,256]{2,1,0:T(8,128)(2,1)S(1)}, u32[]{:S(2)}, u32[]{:S(2)}) collective-permute-start(bf16[4,128,256]{2,1,0:T(8,128)(2,1)S(1)} %pad_maximum_fusion.5.refs_0_), channel_id=1, source_target_pairs={{0,4},{4,0},{8,12},{12,8},{1,5},{5,1},{9,13},{13,9},{2,6},{6,2},{1... | collective-permute-start | bytes 786440 | tf_op jit(solution)/shard_map/ppermute | solution.py:379
  89.4 2.6 %collective-permute-start.23 = (bf16[4,128,256]{2,1,0:T(8,128)(2,1)S(1)}, bf16[4,128,256]{2,1,0:T(8,128)(2,1)S(1)}, u32[]{:S(2)}, u32[]{:S(2)}) collective-permute-start(bf16[4,128,256]{2,1,0:T(8,128)(2,1)S(1)} %pad_maximum_fusion.5.refs_0_), channel_id=1, source_target_pairs={{0,8},{4,12},{8,0},{12,4},{1,9},{5,13},{9,1},{13,5},{2,10},{6,14},... | collective-permute-start | bytes 786440 | tf_op jit(solution)/shard_map/ppermute | solution.py:379
  92.0 1.7 %collective-permute-start.24 = (bf16[4,128,256]{2,1,0:T(8,128)(2,1)S(1)}, bf16[4,128,256]{2,1,0:T(8,128)(2,1)S(1)}, u32[]{:S(2)}, u32[]{:S(2)}) collective-permute-start(bf16[4,128,256]{2,1,0:T(8,128)(2,1)S(1)} %pad_maximum_fusion.5.refs_0_), channel_id=1, source_target_pairs={{0,12},{4,8},{8,4},{12,0},{1,13},{5,9},{9,5},{13,1},{2,14},{6,10},... | collective-permute-start | bytes 786440 | tf_op jit(solution)/shard_map/ppermute | solution.py:379
  93.8 5.0 %collective-permute-done.20.refs_2_ = bf16[2,128,512]{2,1,0:T(8,128)(2,1)S(1)} collective-permute-done((bf16[2,128,512]{2,1,0:T(8,128)(2,1)S(1)}, bf16[2,128,512]{2,1,0:T(8,128)(2,1)S(1)}, u32[]{:S(2)}, u32[]{:S(2)}) %collective-permute-start.20) | collective-permute-done | bytes 262176 | tf_op jit(solution)/shard_map/ppermute | solution.py:379
  98.9 2.5 %collective-permute-done.21.refs_3_ = bf16[2,128,512]{2,1,0:T(8,128)(2,1)S(1)} collective-permute-done((bf16[2,128,512]{2,1,0:T(8,128)(2,1)S(1)}, bf16[2,128,512]{2,1,0:T(8,128)(2,1)S(1)}, u32[]{:S(2)}, u32[]{:S(2)}) %collective-permute-start.21) | collective-permute-done | bytes 262176 | tf_op jit(solution)/shard_map/ppermute | solution.py:379
  101.4 1.0 collective-permute-done.23.refs_2_
  102.4 3.0 %collective-permute-done.24.refs_3_ = bf16[4,128,256]{2,1,0:T(8,128)(2,1)S(1)} collective-permute-done((bf16[4,128,256]{2,1,0:T(8,128)(2,1)S(1)}, bf16[4,128,256]{2,1,0:T(8,128)(2,1)S(1)}, u32[]{:S(2)}, u32[]{:S(2)}) %collective-permute-start.24) | collective-permute-done | bytes 262176 | tf_op jit(solution)/shard_map/ppermute | solution.py:379
  105.4 0.7 choose.1
  106.7 2.3 %collective-permute-start.28 = (bf16[2,128,2048]{2,1,0:T(8,128)(2,1)S(1)}, bf16[2,128,2048]{2,1,0:T(8,128)(2,1)S(1)}, u32[]{:S(2)}, u32[]{:S(2)}) collective-permute-start(bf16[2,128,2048]{2,1,0:T(8,128)(2,1)S(1)} %assemble.1.near_ref), channel_id=1, source_target_pairs={{0,16},{16,0},{1,17},{17,1},{2,18},{18,2},{3,19},{19,3},{4,20},{20... | collective-permute-start | bytes 3145736 | tf_op jit(solution)/shard_map/ppermute | solution.py:379
  109.0 1.3 %collective-permute-start.26 = (bf16[128,256]{1,0:T(8,128)(2,1)S(1)}, bf16[128,256]{1,0:T(8,128)(2,1)S(1)}, u32[]{:S(2)}, u32[]{:S(2)}) collective-permute-start(bf16[128,256]{1,0:T(8,128)(2,1)S(1)} %get-tuple-element.78), channel_id=1, source_target_pairs={{0,2},{1,3},{2,0},{3,1},{4,6},{5,7},{6,4},{7,5},{8,10},{9,11},{10,... | collective-permute-start | bytes 196616 | tf_op jit(solution)/shard_map/ppermute | solution.py:379
  110.3 1.4 %collective-permute-start.27 = (bf16[128,256]{1,0:T(8,128)(2,1)S(1)}, bf16[128,256]{1,0:T(8,128)(2,1)S(1)}, u32[]{:S(2)}, u32[]{:S(2)}) collective-permute-start(bf16[128,256]{1,0:T(8,128)(2,1)S(1)} %get-tuple-element.79), channel_id=1, source_target_pairs={{0,3},{1,2},{2,1},{3,0},{4,7},{5,6},{6,5},{7,4},{8,11},{9,10},{10,... | collective-permute-start | bytes 196616 | tf_op jit(solution)/shard_map/ppermute | solution.py:379
  111.7 1.0 collective-permute-done.25.q1
  112.6 1.3 collective-permute-done.26.q2
  113.9 4.1 %collective-permute-done.27.q3 = bf16[128,256]{1,0:T(8,128)(2,1)S(1)} collective-permute-done((bf16[128,256]{1,0:T(8,128)(2,1)S(1)}, bf16[128,256]{1,0:T(8,128)(2,1)S(1)}, u32[]{:S(2)}, u32[]{:S(2)}) %collective-permute-start.27) | collective-permute-done | bytes 65568 | tf_op jit(solution)/shard_map/ppermute | solution.py:379
  118.0 11.4 %attention.1 = bf16[512,256]{1,0:T(8,128)(2,1)} custom-call(s32[16]{0:T(128)S(1)} %concatenate.9.tab, bf16[128,256]{1,0:T(8,128)(2,1)S(1)} %get-tuple-element.76.q0, bf16[128,256]{1,0:T(8,128)(2,1)S(1)} %collective-permute-done.25.q1, bf16[128,256]{1,0:T(8,128)(2,1)S(1)} %collective-permute-done.26.q2, bf16[128,256]{1,0:T(8,128)(2,1)S(1)} %collective-permute-done.27.q3, ...), custom_call_target="tpu_custom_call" | custom-call | tf_op jit(solution)/shard_map/attention/pallas_call | solution.py:352
  (85 shorter events, 6.2 us)
Async XLA Ops:
  0.0 9.9 %copy-start = (bf16[4,512,256]{2,1,0:T(8,128)(2,1)S(1)}, bf16[4,512,256]{2,1,0:T(8,128)(2,1)}, u32[]{:S(2)}) copy-start(bf16[4,512,256]{2,1,0:T(8,128)(2,1)} %param.13) | copy-start | bytes 3145732
  0.0 23.5 %collective-permute-start = (bf16[512,256]{1,0:T(8,128)(2,1)}, bf16[512,256]{1,0:T(8,128)(2,1)S(1)}, u32[]{:S(2)}, u32[]{:S(2)}) collective-permute-start(bf16[512,256]{1,0:T(8,128)(2,1)} %bitcast.21), channel_id=1, source_target_pairs={{0,128},{128,0},{1,129},{129,1},{2,130},{130,2},{3,131},{131,3},{4... | collective-permute-start | bytes 786440 | tf_op jit(solution)/shard_map/ppermute | solution.py:379
  6.0 17.5 %collective-permute-start.2 = (bf16[512,256]{1,0:T(8,128)(2,1)}, bf16[512,256]{1,0:T(8,128)(2,1)S(1)}, u32[]{:S(2)}, u32[]{:S(2)}) collective-permute-start(bf16[512,256]{1,0:T(8,128)(2,1)} %bitcast.22), channel_id=1, source_target_pairs={{0,32},{32,0},{64,96},{96,64},{1,33},{33,1},{65,97},{97,65},{2,34}... | collective-permute-start | bytes 786440 | tf_op jit(solution)/shard_map/ppermute | solution.py:379
  6.6 17.0 %collective-permute-start.3 = (bf16[512,256]{1,0:T(8,128)(2,1)}, bf16[512,256]{1,0:T(8,128)(2,1)S(1)}, u32[]{:S(2)}, u32[]{:S(2)}) collective-permute-start(bf16[512,256]{1,0:T(8,128)(2,1)} %bitcast.23), channel_id=1, source_target_pairs={{0,64},{32,96},{64,0},{96,32},{1,65},{33,97},{65,1},{97,33},{2,66}... | collective-permute-start | bytes 786440 | tf_op jit(solution)/shard_map/ppermute | solution.py:379
  7.4 16.2 %collective-permute-start.4 = (bf16[512,256]{1,0:T(8,128)(2,1)}, bf16[512,256]{1,0:T(8,128)(2,1)S(1)}, u32[]{:S(2)}, u32[]{:S(2)}) collective-permute-start(bf16[512,256]{1,0:T(8,128)(2,1)} %bitcast.24), channel_id=1, source_target_pairs={{0,96},{32,64},{64,32},{96,0},{1,97},{33,65},{65,33},{97,1},{2,98}... | collective-permute-start | bytes 786440 | tf_op jit(solution)/shard_map/ppermute | solution.py:379
  10.0 13.5 %collective-permute-start.1 = (bf16[512,128]{1,0:T(8,128)(2,1)S(1)}, bf16[512,128]{1,0:T(8,128)(2,1)S(1)}, u32[]{:S(2)}, u32[]{:S(2)}) collective-permute-start(bf16[512,128]{1,0:T(8,128)(2,1)S(1)} %fusion.15), channel_id=1, source_target_pairs={{0,128},{128,0},{1,129},{129,1},{2,130},{130,2},{3,131},{131,3},{4... | collective-permute-start | bytes 393224 | tf_op jit(solution)/shard_map/ppermute | solution.py:379
  10.9 14.1 %copy-start.15 = (s32[2,17]{1,0:T(2,128)S(1)}, s32[2,17]{1,0:T(2,128)}, u32[]{:S(2)}) copy-start(s32[2,17]{1,0:T(2,128)} %param.16) | copy-start | bytes 412
  20.2 2.0 %copy-start.1 = (bf16[8,512,512]{2,1,0:T(8,128)(2,1)}, bf16[8,512,512]{2,1,0:T(8,128)(2,1)S(1)}, u32[]{:S(2)}) copy-start(bf16[8,512,512]{2,1,0:T(8,128)(2,1)S(1)} %get-tuple-element.54.near_ref) | copy-start | bytes 12582916
  23.5 20.5 %copy-start.6 = (bf16[2,512,128]{2,1,0:T(8,128)(2,1)}, bf16[2,512,128]{2,1,0:T(8,128)(2,1)S(1)}, u32[]{:S(2)}) copy-start(bf16[2,512,128]{2,1,0:T(8,128)(2,1)S(1)} %pad_maximum_fusion.2.refs_0_) | copy-start | bytes 786436
  23.5 20.5 %copy-start.7 = (bf16[512,256]{1,0:T(8,128)(2,1)}, bf16[512,256]{1,0:T(8,128)(2,1)S(1)}, u32[]{:S(2)}) copy-start(bf16[512,256]{1,0:T(8,128)(2,1)S(1)} %collective-permute-done.refs_0_) | copy-start | bytes 786436
  23.5 14.8 %copy-start.8 = (bf16[512,256]{1,0:T(8,128)(2,1)}, bf16[512,256]{1,0:T(8,128)(2,1)S(1)}, u32[]{:S(2)}) copy-start(bf16[512,256]{1,0:T(8,128)(2,1)S(1)} %collective-permute-done.2.refs_1_) | copy-start | bytes 786436
  23.6 14.7 %copy-start.9 = (bf16[512,256]{1,0:T(8,128)(2,1)}, bf16[512,256]{1,0:T(8,128)(2,1)S(1)}, u32[]{:S(2)}) copy-start(bf16[512,256]{1,0:T(8,128)(2,1)S(1)} %collective-permute-done.3.refs_2_) | copy-start | bytes 786436
  23.6 14.7 %copy-start.10 = (bf16[512,256]{1,0:T(8,128)(2,1)}, bf16[512,256]{1,0:T(8,128)(2,1)S(1)}, u32[]{:S(2)}) copy-start(bf16[512,256]{1,0:T(8,128)(2,1)S(1)} %collective-permute-done.4.refs_3_) | copy-start | bytes 786436
  23.6 11.4 %collective-permute-start.5 = (bf16[8,512,512]{2,1,0:T(8,128)(2,1)S(1)}, bf16[8,512,512]{2,1,0:T(8,128)(2,1)S(1)}, u32[]{:S(2)}, u32[]{:S(2)}) collective-permute-start(bf16[8,512,512]{2,1,0:T(8,128)(2,1)S(1)} %get-tuple-element.48), channel_id=1, source_target_pairs={{0,16},{16,0},{1,17},{17,1},{2,18},{18,2},{3,19},{19,3},{4,20},{20... | collective-permute-start | bytes 12582920 | tf_op jit(solution)/shard_map/ppermute | solution.py:379
  25.1 8.0 %collective-permute-start.6 = (bf16[2,512,128]{2,1,0:T(8,128)(2,1)S(1)}, bf16[2,512,128]{2,1,0:T(8,128)(2,1)S(1)}, u32[]{:S(2)}, u32[]{:S(2)}) collective-permute-start(bf16[2,512,128]{2,1,0:T(8,128)(2,1)S(1)} %pad_maximum_fusion.2.refs_0_), channel_id=1, source_target_pairs={{0,32},{32,0},{64,96},{96,64},{1,33},{33,1},{65,97},{97,65},{2,34}... | collective-permute-start | bytes 786440 | tf_op jit(solution)/shard_map/ppermute | solution.py:379
  27.8 16.3 %collective-permute-start.7 = (bf16[2,512,128]{2,1,0:T(8,128)(2,1)S(1)}, bf16[2,512,128]{2,1,0:T(8,128)(2,1)}, u32[]{:S(2)}, u32[]{:S(2)}) collective-permute-start(bf16[2,512,128]{2,1,0:T(8,128)(2,1)S(1)} %pad_maximum_fusion.2.refs_0_), channel_id=1, source_target_pairs={{0,64},{32,96},{64,0},{96,32},{1,65},{33,97},{65,1},{97,33},{2,66}... | collective-permute-start | bytes 786440 | tf_op jit(solution)/shard_map/ppermute | solution.py:379
  29.1 14.9 %collective-permute-start.8 = (bf16[2,512,128]{2,1,0:T(8,128)(2,1)S(1)}, bf16[2,512,128]{2,1,0:T(8,128)(2,1)}, u32[]{:S(2)}, u32[]{:S(2)}) collective-permute-start(bf16[2,512,128]{2,1,0:T(8,128)(2,1)S(1)} %pad_maximum_fusion.2.refs_0_), channel_id=1, source_target_pairs={{0,96},{32,64},{64,32},{96,0},{1,97},{33,65},{65,33},{97,1},{2,98}... | collective-permute-start | bytes 786440 | tf_op jit(solution)/shard_map/ppermute | solution.py:379
  33.1 1.8 %copy-start.14 = (bf16[2,512,128]{2,1,0:T(8,128)(2,1)}, bf16[2,512,128]{2,1,0:T(8,128)(2,1)S(1)}, u32[]{:S(2)}) copy-start(bf16[2,512,128]{2,1,0:T(8,128)(2,1)S(1)} %collective-permute-done.6.refs_1_) | copy-start | bytes 786436
  33.1 18.8 %collective-permute-start.9 = (bf16[512,256]{1,0:T(8,128)(2,1)S(1)}, bf16[512,256]{1,0:T(8,128)(2,1)S(1)}, u32[]{:S(2)}, u32[]{:S(2)}) collective-permute-start(bf16[512,256]{1,0:T(8,128)(2,1)S(1)} %collective-permute-done.refs_0_), channel_id=1, source_target_pairs={{0,32},{32,0},{64,96},{96,64},{1,33},{33,1},{65,97},{97,65},{2,34}... | collective-permute-start | bytes 786440 | tf_op jit(solution)/shard_map/ppermute | solution.py:379
  33.8 18.1 %collective-permute-start.10 = (bf16[512,256]{1,0:T(8,128)(2,1)S(1)}, bf16[512,256]{1,0:T(8,128)(2,1)S(1)}, u32[]{:S(2)}, u32[]{:S(2)}) collective-permute-start(bf16[512,256]{1,0:T(8,128)(2,1)S(1)} %collective-permute-done.refs_0_), channel_id=1, source_target_pairs={{0,64},{32,96},{64,0},{96,32},{1,65},{33,97},{65,1},{97,33},{2,66}... | collective-permute-start | bytes 786440 | tf_op jit(solution)/shard_map/ppermute | solution.py:379
  35.0 3.1 %copy-start.5 = (bf16[8,512,512]{2,1,0:T(8,128)(2,1)}, bf16[8,512,512]{2,1,0:T(8,128)(2,1)S(1)}, u32[]{:S(2)}) copy-start(bf16[8,512,512]{2,1,0:T(8,128)(2,1)S(1)} %collective-permute-done.5.far_ref) | copy-start | bytes 12582916
  35.0 19.8 %collective-permute-start.11 = (bf16[512,256]{1,0:T(8,128)(2,1)S(1)}, bf16[512,256]{1,0:T(8,128)(2,1)S(1)}, u32[]{:S(2)}, u32[]{:S(2)}) collective-permute-start(bf16[512,256]{1,0:T(8,128)(2,1)S(1)} %collective-permute-done.refs_0_), channel_id=1, source_target_pairs={{0,96},{32,64},{64,32},{96,0},{1,97},{33,65},{65,33},{97,1},{2,98}... | collective-permute-start | bytes 786440 | tf_op jit(solution)/shard_map/ppermute | solution.py:379
  51.9 11.6 %copy-start.11 = (bf16[512,256]{1,0:T(8,128)(2,1)}, bf16[512,256]{1,0:T(8,128)(2,1)S(1)}, u32[]{:S(2)}) copy-start(bf16[512,256]{1,0:T(8,128)(2,1)S(1)} %collective-permute-done.9.refs_1_) | copy-start | bytes 786436
  51.9 11.6 %copy-start.12 = (bf16[512,256]{1,0:T(8,128)(2,1)}, bf16[512,256]{1,0:T(8,128)(2,1)S(1)}, u32[]{:S(2)}) copy-start(bf16[512,256]{1,0:T(8,128)(2,1)S(1)} %collective-permute-done.10.refs_2_) | copy-start | bytes 786436
  54.8 8.8 %copy-start.13 = (bf16[512,256]{1,0:T(8,128)(2,1)}, bf16[512,256]{1,0:T(8,128)(2,1)S(1)}, u32[]{:S(2)}) copy-start(bf16[512,256]{1,0:T(8,128)(2,1)S(1)} %collective-permute-done.11.refs_3_) | copy-start | bytes 786436
  54.8 2.5 %collective-permute-start.16 = (f32[128,512]{1,0:T(8,128)}, f32[128,512]{1,0:T(8,128)S(1)}, u32[]{:S(2)}, u32[]{:S(2)}) collective-permute-start(f32[128,512]{1,0:T(8,128)} %get-tuple-element.72), channel_id=1, source_target_pairs={{0,16},{16,0},{1,17},{17,1},{2,18},{18,2},{3,19},{19,3},{4,20},{20... | collective-permute-start | bytes 786440 | tf_op jit(solution)/shard_map/ppermute | solution.py:379
  57.3 1.0 copy-start.3
  58.4 13.0 %collective-permute-start.17 = (bf16[128,512]{1,0:T(8,128)(2,1)S(1)}, bf16[128,512]{1,0:T(8,128)(2,1)S(1)}, u32[]{:S(2)}, u32[]{:S(2)}) collective-permute-start(bf16[128,512]{1,0:T(8,128)(2,1)S(1)} %kv_finish.1), channel_id=1, source_target_pairs={{0,128},{128,0},{1,129},{129,1},{2,130},{130,2},{3,131},{131,3},{4... | collective-permute-start | bytes 393224 | tf_op jit(solution)/shard_map/ppermute | solution.py:379
  63.6 7.7 %copy-start.16 = (s32[16]{0:T(128)S(1)}, s32[16]{0:T(128)}, u32[]{:S(2)}) copy-start(s32[16]{0:T(128)} %param.17) | copy-start | bytes 196
  63.6 9.4 %copy-start.4 = (bf16[1,256]{1,0:T(2,128)(2,1)S(1)}, bf16[1,256]{1,0:T(2,128)(2,1)}, u32[]{:S(2)}) copy-start(bf16[1,256]{1,0:T(2,128)(2,1)} %bias_ref.1) | copy-start | bytes 1540
  63.6 20.4 %copy-start.17 = (s32[16]{0:T(128)S(1)}, s32[16]{0:T(128)}, u32[]{:S(2)}) copy-start(s32[16]{0:T(128)} %param.15) | copy-start | bytes 196
  70.5 2.5 %collective-permute-start.12 = (f32[512,256]{1,0:T(8,128)}, f32[512,256]{1,0:T(8,128)S(1)}, u32[]{:S(2)}, u32[]{:S(2)}) collective-permute-start(f32[512,256]{1,0:T(8,128)} %get-tuple-element.66), channel_id=1, source_target_pairs={{0,16},{16,0},{1,17},{17,1},{2,18},{18,2},{3,19},{19,3},{4,20},{20... | collective-permute-start | bytes 1572872 | tf_op jit(solution)/shard_map/ppermute | solution.py:379
  71.5 12.3 %collective-permute-start.18 = (bf16[2,128,512]{2,1,0:T(8,128)(2,1)S(1)}, bf16[2,128,512]{2,1,0:T(8,128)(2,1)S(1)}, u32[]{:S(2)}, u32[]{:S(2)}) collective-permute-start(bf16[2,128,512]{2,1,0:T(8,128)(2,1)S(1)} %pad_maximum_fusion), channel_id=1, source_target_pairs={{0,1},{1,0},{2,3},{3,2},{4,5},{5,4},{6,7},{7,6},{8,9},{9,8},{10,11... | collective-permute-start | bytes 786440 | tf_op jit(solution)/shard_map/ppermute | solution.py:379
  73.0 1.0 copy-start.2
  74.8 3.5 %collective-permute-start.15 = (bf16[128,256]{1,0:T(8,128)(2,1)S(1)}, bf16[128,256]{1,0:T(8,128)(2,1)S(1)}, u32[]{:S(2)}, u32[]{:S(2)}) collective-permute-start(bf16[128,256]{1,0:T(8,128)(2,1)S(1)} %get-tuple-element.70), channel_id=1, source_target_pairs={{0,3},{1,2},{2,1},{3,0},{4,7},{5,6},{6,5},{7,4},{8,11},{9,10},{10,... | collective-permute-start | bytes 196616 | tf_op jit(solution)/shard_map/ppermute | solution.py:379
  75.2 6.5 %collective-permute-start.14 = (bf16[128,256]{1,0:T(8,128)(2,1)S(1)}, bf16[128,256]{1,0:T(8,128)(2,1)S(1)}, u32[]{:S(2)}, u32[]{:S(2)}) collective-permute-start(bf16[128,256]{1,0:T(8,128)(2,1)S(1)} %get-tuple-element.69), channel_id=1, source_target_pairs={{0,2},{1,3},{2,0},{3,1},{4,6},{5,7},{6,4},{7,5},{8,10},{9,11},{10,... | collective-permute-start | bytes 196616 | tf_op jit(solution)/shard_map/ppermute | solution.py:379
  77.3 6.5 %collective-permute-start.13 = (bf16[128,256]{1,0:T(8,128)(2,1)S(1)}, bf16[128,256]{1,0:T(8,128)(2,1)S(1)}, u32[]{:S(2)}, u32[]{:S(2)}) collective-permute-start(bf16[128,256]{1,0:T(8,128)(2,1)S(1)} %get-tuple-element.68), channel_id=1, source_target_pairs={{0,1},{1,0},{2,3},{3,2},{4,5},{5,4},{6,7},{7,6},{8,9},{9,8},{10,11... | collective-permute-start | bytes 196616 | tf_op jit(solution)/shard_map/ppermute | solution.py:379
  83.9 8.1 %collective-permute-start.19 = (bf16[2,128,512]{2,1,0:T(8,128)(2,1)S(1)}, bf16[2,128,512]{2,1,0:T(8,128)(2,1)S(1)}, u32[]{:S(2)}, u32[]{:S(2)}) collective-permute-start(bf16[2,128,512]{2,1,0:T(8,128)(2,1)S(1)} %pad_maximum_fusion.1.refs_0_), channel_id=1, source_target_pairs={{0,32},{32,0},{64,96},{96,64},{1,33},{33,1},{65,97},{97,65},{2,34}... | collective-permute-start | bytes 786440 | tf_op jit(solution)/shard_map/ppermute | solution.py:379
  84.2 14.7 %collective-permute-start.20 = (bf16[2,128,512]{2,1,0:T(8,128)(2,1)S(1)}, bf16[2,128,512]{2,1,0:T(8,128)(2,1)S(1)}, u32[]{:S(2)}, u32[]{:S(2)}) collective-permute-start(bf16[2,128,512]{2,1,0:T(8,128)(2,1)S(1)} %pad_maximum_fusion.1.refs_0_), channel_id=1, source_target_pairs={{0,64},{32,96},{64,0},{96,32},{1,65},{33,97},{65,1},{97,33},{2,66}... | collective-permute-start | bytes 786440 | tf_op jit(solution)/shard_map/ppermute | solution.py:379
  87.9 13.5 %collective-permute-start.21 = (bf16[2,128,512]{2,1,0:T(8,128)(2,1)S(1)}, bf16[2,128,512]{2,1,0:T(8,128)(2,1)S(1)}, u32[]{:S(2)}, u32[]{:S(2)}) collective-permute-start(bf16[2,128,512]{2,1,0:T(8,128)(2,1)S(1)} %pad_maximum_fusion.1.refs_0_), channel_id=1, source_target_pairs={{0,96},{32,64},{64,32},{96,0},{1,97},{33,65},{65,33},{97,1},{2,98}... | collective-permute-start | bytes 786440 | tf_op jit(solution)/shard_map/ppermute | solution.py:379
  88.1 13.3 %collective-permute-start.22 = (bf16[4,128,256]{2,1,0:T(8,128)(2,1)S(1)}, bf16[4,128,256]{2,1,0:T(8,128)(2,1)S(1)}, u32[]{:S(2)}, u32[]{:S(2)}) collective-permute-start(bf16[4,128,256]{2,1,0:T(8,128)(2,1)S(1)} %pad_maximum_fusion.5.refs_0_), channel_id=1, source_target_pairs={{0,4},{4,0},{8,12},{12,8},{1,5},{5,1},{9,13},{13,9},{2,6},{6,2},{1... | collective-permute-start | bytes 786440 | tf_op jit(solution)/shard_map/ppermute | solution.py:379
  89.4 13.0 %collective-permute-start.23 = (bf16[4,128,256]{2,1,0:T(8,128)(2,1)S(1)}, bf16[4,128,256]{2,1,0:T(8,128)(2,1)S(1)}, u32[]{:S(2)}, u32[]{:S(2)}) collective-permute-start(bf16[4,128,256]{2,1,0:T(8,128)(2,1)S(1)} %pad_maximum_fusion.5.refs_0_), channel_id=1, source_target_pairs={{0,8},{4,12},{8,0},{12,4},{1,9},{5,13},{9,1},{13,5},{2,10},{6,14},... | collective-permute-start | bytes 786440 | tf_op jit(solution)/shard_map/ppermute | solution.py:379
  92.0 13.4 %collective-permute-start.24 = (bf16[4,128,256]{2,1,0:T(8,128)(2,1)S(1)}, bf16[4,128,256]{2,1,0:T(8,128)(2,1)S(1)}, u32[]{:S(2)}, u32[]{:S(2)}) collective-permute-start(bf16[4,128,256]{2,1,0:T(8,128)(2,1)S(1)} %pad_maximum_fusion.5.refs_0_), channel_id=1, source_target_pairs={{0,12},{4,8},{8,4},{12,0},{1,13},{5,9},{9,5},{13,1},{2,14},{6,10},... | collective-permute-start | bytes 786440 | tf_op jit(solution)/shard_map/ppermute | solution.py:379
  106.7 11.3 %collective-permute-start.28 = (bf16[2,128,2048]{2,1,0:T(8,128)(2,1)S(1)}, bf16[2,128,2048]{2,1,0:T(8,128)(2,1)S(1)}, u32[]{:S(2)}, u32[]{:S(2)}) collective-permute-start(bf16[2,128,2048]{2,1,0:T(8,128)(2,1)S(1)} %assemble.1.near_ref), channel_id=1, source_target_pairs={{0,16},{16,0},{1,17},{17,1},{2,18},{18,2},{3,19},{19,3},{4,20},{20... | collective-permute-start | bytes 3145736 | tf_op jit(solution)/shard_map/ppermute | solution.py:379
  109.0 3.7 %collective-permute-start.25 = (bf16[128,256]{1,0:T(8,128)(2,1)S(1)}, bf16[128,256]{1,0:T(8,128)(2,1)S(1)}, u32[]{:S(2)}, u32[]{:S(2)}) collective-permute-start(bf16[128,256]{1,0:T(8,128)(2,1)S(1)} %get-tuple-element.77), channel_id=1, source_target_pairs={{0,1},{1,0},{2,3},{3,2},{4,5},{5,4},{6,7},{7,6},{8,9},{9,8},{10,11... | collective-permute-start | bytes 196616 | tf_op jit(solution)/shard_map/ppermute | solution.py:379
  109.0 4.9 %collective-permute-start.26 = (bf16[128,256]{1,0:T(8,128)(2,1)S(1)}, bf16[128,256]{1,0:T(8,128)(2,1)S(1)}, u32[]{:S(2)}, u32[]{:S(2)}) collective-permute-start(bf16[128,256]{1,0:T(8,128)(2,1)S(1)} %get-tuple-element.78), channel_id=1, source_target_pairs={{0,2},{1,3},{2,0},{3,1},{4,6},{5,7},{6,4},{7,5},{8,10},{9,11},{10,... | collective-permute-start | bytes 196616 | tf_op jit(solution)/shard_map/ppermute | solution.py:379
  110.3 7.7 %collective-permute-start.27 = (bf16[128,256]{1,0:T(8,128)(2,1)S(1)}, bf16[128,256]{1,0:T(8,128)(2,1)S(1)}, u32[]{:S(2)}, u32[]{:S(2)}) collective-permute-start(bf16[128,256]{1,0:T(8,128)(2,1)S(1)} %get-tuple-element.79), channel_id=1, source_target_pairs={{0,3},{1,2},{2,1},{3,0},{4,7},{5,6},{6,5},{7,4},{8,11},{9,10},{10,... | collective-permute-start | bytes 196616 | tf_op jit(solution)/shard_map/ppermute | solution.py:379

commit v2 on v1

--- a/solution.py
+++ b/solution.py
@@ -31,26 +31,49 @@
 THREE_US = pl.CostEstimate(flops=0, bytes_accessed=10 << 20, transcendentals=0)
 
 
-def norm_kernel(order, h_ref, g_ref, near_ref, far_ref):
-    parts, step, width = near_ref.shape
-
-    def square(k, total):
-        piece = h_ref[:, pl.ds(pl.multiple_of(k * width, width), width)].astype(F32)
-        return total + piece * piece
-
-    total = lax.fori_loop(0, 2 * parts, square, jnp.zeros((step, width), F32), unroll=4)
-    mean = jnp.sum(total, axis=1, keepdims=True) * (1.0 / (2 * parts * width))
-    rs = lax.rsqrt(mean + EPSILON)
-    for half, o_ref in ((0, near_ref), (parts, far_ref)):
-
-        def scale(k, carry):
-            off = pl.multiple_of(order[half + k] * width, width)
-            piece = h_ref[:, pl.ds(off, width)].astype(F32)
-            gain = g_ref[:, pl.ds(off, width)].astype(F32)
-            o_ref[k] = (piece * rs * gain).astype(BF)
-            return carry
-
-        lax.fori_loop(0, parts, scale, 0, unroll=4)
+def norm_kernel(order, h_hbm, g_ref, near_hbm, far_hbm, hbuf, near, far, in_sem, out_sem):
+    parts, rows, width = near.shape
+    count, step, _ = hbuf.shape
+
+    def load(i):
+        return pltpu.make_async_copy(h_hbm.at[pl.ds(i * step, step)], hbuf.at[i], in_sem.at[i])
+
+    def store(i, t):
+        here, there = ((near, near_hbm), (far, far_hbm))[t]
+        rows_i = pl.ds(pl.multiple_of(i * step, step), step)
+        return pltpu.make_async_copy(here.at[:, rows_i], there.at[:, rows_i], out_sem.at[t, i])
+
+    for i in range(count):
+        load(i).start()
+
+    def block(i, carry):
+        pltpu.make_async_copy(h_hbm.at[pl.ds(0, step)], hbuf.at[i], in_sem.at[i]).wait()
+
+        def square(k, total):
+            piece = hbuf[i, :, pl.ds(pl.multiple_of(k * width, width), width)].astype(F32)
+            return total + piece * piece
+
+        total = lax.fori_loop(0, 2 * parts, square, jnp.zeros((step, width), F32), unroll=4)
+        mean = jnp.sum(total, axis=1, keepdims=True) * (1.0 / (2 * parts * width))
+        rs = lax.rsqrt(mean + EPSILON)
+        rows_i = pl.ds(pl.multiple_of(i * step, step), step)
+        for t, half, o_ref in ((0, 0, near), (1, parts, far)):
+
+            def scale(k, inner):
+                off = pl.multiple_of(order[half + k] * width, width)
+                piece = hbuf[i, :, pl.ds(off, width)].astype(F32)
+                gain = g_ref[:, pl.ds(off, width)].astype(F32)
+                o_ref[k, rows_i, :] = (piece * rs * gain).astype(BF)
+                return inner
+
+            lax.fori_loop(0, parts, scale, 0, unroll=4)
+            store(i, t).start()
+        return carry
+
+    lax.fori_loop(0, count, block, 0)
+    for i in range(count):
+        for t in range(2):
+            store(i, t).wait()
 
 
 def norm(hidden, gain, order):
@@ -58,55 +81,70 @@
     parts = 8
     width = d // parts // 2
     step = 64
-    block = pl.BlockSpec((parts, step, width), lambda i, o: (0, i, 0))
+    count = rows // step
+    shape = jax.ShapeDtypeStruct((parts, rows, width), BF)
     return pl.pallas_call(
         norm_kernel,
         grid_spec=pltpu.PrefetchScalarGridSpec(
             num_scalar_prefetch=1,
-            grid=(rows // step,),
-            in_specs=[
-                pl.BlockSpec((step, d), lambda i, o: (i, 0)),
-                pl.BlockSpec((1, d), lambda i, o: (0, 0)),
+            grid=(1,),
+            in_specs=[HBM, full((1, d))],
+            out_specs=[HBM, HBM],
+            scratch_shapes=[
+                pltpu.VMEM((count, step, d), BF),
+                pltpu.VMEM(shape.shape, BF),
+                pltpu.VMEM(shape.shape, BF),
+                pltpu.SemaphoreType.DMA((count,)),
+                pltpu.SemaphoreType.DMA((2, count)),
             ],
-            out_specs=[block, block],
         ),
-        out_shape=[jax.ShapeDtypeStruct((parts, rows, width), BF)] * 2,
-        compiler_params=pltpu.CompilerParams(vmem_limit_bytes=VMEM_LIMIT),
+        out_shape=[shape] * 2,
+        compiler_params=pltpu.CompilerParams(vmem_limit_bytes=VMEM_MOST),
         cost_estimate=SIX_US,
         name="norm",
     )(order, hidden, gain.reshape(1, d))
 
 
-def fetch(n_refs, ks, nbuf, nsem, w_refs, wbuf, wsem):
-    per = len(ks) // len(w_refs)
-    for i, w_ref in enumerate(w_refs):
-        pltpu.make_async_copy(w_ref, wbuf.at[i], wsem.at[i]).start()
-        for j in range(i * per, (i + 1) * per):
-            for t, n_ref in enumerate(n_refs):
-                pltpu.make_async_copy(n_ref.at[ks[j]], nbuf.at[t, j], nsem.at[t, j]).start()
+def tokens(n_refs, k, nbuf, nsem, j):
+    rows = nbuf.shape[1] // 2
+    return [
+        pltpu.make_async_copy(n_ref.at[k], nbuf.at[j, pl.ds(t * rows, rows)], nsem.at[t, j])
+        for t, n_ref in enumerate(n_refs)
+    ]
 
 
 def kv_kernel(near_ref, far_ref, *refs):
     w_refs = refs[:4]
     own_ref, other_ref, nbuf, wbuf, acc, nsem, wsem = refs[4:]
-    fetch((near_ref, far_ref), (0, 4, 1, 5, 2, 6, 3, 7), nbuf, nsem, w_refs, wbuf, wsem)
+    load = lambda i, r: tokens((near_ref, far_ref), i + 4 * r, nbuf, nsem, 2 * i + r)
+    for i, w_ref in enumerate(w_refs):
+        pltpu.make_async_copy(w_ref, wbuf.at[i], wsem.at[i]).start()
+        if i == 0:
+            for r in range(2):
+                for copy in load(0, r):
+                    copy.start()
     acc[...] = jnp.zeros_like(acc)
 
     def step(i, carry):
+        @pl.when(i < 3)
+        def _():
+            for r in range(2):
+                for copy in load(i + 1, r):
+                    copy.start()
+
         pltpu.make_async_copy(w_refs[0], wbuf.at[i], wsem.at[i]).wait()
-        for t in range(2):
-            out = None
-            for r in range(2):
-                k = 2 * i + r
-                pltpu.make_async_copy(near_ref.at[0], nbuf.at[t, k], nsem.at[t, k]).wait()
-                part = jnp.dot(nbuf[t, k], wbuf[i, r], preferred_element_type=F32)
-                out = part if out is None else out + part
-            acc[t] += out
+        out = None
+        for r in range(2):
+            for copy in load(i, r):
+                copy.wait()
+            part = jnp.dot(nbuf[2 * i + r], wbuf[i, r], preferred_element_type=F32)
+            out = part if out is None else out + part
+        acc[...] += out
         return carry
 
     lax.fori_loop(0, 4, step, 0)
-    for t, o_ref in ((0, own_ref), (1, other_ref)):
-        o_ref[...] = acc[t].T
+    own_ref[...] = acc[:512].T
+    other_ref[...] = acc[512:].T
 
 
 def kv_project(near, far, pieces):
@@ -117,9 +155,9 @@
         out_specs=[full((128, rows))] * 2,
         out_shape=[jax.ShapeDtypeStruct((128, rows), F32)] * 2,
         scratch_shapes=[
-            pltpu.VMEM((2, parts, rows, width), BF),
+            pltpu.VMEM((parts, 2 * rows, width), BF),
             pltpu.VMEM((4, 2, 512, 128), BF),
-            pltpu.VMEM((2, rows, 128), F32),
+            pltpu.VMEM((2 * rows, 128), F32),
             pltpu.SemaphoreType.DMA((2, 8)),
             pltpu.SemaphoreType.DMA((4,)),
         ],
@@ -152,27 +190,41 @@
 
 def q_kernel(first, near_ref, far_ref, *refs):
     w_refs, refs = refs[:4], refs[4:]
-    if first:
-        so_far, refs = refs[:2], refs[2:]
-    own_ref, other_ref, nbuf, wbuf, nsem, wsem = refs
-    fetch((near_ref, far_ref), range(first, first + 4), nbuf, nsem, w_refs, wbuf, wsem)
+    so_far, refs = refs[:-9], refs[-9:]
+    own_ref, other_ref, nbuf, wbuf, acc, nsem, wsem, before, bsem = refs
+    rows = own_ref.shape[0]
+    load = lambda k: tokens((near_ref, far_ref), first + k, nbuf, nsem, k)
+    for k, w_ref in enumerate(w_refs):
+        pltpu.make_async_copy(w_ref, wbuf.at[k], wsem.at[k]).start()
+        if k < 2:
+            for copy in load(k):
+                copy.start()
+
+    earlier = [pltpu.make_async_copy(ref, before.at[t], bsem.at[t]) for t, ref in enumerate(so_far)]
+    for copy in earlier:
+        copy.start()
+
+    def part(i):
+        out = None
+        for r in range(2):
+            k = 2 * i + r
+            if k < 2:
+                for copy in load(k + 2):
+                    copy.start()
+            pltpu.make_async_copy(w_refs[0], wbuf.at[k], wsem.at[k]).wait()
+            for copy in load(k):
+                copy.wait()
+            one = jnp.dot(nbuf[k], wbuf[k], preferred_element_type=F32)
+            out = one if out is None else out + one
+        return out
+
+    acc[...] = part(0)
+    total = acc[...] + part(1)
+    for copy in earlier:
+        copy.wait()
     for t, o_ref in ((0, own_ref), (1, other_ref)):
-        o_ref[...] = so_far[t][...] if first else jnp.zeros_like(o_ref)
-
-    def step(i, carry):
-        for r in range(2):
-            pltpu.make_async_copy(w_refs[0], wbuf.at[2 * i + r], wsem.at[2 * i + r]).wait()
-        for t, o_ref in ((0, own_ref), (1, other_ref)):
-            out = None
-            for r in range(2):
-                k = 2 * i + r
-                pltpu.make_async_copy(near_ref.at[0], nbuf.at[t, k], nsem.at[t, k]).wait()
-                part = jnp.dot(nbuf[t, k], wbuf[k], preferred_element_type=F32)
-                out = part if out is None else out + part
-            o_ref[...] += out
-        return carry
-
-    lax.fori_loop(0, 2, step, 0)
+        half = total[t * rows : (t + 1) * rows]
+        o_ref[...] = half + before[t] if so_far else half
 
 
 def q_project(first, near, far, pieces, so_far):
@@ -180,14 +232,17 @@
     shape = jax.ShapeDtypeStruct((rows, 256), F32)
     return pl.pallas_call(
         functools.partial(q_kernel, first),
-        in_specs=[HBM] * 6 + [full(shape.shape)] * len(so_far),
+        in_specs=[HBM] * (6 + len(so_far)),
         out_specs=[full(shape.shape)] * 2,
         out_shape=[shape] * 2,
         scratch_shapes=[
-            pltpu.VMEM((2, 4, rows, width), BF),
+            pltpu.VMEM((4, 2 * rows, width), BF),
             pltpu.VMEM((4, 512, 256), BF),
+            pltpu.VMEM((2 * rows, 256), F32),
             pltpu.SemaphoreType.DMA((2, 4)),
             pltpu.SemaphoreType.DMA((4,)),
+            pltpu.VMEM((2, rows, 256), F32),
+            pltpu.SemaphoreType.DMA((2,)),
         ],
         compiler_params=pltpu.CompilerParams(vmem_limit_bytes=VMEM_MOST),
         cost_estimate=THREE_US,
@@ -424,7 +479,9 @@
     z0 = after(z0, p_near[1])
     z_near = [z0] + [flip(z0, X, d) for d in (1, 2, 3)]
 
-    counts = jnp.sum((block_lists >= 0).astype(jnp.int32), axis=1)
+    q_half = list(q_project(0, near, far, s_near, []))
+    kv_own, kv_other = kv_project(after(near, q_half[0]), far, p_near)
+    counts = jnp.sum((after(block_lists, kv_own) >= 0).astype(jnp.int32), axis=1)
     token = jnp.arange(rows, dtype=jnp.int32)
     positions = (jnp.where(token < BLK, counts[0], counts[1]) - 1) * BLK + token % BLK
     freqs = THETA ** (-2.0 * jnp.arange(64, dtype=F32) / 128)
@@ -435,9 +492,9 @@
     cos_t = jnp.where(value_side == 0, cosine.T, 1.0)
     sin_t = jnp.where(value_side == 0, sine.T, 0.0)
 
-    q_half = list(q_project(0, near, far, s_near, []))
-    kv_own, kv_other = kv_project(after(near, q_half[0]), far, p_near)
-    kv_other, q_half[0], *z_near = lax.optimization_barrier((kv_other, q_half[0], *z_near))
+    kv_other, q_half[0], cos_t, sin_t, cos2, sin2, *z_near = lax.optimization_barrier(
+        (kv_other, q_half[0], cos_t, sin_t, cos2, sin2, *z_near)
+    )
     piece = kv_finish(kv_own, flip(kv_other, CORE, 1), own_bias, cos_t, sin_t)
     over = flip(piece, ZH, 1)
     start = jnp.where(zh == 0, piece, over)

time: 130 us -> 127 us (0.977)
  Pallas kernels: 43.3 us -> 39.7 us
  waiting for transfers between devices: 31.2 us -> 32.8 us
  local copies, waits for them, and re-layouts: 5.83 us -> 4.46 us
    pallas_call x2, Pallas kernels: 12.6 us -> 10.6 us  [q_project(): pl.pallas_call(functools.partial(q_kernel, first), in_specs=[HBM] * (6 +...]
    unnamed x36 -> x32, local copies, waits for them, and re-layouts: 4.03 us -> 2.06 us
    ppermute x29, waiting for transfers between devices: 31.2 us -> 32.8 us  [flip(): return lax.ppermute(v, axis, [(i, i ^ bits) for i in range(n)])]
  transfers between devices with their start and end apart: 29 -> 29, of which waited for: 15 -> 14; matrix products, arithmetic and copies ran while one was open for 5% -> 6% of each run, Pallas kernels for 23% -> 21%
where the time goes in v2:
time: 127 us; the launch traced here: 126 us
  starting transfers between devices  44 us (35%)
  Pallas kernels  39.7 us (31%)
  waiting for transfers between devices  32.8 us (26%)
  other arithmetic  5 us (4%)
  local copies, waits for them, and re-layouts  4.46 us (4%)
    ppermute x29, starting transfers between devices, flip(): return lax.ppermute(v, axis, [(i, i ^ bits) for i in range(n)])  44 us
    ppermute x29, waiting for transfers between devices, flip(): return lax.ppermute(v, axis, [(i, i ^ bits) for i in range(n)])  32.8 us
    pallas_call x1, Pallas kernels, attention(): pl.pallas_call(attention_kernel, grid_spec=pltpu.PrefetchScalarGridSpec(n...  11.4 us
    pallas_call x2, Pallas kernels, q_project(): pl.pallas_call(functools.partial(q_kernel, first), in_specs=[HBM] * (6 +...  10.6 us
    pallas_call x1, Pallas kernels, norm(): pl.pallas_call(norm_kernel, grid_spec=pltpu.PrefetchScalarGridSpec(num_sc...  8.77 us
    pallas_call x1, Pallas kernels, kv_project(): pl.pallas_call(kv_kernel, in_specs=[HBM] * 6, out_specs=[full((128, rows)...  6.76 us
  transfers between devices with their start and end apart: 29, of which 14 were waited for; matrix products, arithmetic and copies ran while one was open for 6% of the time, Pallas kernels for 21%

profile of v2, /device:TPU:39, one launch (start us, length us, event | category | flops | bytes accessed | tf_op | source)
XLA Modules:
  0.0 126.5 jit_solution(13663229797166653513)
XLA Ops:
  0.0 6.0 %collective-permute-start = (bf16[512,256]{1,0:T(8,128)(2,1)}, bf16[512,256]{1,0:T(8,128)(2,1)S(1)}, u32[]{:S(2)}, u32[]{:S(2)}) collective-permute-start(bf16[512,256]{1,0:T(8,128)(2,1)} %bitcast.21), channel_id=1, source_target_pairs={{0,128},{128,0},{1,129},{129,1},{2,130},{130,2},{3,131},{131,3},{4... | collective-permute-start | bytes 786440 | tf_op jit(solution)/shard_map/ppermute | solution.py:434
  6.6 0.8 collective-permute-start.3
  7.4 2.5 %collective-permute-start.4 = (bf16[512,256]{1,0:T(8,128)(2,1)}, bf16[512,256]{1,0:T(8,128)(2,1)S(1)}, u32[]{:S(2)}, u32[]{:S(2)}) collective-permute-start(bf16[512,256]{1,0:T(8,128)(2,1)} %bitcast.24), channel_id=1, source_target_pairs={{0,96},{32,64},{64,32},{96,0},{1,97},{33,65},{65,33},{97,1},{2,98}... | collective-permute-start | bytes 786440 | tf_op jit(solution)/shard_map/ppermute | solution.py:434
  10.7 1.3 %reshape.47.g_ref = bf16[1,8192]{1,0:T(2,128)(2,1)} reshape(bf16[8192]{0:T(1024)(128)(2,1)} %param.10) | data formatting | bytes 32768 | tf_op jit(solution)/shard_map/reshape | solution.py:105
  12.1 8.8 %norm.1 = (bf16[8,512,512]{2,1,0:T(8,128)(2,1)}, bf16[8,512,512]{2,1,0:T(8,128)(2,1)}) custom-call(s32[16]{0:T(128)} %xor_add_fusion.order, bf16[512,8192]{1,0:T(8,128)(2,1)} %h_hbm.1, bf16[1,8192]{1,0:T(2,128)(2,1)} %reshape.47.g_ref), custom_call_target="tpu_custom_call" | custom-call | bytes 20971520 | tf_op jit(solution)/shard_map/norm/pallas_call | solution.py:86
  21.0 2.5 %collective-permute-done.1 = bf16[512,128]{1,0:T(8,128)(2,1)S(1)} collective-permute-done((bf16[512,128]{1,0:T(8,128)(2,1)S(1)}, bf16[512,128]{1,0:T(8,128)(2,1)S(1)}, u32[]{:S(2)}, u32[]{:S(2)}) %collective-permute-start.1) | collective-permute-done | bytes 131104 | tf_op jit(solution)/shard_map/ppermute | solution.py:434
  23.6 1.4 %collective-permute-start.5 = (bf16[8,512,512]{2,1,0:T(8,128)(2,1)}, bf16[8,512,512]{2,1,0:T(8,128)(2,1)}, u32[]{:S(2)}, u32[]{:S(2)}) collective-permute-start(bf16[8,512,512]{2,1,0:T(8,128)(2,1)} %get-tuple-element.53), channel_id=1, source_target_pairs={{0,16},{16,0},{1,17},{17,1},{2,18},{18,2},{3,19},{19,3},{4,20},{20... | collective-permute-start | bytes 12582920 | tf_op jit(solution)/shard_map/ppermute | solution.py:434
  25.0 0.6 collective-permute-start.6
  25.6 1.2 collective-permute-start.7
  26.8 2.1 %collective-permute-start.8 = (bf16[2,512,128]{2,1,0:T(8,128)(2,1)S(1)}, bf16[2,512,128]{2,1,0:T(8,128)(2,1)}, u32[]{:S(2)}, u32[]{:S(2)}) collective-permute-start(bf16[2,512,128]{2,1,0:T(8,128)(2,1)S(1)} %pad_maximum_fusion.2.refs_0_), channel_id=1, source_target_pairs={{0,96},{32,64},{64,32},{96,0},{1,97},{33,65},{65,33},{97,1},{2,98}... | collective-permute-start | bytes 786440 | tf_op jit(solution)/shard_map/ppermute | solution.py:434
  28.9 4.1 %collective-permute-done.6.refs_1_ = bf16[2,512,128]{2,1,0:T(8,128)(2,1)S(1)} collective-permute-done((bf16[2,512,128]{2,1,0:T(8,128)(2,1)S(1)}, bf16[2,512,128]{2,1,0:T(8,128)(2,1)S(1)}, u32[]{:S(2)}, u32[]{:S(2)}) %collective-permute-start.6) | collective-permute-done | bytes 262176 | tf_op jit(solution)/shard_map/ppermute | solution.py:434
  33.5 1.2 collective-permute-start.10
  34.8 2.1 %collective-permute-start.11 = (bf16[512,256]{1,0:T(8,128)(2,1)S(1)}, bf16[512,256]{1,0:T(8,128)(2,1)S(1)}, u32[]{:S(2)}, u32[]{:S(2)}) collective-permute-start(bf16[512,256]{1,0:T(8,128)(2,1)S(1)} %collective-permute-done.refs_0_), channel_id=1, source_target_pairs={{0,96},{32,64},{64,32},{96,0},{1,97},{33,65},{65,33},{97,1},{2,98}... | collective-permute-start | bytes 786440 | tf_op jit(solution)/shard_map/ppermute | solution.py:434
  36.9 5.2 %q_project.2 = (f32[512,256]{1,0:T(8,128)}, f32[512,256]{1,0:T(8,128)}) custom-call(bf16[8,512,512]{2,1,0:T(8,128)(2,1)} %get-tuple-element.59.near_ref, bf16[8,512,512]{2,1,0:T(8,128)(2,1)} %collective-permute-done.5.far_ref, bf16[512,256]{1,0:T(8,128)(2,1)} %bitcast.25, bf16[512,256]{1,0:T(8,128)(2,1)} %copy-done.6, bf16[512,256]{1,0:T(8,128)(2,1)} %copy-done.7, ...), custom_call_target="tpu_custom_call" | custom-call | bytes 10485760 | tf_op jit(solution)/shard_map/q_project/pallas_call | solution.py:233
  42.1 6.8 %kv_project.1 = (f32[128,512]{1,0:T(8,128)}, f32[128,512]{1,0:T(8,128)}) custom-call(bf16[8,512,512]{2,1,0:T(8,128)(2,1)} %get-tuple-element.59.near_ref, bf16[8,512,512]{2,1,0:T(8,128)(2,1)} %collective-permute-done.5.far_ref, bf16[2,512,128]{2,1,0:T(8,128)(2,1)} %copy-done.4, bf16[2,512,128]{2,1,0:T(8,128)(2,1)} %copy-done.12, ...), custom_call_target="tpu_custom_call" | custom-call | bytes 20971520 | tf_op jit(solution)/shard_map/kv_project/pallas_call | solution.py:152
  49.0 0.6 fusion.14
  49.6 1.3 fusion.4
  50.9 1.0 fusion.2
  52.7 2.3 %collective-permute-start.16 = (f32[128,512]{1,0:T(8,128)}, f32[128,512]{1,0:T(8,128)S(1)}, u32[]{:S(2)}, u32[]{:S(2)}) collective-permute-start(f32[128,512]{1,0:T(8,128)} %get-tuple-element.80), channel_id=1, source_target_pairs={{0,16},{16,0},{1,17},{17,1},{2,18},{18,2},{3,19},{19,3},{4,20},{20... | collective-permute-start | bytes 786440 | tf_op jit(solution)/shard_map/ppermute | solution.py:434
  55.1 0.8 bitcast_convert_fusion
  55.8 0.6 collective-permute-done.16.two_ref
  56.5 1.0 copy-done.2
  57.6 5.4 %collective-permute-start.17 = (bf16[128,512]{1,0:T(8,128)(2,1)S(1)}, bf16[128,512]{1,0:T(8,128)(2,1)S(1)}, u32[]{:S(2)}, u32[]{:S(2)}) collective-permute-start(bf16[128,512]{1,0:T(8,128)(2,1)S(1)} %kv_finish.1), channel_id=1, source_target_pairs={{0,128},{128,0},{1,129},{129,1},{2,130},{130,2},{3,131},{131,3},{4... | collective-permute-start | bytes 393224 | tf_op jit(solution)/shard_map/ppermute | solution.py:434
  63.0 5.4 %q_project.3 = (f32[512,256]{1,0:T(8,128)}, f32[512,256]{1,0:T(8,128)}) custom-call(bf16[8,512,512]{2,1,0:T(8,128)(2,1)} %get-tuple-element.59.near_ref, bf16[8,512,512]{2,1,0:T(8,128)(2,1)} %collective-permute-done.5.far_ref, bf16[512,256]{1,0:T(8,128)(2,1)} %copy-done.5, bf16[512,256]{1,0:T(8,128)(2,1)} %copy-done.9, bf16[512,256]{1,0:T(8,128)(2,1)} %copy-done.10, ...), custom_call_target="tpu_custom_call" | custom-call | bytes 10485760 | tf_op jit(solution)/shard_map/q_project/pallas_call | solution.py:233
  68.4 0.7 collective-permute-start.12
  69.6 1.3 %collective-permute-done.12.two_ref = f32[512,256]{1,0:T(8,128)S(1)} collective-permute-done((f32[512,256]{1,0:T(8,128)}, f32[512,256]{1,0:T(8,128)S(1)}, u32[]{:S(2)}, u32[]{:S(2)}) %collective-permute-start.12) | collective-permute-done | bytes 524320 | tf_op jit(solution)/shard_map/ppermute | solution.py:434
  70.9 1.0 copy-done.1
  71.9 0.8 q_finish.1
  72.8 2.2 %collective-permute-start.14 = (bf16[128,256]{1,0:T(8,128)(2,1)S(1)}, bf16[128,256]{1,0:T(8,128)(2,1)S(1)}, u32[]{:S(2)}, u32[]{:S(2)}) collective-permute-start(bf16[128,256]{1,0:T(8,128)(2,1)S(1)} %get-tuple-element.78), channel_id=1, source_target_pairs={{0,2},{1,3},{2,0},{3,1},{4,6},{5,7},{6,4},{7,5},{8,10},{9,11},{10,... | collective-permute-start | bytes 196616 | tf_op jit(solution)/shard_map/ppermute | solution.py:434
  75.5 0.8 collective-permute-done.15
  76.2 2.7 %collective-permute-done.14 = bf16[128,256]{1,0:T(8,128)(2,1)S(1)} collective-permute-done((bf16[128,256]{1,0:T(8,128)(2,1)S(1)}, bf16[128,256]{1,0:T(8,128)(2,1)S(1)}, u32[]{:S(2)}, u32[]{:S(2)}) %collective-permute-start.14) | collective-permute-done | bytes 65568 | tf_op jit(solution)/shard_map/ppermute | solution.py:434
  78.9 1.6 %collective-permute-done.13 = bf16[128,256]{1,0:T(8,128)(2,1)S(1)} collective-permute-done((bf16[128,256]{1,0:T(8,128)(2,1)S(1)}, bf16[128,256]{1,0:T(8,128)(2,1)S(1)}, u32[]{:S(2)}, u32[]{:S(2)}) %collective-permute-start.13) | collective-permute-done | bytes 65568 | tf_op jit(solution)/shard_map/ppermute | solution.py:434
  81.0 2.7 %collective-permute-start.20 = (bf16[2,128,512]{2,1,0:T(8,128)(2,1)S(1)}, bf16[2,128,512]{2,1,0:T(8,128)(2,1)S(1)}, u32[]{:S(2)}, u32[]{:S(2)}) collective-permute-start(bf16[2,128,512]{2,1,0:T(8,128)(2,1)S(1)} %pad_maximum_fusion.1.refs_0_), channel_id=1, source_target_pairs={{0,64},{32,96},{64,0},{96,32},{1,65},{33,97},{65,1},{97,33},{2,66}... | collective-permute-start | bytes 786440 | tf_op jit(solution)/shard_map/ppermute | solution.py:434
  83.7 1.2 collective-permute-start.21
  84.9 1.3 %collective-permute-start.22 = (bf16[4,128,256]{2,1,0:T(8,128)(2,1)S(1)}, bf16[4,128,256]{2,1,0:T(8,128)(2,1)S(1)}, u32[]{:S(2)}, u32[]{:S(2)}) collective-permute-start(bf16[4,128,256]{2,1,0:T(8,128)(2,1)S(1)} %pad_maximum_fusion.5.refs_0_), channel_id=1, source_target_pairs={{0,4},{4,0},{8,12},{12,8},{1,5},{5,1},{9,13},{13,9},{2,6},{6,2},{1... | collective-permute-start | bytes 786440 | tf_op jit(solution)/shard_map/ppermute | solution.py:434
  86.2 2.6 %collective-permute-start.23 = (bf16[4,128,256]{2,1,0:T(8,128)(2,1)S(1)}, bf16[4,128,256]{2,1,0:T(8,128)(2,1)S(1)}, u32[]{:S(2)}, u32[]{:S(2)}) collective-permute-start(bf16[4,128,256]{2,1,0:T(8,128)(2,1)S(1)} %pad_maximum_fusion.5.refs_0_), channel_id=1, source_target_pairs={{0,8},{4,12},{8,0},{12,4},{1,9},{5,13},{9,1},{13,5},{2,10},{6,14},... | collective-permute-start | bytes 786440 | tf_op jit(solution)/shard_map/ppermute | solution.py:434
  89.5 4.0 %collective-permute-done.20.refs_2_ = bf16[2,128,512]{2,1,0:T(8,128)(2,1)S(1)} collective-permute-done((bf16[2,128,512]{2,1,0:T(8,128)(2,1)S(1)}, bf16[2,128,512]{2,1,0:T(8,128)(2,1)S(1)}, u32[]{:S(2)}, u32[]{:S(2)}) %collective-permute-start.20) | collective-permute-done | bytes 262176 | tf_op jit(solution)/shard_map/ppermute | solution.py:434
  93.4 3.8 %collective-permute-done.21.refs_3_ = bf16[2,128,512]{2,1,0:T(8,128)(2,1)S(1)} collective-permute-done((bf16[2,128,512]{2,1,0:T(8,128)(2,1)S(1)}, bf16[2,128,512]{2,1,0:T(8,128)(2,1)S(1)}, u32[]{:S(2)}, u32[]{:S(2)}) %collective-permute-start.21) | collective-permute-done | bytes 262176 | tf_op jit(solution)/shard_map/ppermute | solution.py:434
  97.7 4.5 %collective-permute-done.24.refs_3_ = bf16[4,128,256]{2,1,0:T(8,128)(2,1)S(1)} collective-permute-done((bf16[4,128,256]{2,1,0:T(8,128)(2,1)S(1)}, bf16[4,128,256]{2,1,0:T(8,128)(2,1)S(1)}, u32[]{:S(2)}, u32[]{:S(2)}) %collective-permute-start.24) | collective-permute-done | bytes 262176 | tf_op jit(solution)/shard_map/ppermute | solution.py:434
  102.2 0.7 choose.1
  102.9 0.6 assemble.1.near_ref
  103.5 2.3 %collective-permute-start.28 = (bf16[2,128,2048]{2,1,0:T(8,128)(2,1)S(1)}, bf16[2,128,2048]{2,1,0:T(8,128)(2,1)S(1)}, u32[]{:S(2)}, u32[]{:S(2)}) collective-permute-start(bf16[2,128,2048]{2,1,0:T(8,128)(2,1)S(1)} %assemble.1.near_ref), channel_id=1, source_target_pairs={{0,16},{16,0},{1,17},{17,1},{2,18},{18,2},{3,19},{19,3},{4,20},{20... | collective-permute-start | bytes 3145736 | tf_op jit(solution)/shard_map/ppermute | solution.py:434
  105.8 0.7 collective-permute-start.25
  106.9 1.5 %collective-permute-start.27 = (bf16[128,256]{1,0:T(8,128)(2,1)S(1)}, bf16[128,256]{1,0:T(8,128)(2,1)S(1)}, u32[]{:S(2)}, u32[]{:S(2)}) collective-permute-start(bf16[128,256]{1,0:T(8,128)(2,1)S(1)} %get-tuple-element.89), channel_id=1, source_target_pairs={{0,3},{1,2},{2,1},{3,0},{4,7},{5,6},{6,5},{7,4},{8,11},{9,10},{10,... | collective-permute-start | bytes 196616 | tf_op jit(solution)/shard_map/ppermute | solution.py:434
  108.5 1.0 collective-permute-done.25.q1
  109.4 1.1 collective-permute-done.26.q2
  110.5 4.3 %collective-permute-done.27.q3 = bf16[128,256]{1,0:T(8,128)(2,1)S(1)} collective-permute-done((bf16[128,256]{1,0:T(8,128)(2,1)S(1)}, bf16[128,256]{1,0:T(8,128)(2,1)S(1)}, u32[]{:S(2)}, u32[]{:S(2)}) %collective-permute-start.27) | collective-permute-done | bytes 65568 | tf_op jit(solution)/shard_map/ppermute | solution.py:434
  114.9 11.4 %attention.1 = bf16[512,256]{1,0:T(8,128)(2,1)} custom-call(s32[16]{0:T(128)S(1)} %concatenate.9.tab, bf16[128,256]{1,0:T(8,128)(2,1)S(1)} %get-tuple-element.86.q0, bf16[128,256]{1,0:T(8,128)(2,1)S(1)} %collective-permute-done.25.q1, bf16[128,256]{1,0:T(8,128)(2,1)S(1)} %collective-permute-done.26.q2, bf16[128,256]{1,0:T(8,128)(2,1)S(1)} %collective-permute-done.27.q3, ...), custom_call_target="tpu_custom_call" | custom-call | tf_op jit(solution)/shard_map/attention/pallas_call | solution.py:407
  (81 shorter events, 6.3 us)
Async XLA Ops:
  0.0 9.9 %copy-start = (bf16[4,512,256]{2,1,0:T(8,128)(2,1)S(1)}, bf16[4,512,256]{2,1,0:T(8,128)(2,1)}, u32[]{:S(2)}) copy-start(bf16[4,512,256]{2,1,0:T(8,128)(2,1)} %param.13) | copy-start | bytes 3145732
  0.0 23.5 %collective-permute-start = (bf16[512,256]{1,0:T(8,128)(2,1)}, bf16[512,256]{1,0:T(8,128)(2,1)S(1)}, u32[]{:S(2)}, u32[]{:S(2)}) collective-permute-start(bf16[512,256]{1,0:T(8,128)(2,1)} %bitcast.21), channel_id=1, source_target_pairs={{0,128},{128,0},{1,129},{129,1},{2,130},{130,2},{3,131},{131,3},{4... | collective-permute-start | bytes 786440 | tf_op jit(solution)/shard_map/ppermute | solution.py:434
  6.0 17.5 %collective-permute-start.2 = (bf16[512,256]{1,0:T(8,128)(2,1)}, bf16[512,256]{1,0:T(8,128)(2,1)S(1)}, u32[]{:S(2)}, u32[]{:S(2)}) collective-permute-start(bf16[512,256]{1,0:T(8,128)(2,1)} %bitcast.22), channel_id=1, source_target_pairs={{0,32},{32,0},{64,96},{96,64},{1,33},{33,1},{65,97},{97,65},{2,34}... | collective-permute-start | bytes 786440 | tf_op jit(solution)/shard_map/ppermute | solution.py:434
  6.6 17.0 %collective-permute-start.3 = (bf16[512,256]{1,0:T(8,128)(2,1)}, bf16[512,256]{1,0:T(8,128)(2,1)S(1)}, u32[]{:S(2)}, u32[]{:S(2)}) collective-permute-start(bf16[512,256]{1,0:T(8,128)(2,1)} %bitcast.23), channel_id=1, source_target_pairs={{0,64},{32,96},{64,0},{96,32},{1,65},{33,97},{65,1},{97,33},{2,66}... | collective-permute-start | bytes 786440 | tf_op jit(solution)/shard_map/ppermute | solution.py:434
  7.4 16.2 %collective-permute-start.4 = (bf16[512,256]{1,0:T(8,128)(2,1)}, bf16[512,256]{1,0:T(8,128)(2,1)S(1)}, u32[]{:S(2)}, u32[]{:S(2)}) collective-permute-start(bf16[512,256]{1,0:T(8,128)(2,1)} %bitcast.24), channel_id=1, source_target_pairs={{0,96},{32,64},{64,32},{96,0},{1,97},{33,65},{65,33},{97,1},{2,98}... | collective-permute-start | bytes 786440 | tf_op jit(solution)/shard_map/ppermute | solution.py:434
  10.0 13.5 %collective-permute-start.1 = (bf16[512,128]{1,0:T(8,128)(2,1)S(1)}, bf16[512,128]{1,0:T(8,128)(2,1)S(1)}, u32[]{:S(2)}, u32[]{:S(2)}) collective-permute-start(bf16[512,128]{1,0:T(8,128)(2,1)S(1)} %fusion.15), channel_id=1, source_target_pairs={{0,128},{128,0},{1,129},{129,1},{2,130},{130,2},{3,131},{131,3},{4... | collective-permute-start | bytes 393224 | tf_op jit(solution)/shard_map/ppermute | solution.py:434
  23.5 18.5 %copy-start.4 = (bf16[2,512,128]{2,1,0:T(8,128)(2,1)}, bf16[2,512,128]{2,1,0:T(8,128)(2,1)S(1)}, u32[]{:S(2)}) copy-start(bf16[2,512,128]{2,1,0:T(8,128)(2,1)S(1)} %pad_maximum_fusion.2.refs_0_) | copy-start | bytes 786436
  23.5 18.5 %copy-start.5 = (bf16[512,256]{1,0:T(8,128)(2,1)}, bf16[512,256]{1,0:T(8,128)(2,1)S(1)}, u32[]{:S(2)}) copy-start(bf16[512,256]{1,0:T(8,128)(2,1)S(1)} %collective-permute-done.refs_0_) | copy-start | bytes 786436
  23.5 13.3 %copy-start.6 = (bf16[512,256]{1,0:T(8,128)(2,1)}, bf16[512,256]{1,0:T(8,128)(2,1)S(1)}, u32[]{:S(2)}) copy-start(bf16[512,256]{1,0:T(8,128)(2,1)S(1)} %collective-permute-done.2.refs_1_) | copy-start | bytes 786436
  23.6 13.3 %copy-start.7 = (bf16[512,256]{1,0:T(8,128)(2,1)}, bf16[512,256]{1,0:T(8,128)(2,1)S(1)}, u32[]{:S(2)}) copy-start(bf16[512,256]{1,0:T(8,128)(2,1)S(1)} %collective-permute-done.3.refs_2_) | copy-start | bytes 786436
  23.6 13.3 %copy-start.8 = (bf16[512,256]{1,0:T(8,128)(2,1)}, bf16[512,256]{1,0:T(8,128)(2,1)S(1)}, u32[]{:S(2)}) copy-start(bf16[512,256]{1,0:T(8,128)(2,1)S(1)} %collective-permute-done.4.refs_3_) | copy-start | bytes 786436
  23.6 11.2 %collective-permute-start.5 = (bf16[8,512,512]{2,1,0:T(8,128)(2,1)}, bf16[8,512,512]{2,1,0:T(8,128)(2,1)}, u32[]{:S(2)}, u32[]{:S(2)}) collective-permute-start(bf16[8,512,512]{2,1,0:T(8,128)(2,1)} %get-tuple-element.53), channel_id=1, source_target_pairs={{0,16},{16,0},{1,17},{17,1},{2,18},{18,2},{3,19},{19,3},{4,20},{20... | collective-permute-start | bytes 12582920 | tf_op jit(solution)/shard_map/ppermute | solution.py:434
  25.0 8.0 %collective-permute-start.6 = (bf16[2,512,128]{2,1,0:T(8,128)(2,1)S(1)}, bf16[2,512,128]{2,1,0:T(8,128)(2,1)S(1)}, u32[]{:S(2)}, u32[]{:S(2)}) collective-permute-start(bf16[2,512,128]{2,1,0:T(8,128)(2,1)S(1)} %pad_maximum_fusion.2.refs_0_), channel_id=1, source_target_pairs={{0,32},{32,0},{64,96},{96,64},{1,33},{33,1},{65,97},{97,65},{2,34}... | collective-permute-start | bytes 786440 | tf_op jit(solution)/shard_map/ppermute | solution.py:434
  25.6 16.5 %collective-permute-start.7 = (bf16[2,512,128]{2,1,0:T(8,128)(2,1)S(1)}, bf16[2,512,128]{2,1,0:T(8,128)(2,1)}, u32[]{:S(2)}, u32[]{:S(2)}) collective-permute-start(bf16[2,512,128]{2,1,0:T(8,128)(2,1)S(1)} %pad_maximum_fusion.2.refs_0_), channel_id=1, source_target_pairs={{0,64},{32,96},{64,0},{96,32},{1,65},{33,97},{65,1},{97,33},{2,66}... | collective-permute-start | bytes 786440 | tf_op jit(solution)/shard_map/ppermute | solution.py:434
  26.8 15.3 %collective-permute-start.8 = (bf16[2,512,128]{2,1,0:T(8,128)(2,1)S(1)}, bf16[2,512,128]{2,1,0:T(8,128)(2,1)}, u32[]{:S(2)}, u32[]{:S(2)}) collective-permute-start(bf16[2,512,128]{2,1,0:T(8,128)(2,1)S(1)} %pad_maximum_fusion.2.refs_0_), channel_id=1, source_target_pairs={{0,96},{32,64},{64,32},{96,0},{1,97},{33,65},{65,33},{97,1},{2,98}... | collective-permute-start | bytes 786440 | tf_op jit(solution)/shard_map/ppermute | solution.py:434
  33.0 9.1 %copy-start.12 = (bf16[2,512,128]{2,1,0:T(8,128)(2,1)}, bf16[2,512,128]{2,1,0:T(8,128)(2,1)S(1)}, u32[]{:S(2)}) copy-start(bf16[2,512,128]{2,1,0:T(8,128)(2,1)S(1)} %collective-permute-done.6.refs_1_) | copy-start | bytes 786436
  33.0 19.7 %collective-permute-start.9 = (bf16[512,256]{1,0:T(8,128)(2,1)S(1)}, bf16[512,256]{1,0:T(8,128)(2,1)S(1)}, u32[]{:S(2)}, u32[]{:S(2)}) collective-permute-start(bf16[512,256]{1,0:T(8,128)(2,1)S(1)} %collective-permute-done.refs_0_), channel_id=1, source_target_pairs={{0,32},{32,0},{64,96},{96,64},{1,33},{33,1},{65,97},{97,65},{2,34}... | collective-permute-start | bytes 786440 | tf_op jit(solution)/shard_map/ppermute | solution.py:434
  33.5 19.1 %collective-permute-start.10 = (bf16[512,256]{1,0:T(8,128)(2,1)S(1)}, bf16[512,256]{1,0:T(8,128)(2,1)S(1)}, u32[]{:S(2)}, u32[]{:S(2)}) collective-permute-start(bf16[512,256]{1,0:T(8,128)(2,1)S(1)} %collective-permute-done.refs_0_), channel_id=1, source_target_pairs={{0,64},{32,96},{64,0},{96,32},{1,65},{33,97},{65,1},{97,33},{2,66}... | collective-permute-start | bytes 786440 | tf_op jit(solution)/shard_map/ppermute | solution.py:434
  34.8 17.9 %collective-permute-start.11 = (bf16[512,256]{1,0:T(8,128)(2,1)S(1)}, bf16[512,256]{1,0:T(8,128)(2,1)S(1)}, u32[]{:S(2)}, u32[]{:S(2)}) collective-permute-start(bf16[512,256]{1,0:T(8,128)(2,1)S(1)} %collective-permute-done.refs_0_), channel_id=1, source_target_pairs={{0,96},{32,64},{64,32},{96,0},{1,97},{33,65},{65,33},{97,1},{2,98}... | collective-permute-start | bytes 786440 | tf_op jit(solution)/shard_map/ppermute | solution.py:434
  42.1 6.8 %copy-start.13 = (s32[2,17]{1,0:T(2,128)S(1)}, s32[2,17]{1,0:T(2,128)}, u32[]{:S(2)}) copy-start(s32[2,17]{1,0:T(2,128)} %param.16) | copy-start | bytes 412
  52.7 10.3 %copy-start.9 = (bf16[512,256]{1,0:T(8,128)(2,1)}, bf16[512,256]{1,0:T(8,128)(2,1)S(1)}, u32[]{:S(2)}) copy-start(bf16[512,256]{1,0:T(8,128)(2,1)S(1)} %collective-permute-done.9.refs_1_) | copy-start | bytes 786436
  52.7 10.3 %copy-start.10 = (bf16[512,256]{1,0:T(8,128)(2,1)}, bf16[512,256]{1,0:T(8,128)(2,1)S(1)}, u32[]{:S(2)}) copy-start(bf16[512,256]{1,0:T(8,128)(2,1)S(1)} %collective-permute-done.10.refs_2_) | copy-start | bytes 786436
  52.7 10.3 %copy-start.11 = (bf16[512,256]{1,0:T(8,128)(2,1)}, bf16[512,256]{1,0:T(8,128)(2,1)S(1)}, u32[]{:S(2)}) copy-start(bf16[512,256]{1,0:T(8,128)(2,1)S(1)} %collective-permute-done.11.refs_3_) | copy-start | bytes 786436
  52.7 3.7 %collective-permute-start.16 = (f32[128,512]{1,0:T(8,128)}, f32[128,512]{1,0:T(8,128)S(1)}, u32[]{:S(2)}, u32[]{:S(2)}) collective-permute-start(f32[128,512]{1,0:T(8,128)} %get-tuple-element.80), channel_id=1, source_target_pairs={{0,16},{16,0},{1,17},{17,1},{2,18},{18,2},{3,19},{19,3},{4,20},{20... | collective-permute-start | bytes 786440 | tf_op jit(solution)/shard_map/ppermute | solution.py:434
  56.5 1.0 copy-start.2
  57.6 11.8 %collective-permute-start.17 = (bf16[128,512]{1,0:T(8,128)(2,1)S(1)}, bf16[128,512]{1,0:T(8,128)(2,1)S(1)}, u32[]{:S(2)}, u32[]{:S(2)}) collective-permute-start(bf16[128,512]{1,0:T(8,128)(2,1)S(1)} %kv_finish.1), channel_id=1, source_target_pairs={{0,128},{128,0},{1,129},{129,1},{2,130},{130,2},{3,131},{131,3},{4... | collective-permute-start | bytes 393224 | tf_op jit(solution)/shard_map/ppermute | solution.py:434
  63.0 6.2 %copy-start.14 = (s32[16]{0:T(128)S(1)}, s32[16]{0:T(128)}, u32[]{:S(2)}) copy-start(s32[16]{0:T(128)} %param.17) | copy-start | bytes 196
  63.0 7.9 %copy-start.3 = (bf16[1,256]{1,0:T(2,128)(2,1)S(1)}, bf16[1,256]{1,0:T(2,128)(2,1)}, u32[]{:S(2)}) copy-start(bf16[1,256]{1,0:T(2,128)(2,1)} %bias_ref.1) | copy-start | bytes 1540
  63.0 17.7 %copy-start.15 = (s32[16]{0:T(128)S(1)}, s32[16]{0:T(128)}, u32[]{:S(2)}) copy-start(s32[16]{0:T(128)} %param.15) | copy-start | bytes 196
  68.4 2.5 %collective-permute-start.12 = (f32[512,256]{1,0:T(8,128)}, f32[512,256]{1,0:T(8,128)S(1)}, u32[]{:S(2)}, u32[]{:S(2)}) collective-permute-start(f32[512,256]{1,0:T(8,128)} %get-tuple-element.73), channel_id=1, source_target_pairs={{0,16},{16,0},{1,17},{17,1},{2,18},{18,2},{3,19},{19,3},{4,20},{20... | collective-permute-start | bytes 1572872 | tf_op jit(solution)/shard_map/ppermute | solution.py:434
  69.4 11.2 %collective-permute-start.18 = (bf16[2,128,512]{2,1,0:T(8,128)(2,1)S(1)}, bf16[2,128,512]{2,1,0:T(8,128)(2,1)S(1)}, u32[]{:S(2)}, u32[]{:S(2)}) collective-permute-start(bf16[2,128,512]{2,1,0:T(8,128)(2,1)S(1)} %pad_maximum_fusion), channel_id=1, source_target_pairs={{0,1},{1,0},{2,3},{3,2},{4,5},{5,4},{6,7},{7,6},{8,9},{9,8},{10,11... | collective-permute-start | bytes 786440 | tf_op jit(solution)/shard_map/ppermute | solution.py:434
  70.9 1.0 copy-start.1
  72.7 3.5 %collective-permute-start.15 = (bf16[128,256]{1,0:T(8,128)(2,1)S(1)}, bf16[128,256]{1,0:T(8,128)(2,1)S(1)}, u32[]{:S(2)}, u32[]{:S(2)}) collective-permute-start(bf16[128,256]{1,0:T(8,128)(2,1)S(1)} %get-tuple-element.79), channel_id=1, source_target_pairs={{0,3},{1,2},{2,1},{3,0},{4,7},{5,6},{6,5},{7,4},{8,11},{9,10},{10,... | collective-permute-start | bytes 196616 | tf_op jit(solution)/shard_map/ppermute | solution.py:434
  72.8 6.1 %collective-permute-start.14 = (bf16[128,256]{1,0:T(8,128)(2,1)S(1)}, bf16[128,256]{1,0:T(8,128)(2,1)S(1)}, u32[]{:S(2)}, u32[]{:S(2)}) collective-permute-start(bf16[128,256]{1,0:T(8,128)(2,1)S(1)} %get-tuple-element.78), channel_id=1, source_target_pairs={{0,2},{1,3},{2,0},{3,1},{4,6},{5,7},{6,4},{7,5},{8,10},{9,11},{10,... | collective-permute-start | bytes 196616 | tf_op jit(solution)/shard_map/ppermute | solution.py:434
  75.0 5.6 %collective-permute-start.13 = (bf16[128,256]{1,0:T(8,128)(2,1)S(1)}, bf16[128,256]{1,0:T(8,128)(2,1)S(1)}, u32[]{:S(2)}, u32[]{:S(2)}) collective-permute-start(bf16[128,256]{1,0:T(8,128)(2,1)S(1)} %get-tuple-element.77), channel_id=1, source_target_pairs={{0,1},{1,0},{2,3},{3,2},{4,5},{5,4},{6,7},{7,6},{8,9},{9,8},{10,11... | collective-permute-start | bytes 196616 | tf_op jit(solution)/shard_map/ppermute | solution.py:434
  80.7 8.1 %collective-permute-start.19 = (bf16[2,128,512]{2,1,0:T(8,128)(2,1)S(1)}, bf16[2,128,512]{2,1,0:T(8,128)(2,1)S(1)}, u32[]{:S(2)}, u32[]{:S(2)}) collective-permute-start(bf16[2,128,512]{2,1,0:T(8,128)(2,1)S(1)} %pad_maximum_fusion.1.refs_0_), channel_id=1, source_target_pairs={{0,32},{32,0},{64,96},{96,64},{1,33},{33,1},{65,97},{97,65},{2,34}... | collective-permute-start | bytes 786440 | tf_op jit(solution)/shard_map/ppermute | solution.py:434
  81.0 12.5 %collective-permute-start.20 = (bf16[2,128,512]{2,1,0:T(8,128)(2,1)S(1)}, bf16[2,128,512]{2,1,0:T(8,128)(2,1)S(1)}, u32[]{:S(2)}, u32[]{:S(2)}) collective-permute-start(bf16[2,128,512]{2,1,0:T(8,128)(2,1)S(1)} %pad_maximum_fusion.1.refs_0_), channel_id=1, source_target_pairs={{0,64},{32,96},{64,0},{96,32},{1,65},{33,97},{65,1},{97,33},{2,66}... | collective-permute-start | bytes 786440 | tf_op jit(solution)/shard_map/ppermute | solution.py:434
  83.7 13.5 %collective-permute-start.21 = (bf16[2,128,512]{2,1,0:T(8,128)(2,1)S(1)}, bf16[2,128,512]{2,1,0:T(8,128)(2,1)S(1)}, u32[]{:S(2)}, u32[]{:S(2)}) collective-permute-start(bf16[2,128,512]{2,1,0:T(8,128)(2,1)S(1)} %pad_maximum_fusion.1.refs_0_), channel_id=1, source_target_pairs={{0,96},{32,64},{64,32},{96,0},{1,97},{33,65},{65,33},{97,1},{2,98}... | collective-permute-start | bytes 786440 | tf_op jit(solution)/shard_map/ppermute | solution.py:434
  84.9 12.3 %collective-permute-start.22 = (bf16[4,128,256]{2,1,0:T(8,128)(2,1)S(1)}, bf16[4,128,256]{2,1,0:T(8,128)(2,1)S(1)}, u32[]{:S(2)}, u32[]{:S(2)}) collective-permute-start(bf16[4,128,256]{2,1,0:T(8,128)(2,1)S(1)} %pad_maximum_fusion.5.refs_0_), channel_id=1, source_target_pairs={{0,4},{4,0},{8,12},{12,8},{1,5},{5,1},{9,13},{13,9},{2,6},{6,2},{1... | collective-permute-start | bytes 786440 | tf_op jit(solution)/shard_map/ppermute | solution.py:434
  86.2 11.5 %collective-permute-start.23 = (bf16[4,128,256]{2,1,0:T(8,128)(2,1)S(1)}, bf16[4,128,256]{2,1,0:T(8,128)(2,1)S(1)}, u32[]{:S(2)}, u32[]{:S(2)}) collective-permute-start(bf16[4,128,256]{2,1,0:T(8,128)(2,1)S(1)} %pad_maximum_fusion.5.refs_0_), channel_id=1, source_target_pairs={{0,8},{4,12},{8,0},{12,4},{1,9},{5,13},{9,1},{13,5},{2,10},{6,14},... | collective-permute-start | bytes 786440 | tf_op jit(solution)/shard_map/ppermute | solution.py:434
  88.8 13.4 %collective-permute-start.24 = (bf16[4,128,256]{2,1,0:T(8,128)(2,1)S(1)}, bf16[4,128,256]{2,1,0:T(8,128)(2,1)S(1)}, u32[]{:S(2)}, u32[]{:S(2)}) collective-permute-start(bf16[4,128,256]{2,1,0:T(8,128)(2,1)S(1)} %pad_maximum_fusion.5.refs_0_), channel_id=1, source_target_pairs={{0,12},{4,8},{8,4},{12,0},{1,13},{5,9},{9,5},{13,1},{2,14},{6,10},... | collective-permute-start | bytes 786440 | tf_op jit(solution)/shard_map/ppermute | solution.py:434
  103.5 11.4 %collective-permute-start.28 = (bf16[2,128,2048]{2,1,0:T(8,128)(2,1)S(1)}, bf16[2,128,2048]{2,1,0:T(8,128)(2,1)S(1)}, u32[]{:S(2)}, u32[]{:S(2)}) collective-permute-start(bf16[2,128,2048]{2,1,0:T(8,128)(2,1)S(1)} %assemble.1.near_ref), channel_id=1, source_target_pairs={{0,16},{16,0},{1,17},{17,1},{2,18},{18,2},{3,19},{19,3},{4,20},{20... | collective-permute-start | bytes 3145736 | tf_op jit(solution)/shard_map/ppermute | solution.py:434
  105.8 3.7 %collective-permute-start.25 = (bf16[128,256]{1,0:T(8,128)(2,1)S(1)}, bf16[128,256]{1,0:T(8,128)(2,1)S(1)}, u32[]{:S(2)}, u32[]{:S(2)}) collective-permute-start(bf16[128,256]{1,0:T(8,128)(2,1)S(1)} %get-tuple-element.87), channel_id=1, source_target_pairs={{0,1},{1,0},{2,3},{3,2},{4,5},{5,4},{6,7},{7,6},{8,9},{9,8},{10,11... | collective-permute-start | bytes 196616 | tf_op jit(solution)/shard_map/ppermute | solution.py:434
  106.4 4.1 %collective-permute-start.26 = (bf16[128,256]{1,0:T(8,128)(2,1)S(1)}, bf16[128,256]{1,0:T(8,128)(2,1)S(1)}, u32[]{:S(2)}, u32[]{:S(2)}) collective-permute-start(bf16[128,256]{1,0:T(8,128)(2,1)S(1)} %get-tuple-element.88), channel_id=1, source_target_pairs={{0,2},{1,3},{2,0},{3,1},{4,6},{5,7},{6,4},{7,5},{8,10},{9,11},{10,... | collective-permute-start | bytes 196616 | tf_op jit(solution)/shard_map/ppermute | solution.py:434
  106.9 8.0 %collective-permute-start.27 = (bf16[128,256]{1,0:T(8,128)(2,1)S(1)}, bf16[128,256]{1,0:T(8,128)(2,1)S(1)}, u32[]{:S(2)}, u32[]{:S(2)}) collective-permute-start(bf16[128,256]{1,0:T(8,128)(2,1)S(1)} %get-tuple-element.89), channel_id=1, source_target_pairs={{0,3},{1,2},{2,1},{3,0},{4,7},{5,6},{6,5},{7,4},{8,11},{9,10},{10,... | collective-permute-start | bytes 196616 | tf_op jit(solution)/shard_map/ppermute | solution.py:434

commit v3 on v2

--- a/solution.py
+++ b/solution.py
@@ -53,7 +53,7 @@
             piece = hbuf[i, :, pl.ds(pl.multiple_of(k * width, width), width)].astype(F32)
             return total + piece * piece
 
-        total = lax.fori_loop(0, 2 * parts, square, jnp.zeros((step, width), F32), unroll=4)
+        total = lax.fori_loop(0, 2 * parts, square, jnp.zeros((step, width), F32), unroll=8)
         mean = jnp.sum(total, axis=1, keepdims=True) * (1.0 / (2 * parts * width))
         rs = lax.rsqrt(mean + EPSILON)
         rows_i = pl.ds(pl.multiple_of(i * step, step), step)
@@ -66,7 +66,7 @@
                 o_ref[k, rows_i, :] = (piece * rs * gain).astype(BF)
                 return inner
 
-            lax.fori_loop(0, parts, scale, 0, unroll=4)
+            lax.fori_loop(0, parts, scale, 0, unroll=8)
             store(i, t).start()
         return carry
 

time: 127 us -> 127 us (level)
  no operation moved by 1% of the time
where the time goes in v3:
time: 127 us; the launch traced here: 126 us
  starting transfers between devices  44 us (35%)
  Pallas kernels  39.2 us (31%)
  waiting for transfers between devices  33.3 us (26%)
  other arithmetic  5 us (4%)
  local copies, waits for them, and re-layouts  4.46 us (4%)
    ppermute x29, starting transfers between devices, flip(): return lax.ppermute(v, axis, [(i, i ^ bits) for i in range(n)])  44 us
    ppermute x29, waiting for transfers between devices, flip(): return lax.ppermute(v, axis, [(i, i ^ bits) for i in range(n)])  33.3 us
    pallas_call x1, Pallas kernels, attention(): pl.pallas_call(attention_kernel, grid_spec=pltpu.PrefetchScalarGridSpec(n...  11.4 us
    pallas_call x2, Pallas kernels, q_project(): pl.pallas_call(functools.partial(q_kernel, first), in_specs=[HBM] * (6 +...  10.6 us
    pallas_call x1, Pallas kernels, norm(): pl.pallas_call(norm_kernel, grid_spec=pltpu.PrefetchScalarGridSpec(num_sc...  8.24 us
    pallas_call x1, Pallas kernels, kv_project(): pl.pallas_call(kv_kernel, in_specs=[HBM] * 6, out_specs=[full((128, rows)...  6.76 us
  transfers between devices with their start and end apart: 29, of which 14 were waited for; matrix products, arithmetic and copies ran while one was open for 6% of the time, Pallas kernels for 21%

profile of v3, /device:TPU:39, one launch (start us, length us, event | category | flops | bytes accessed | tf_op | source)
XLA Modules:
  0.0 126.5 jit_solution(7085412267911130521)
XLA Ops:
  0.0 6.0 %collective-permute-start = (bf16[512,256]{1,0:T(8,128)(2,1)}, bf16[512,256]{1,0:T(8,128)(2,1)S(1)}, u32[]{:S(2)}, u32[]{:S(2)}) collective-permute-start(bf16[512,256]{1,0:T(8,128)(2,1)} %bitcast.21), channel_id=1, source_target_pairs={{0,128},{128,0},{1,129},{129,1},{2,130},{130,2},{3,131},{131,3},{4... | collective-permute-start | bytes 786440 | tf_op jit(solution)/shard_map/ppermute | solution.py:434
  6.6 0.8 collective-permute-start.3
  7.4 2.5 %collective-permute-start.4 = (bf16[512,256]{1,0:T(8,128)(2,1)}, bf16[512,256]{1,0:T(8,128)(2,1)S(1)}, u32[]{:S(2)}, u32[]{:S(2)}) collective-permute-start(bf16[512,256]{1,0:T(8,128)(2,1)} %bitcast.24), channel_id=1, source_target_pairs={{0,96},{32,64},{64,32},{96,0},{1,97},{33,65},{65,33},{97,1},{2,98}... | collective-permute-start | bytes 786440 | tf_op jit(solution)/shard_map/ppermute | solution.py:434
  10.7 1.3 %reshape.47.g_ref = bf16[1,8192]{1,0:T(2,128)(2,1)} reshape(bf16[8192]{0:T(1024)(128)(2,1)} %param.10) | data formatting | bytes 32768 | tf_op jit(solution)/shard_map/reshape | solution.py:105
  12.1 8.2 %norm.1 = (bf16[8,512,512]{2,1,0:T(8,128)(2,1)}, bf16[8,512,512]{2,1,0:T(8,128)(2,1)}) custom-call(s32[16]{0:T(128)} %xor_add_fusion.order, bf16[512,8192]{1,0:T(8,128)(2,1)} %h_hbm.1, bf16[1,8192]{1,0:T(2,128)(2,1)} %reshape.47.g_ref), custom_call_target="tpu_custom_call" | custom-call | bytes 20971520 | tf_op jit(solution)/shard_map/norm/pallas_call | solution.py:86
  20.5 3.0 %collective-permute-done.1 = bf16[512,128]{1,0:T(8,128)(2,1)S(1)} collective-permute-done((bf16[512,128]{1,0:T(8,128)(2,1)S(1)}, bf16[512,128]{1,0:T(8,128)(2,1)S(1)}, u32[]{:S(2)}, u32[]{:S(2)}) %collective-permute-start.1) | collective-permute-done | bytes 131104 | tf_op jit(solution)/shard_map/ppermute | solution.py:434
  23.6 1.4 %collective-permute-start.5 = (bf16[8,512,512]{2,1,0:T(8,128)(2,1)}, bf16[8,512,512]{2,1,0:T(8,128)(2,1)}, u32[]{:S(2)}, u32[]{:S(2)}) collective-permute-start(bf16[8,512,512]{2,1,0:T(8,128)(2,1)} %get-tuple-element.53), channel_id=1, source_target_pairs={{0,16},{16,0},{1,17},{17,1},{2,18},{18,2},{3,19},{19,3},{4,20},{20... | collective-permute-start | bytes 12582920 | tf_op jit(solution)/shard_map/ppermute | solution.py:434
  25.0 0.6 collective-permute-start.6
  25.6 1.2 collective-permute-start.7
  26.8 2.1 %collective-permute-start.8 = (bf16[2,512,128]{2,1,0:T(8,128)(2,1)S(1)}, bf16[2,512,128]{2,1,0:T(8,128)(2,1)}, u32[]{:S(2)}, u32[]{:S(2)}) collective-permute-start(bf16[2,512,128]{2,1,0:T(8,128)(2,1)S(1)} %pad_maximum_fusion.2.refs_0_), channel_id=1, source_target_pairs={{0,96},{32,64},{64,32},{96,0},{1,97},{33,65},{65,33},{97,1},{2,98}... | collective-permute-start | bytes 786440 | tf_op jit(solution)/shard_map/ppermute | solution.py:434
  28.9 4.1 %collective-permute-done.6.refs_1_ = bf16[2,512,128]{2,1,0:T(8,128)(2,1)S(1)} collective-permute-done((bf16[2,512,128]{2,1,0:T(8,128)(2,1)S(1)}, bf16[2,512,128]{2,1,0:T(8,128)(2,1)S(1)}, u32[]{:S(2)}, u32[]{:S(2)}) %collective-permute-start.6) | collective-permute-done | bytes 262176 | tf_op jit(solution)/shard_map/ppermute | solution.py:434
  33.5 1.2 collective-permute-start.10
  34.8 2.1 %collective-permute-start.11 = (bf16[512,256]{1,0:T(8,128)(2,1)S(1)}, bf16[512,256]{1,0:T(8,128)(2,1)S(1)}, u32[]{:S(2)}, u32[]{:S(2)}) collective-permute-start(bf16[512,256]{1,0:T(8,128)(2,1)S(1)} %collective-permute-done.refs_0_), channel_id=1, source_target_pairs={{0,96},{32,64},{64,32},{96,0},{1,97},{33,65},{65,33},{97,1},{2,98}... | collective-permute-start | bytes 786440 | tf_op jit(solution)/shard_map/ppermute | solution.py:434
  36.9 5.2 %q_project.2 = (f32[512,256]{1,0:T(8,128)}, f32[512,256]{1,0:T(8,128)}) custom-call(bf16[8,512,512]{2,1,0:T(8,128)(2,1)} %get-tuple-element.59.near_ref, bf16[8,512,512]{2,1,0:T(8,128)(2,1)} %collective-permute-done.5.far_ref, bf16[512,256]{1,0:T(8,128)(2,1)} %bitcast.25, bf16[512,256]{1,0:T(8,128)(2,1)} %copy-done.6, bf16[512,256]{1,0:T(8,128)(2,1)} %copy-done.7, ...), custom_call_target="tpu_custom_call" | custom-call | bytes 10485760 | tf_op jit(solution)/shard_map/q_project/pallas_call | solution.py:233
  42.1 6.8 %kv_project.1 = (f32[128,512]{1,0:T(8,128)}, f32[128,512]{1,0:T(8,128)}) custom-call(bf16[8,512,512]{2,1,0:T(8,128)(2,1)} %get-tuple-element.59.near_ref, bf16[8,512,512]{2,1,0:T(8,128)(2,1)} %collective-permute-done.5.far_ref, bf16[2,512,128]{2,1,0:T(8,128)(2,1)} %copy-done.4, bf16[2,512,128]{2,1,0:T(8,128)(2,1)} %copy-done.12, ...), custom_call_target="tpu_custom_call" | custom-call | bytes 20971520 | tf_op jit(solution)/shard_map/kv_project/pallas_call | solution.py:152
  49.0 0.6 fusion.14
  49.6 1.3 fusion.4
  50.9 1.0 fusion.2
  52.7 2.3 %collective-permute-start.16 = (f32[128,512]{1,0:T(8,128)}, f32[128,512]{1,0:T(8,128)S(1)}, u32[]{:S(2)}, u32[]{:S(2)}) collective-permute-start(f32[128,512]{1,0:T(8,128)} %get-tuple-element.80), channel_id=1, source_target_pairs={{0,16},{16,0},{1,17},{17,1},{2,18},{18,2},{3,19},{19,3},{4,20},{20... | collective-permute-start | bytes 786440 | tf_op jit(solution)/shard_map/ppermute | solution.py:434
  55.1 0.8 bitcast_convert_fusion
  55.8 0.6 collective-permute-done.16.two_ref
  56.5 1.0 copy-done.2
  57.6 5.4 %collective-permute-start.17 = (bf16[128,512]{1,0:T(8,128)(2,1)S(1)}, bf16[128,512]{1,0:T(8,128)(2,1)S(1)}, u32[]{:S(2)}, u32[]{:S(2)}) collective-permute-start(bf16[128,512]{1,0:T(8,128)(2,1)S(1)} %kv_finish.1), channel_id=1, source_target_pairs={{0,128},{128,0},{1,129},{129,1},{2,130},{130,2},{3,131},{131,3},{4... | collective-permute-start | bytes 393224 | tf_op jit(solution)/shard_map/ppermute | solution.py:434
  63.0 5.4 %q_project.3 = (f32[512,256]{1,0:T(8,128)}, f32[512,256]{1,0:T(8,128)}) custom-call(bf16[8,512,512]{2,1,0:T(8,128)(2,1)} %get-tuple-element.59.near_ref, bf16[8,512,512]{2,1,0:T(8,128)(2,1)} %collective-permute-done.5.far_ref, bf16[512,256]{1,0:T(8,128)(2,1)} %copy-done.5, bf16[512,256]{1,0:T(8,128)(2,1)} %copy-done.9, bf16[512,256]{1,0:T(8,128)(2,1)} %copy-done.10, ...), custom_call_target="tpu_custom_call" | custom-call | bytes 10485760 | tf_op jit(solution)/shard_map/q_project/pallas_call | solution.py:233
  68.4 0.7 collective-permute-start.12
  69.6 1.3 %collective-permute-done.12.two_ref = f32[512,256]{1,0:T(8,128)S(1)} collective-permute-done((f32[512,256]{1,0:T(8,128)}, f32[512,256]{1,0:T(8,128)S(1)}, u32[]{:S(2)}, u32[]{:S(2)}) %collective-permute-start.12) | collective-permute-done | bytes 524320 | tf_op jit(solution)/shard_map/ppermute | solution.py:434
  70.9 1.0 copy-done.1
  71.9 0.8 q_finish.1
  72.8 2.2 %collective-permute-start.14 = (bf16[128,256]{1,0:T(8,128)(2,1)S(1)}, bf16[128,256]{1,0:T(8,128)(2,1)S(1)}, u32[]{:S(2)}, u32[]{:S(2)}) collective-permute-start(bf16[128,256]{1,0:T(8,128)(2,1)S(1)} %get-tuple-element.78), channel_id=1, source_target_pairs={{0,2},{1,3},{2,0},{3,1},{4,6},{5,7},{6,4},{7,5},{8,10},{9,11},{10,... | collective-permute-start | bytes 196616 | tf_op jit(solution)/shard_map/ppermute | solution.py:434
  75.5 0.8 collective-permute-done.15
  76.2 2.7 %collective-permute-done.14 = bf16[128,256]{1,0:T(8,128)(2,1)S(1)} collective-permute-done((bf16[128,256]{1,0:T(8,128)(2,1)S(1)}, bf16[128,256]{1,0:T(8,128)(2,1)S(1)}, u32[]{:S(2)}, u32[]{:S(2)}) %collective-permute-start.14) | collective-permute-done | bytes 65568 | tf_op jit(solution)/shard_map/ppermute | solution.py:434
  78.9 1.6 %collective-permute-done.13 = bf16[128,256]{1,0:T(8,128)(2,1)S(1)} collective-permute-done((bf16[128,256]{1,0:T(8,128)(2,1)S(1)}, bf16[128,256]{1,0:T(8,128)(2,1)S(1)}, u32[]{:S(2)}, u32[]{:S(2)}) %collective-permute-start.13) | collective-permute-done | bytes 65568 | tf_op jit(solution)/shard_map/ppermute | solution.py:434
  81.0 2.7 %collective-permute-start.20 = (bf16[2,128,512]{2,1,0:T(8,128)(2,1)S(1)}, bf16[2,128,512]{2,1,0:T(8,128)(2,1)S(1)}, u32[]{:S(2)}, u32[]{:S(2)}) collective-permute-start(bf16[2,128,512]{2,1,0:T(8,128)(2,1)S(1)} %pad_maximum_fusion.1.refs_0_), channel_id=1, source_target_pairs={{0,64},{32,96},{64,0},{96,32},{1,65},{33,97},{65,1},{97,33},{2,66}... | collective-permute-start | bytes 786440 | tf_op jit(solution)/shard_map/ppermute | solution.py:434
  83.7 1.2 collective-permute-start.21
  84.9 1.3 %collective-permute-start.22 = (bf16[4,128,256]{2,1,0:T(8,128)(2,1)S(1)}, bf16[4,128,256]{2,1,0:T(8,128)(2,1)S(1)}, u32[]{:S(2)}, u32[]{:S(2)}) collective-permute-start(bf16[4,128,256]{2,1,0:T(8,128)(2,1)S(1)} %pad_maximum_fusion.5.refs_0_), channel_id=1, source_target_pairs={{0,4},{4,0},{8,12},{12,8},{1,5},{5,1},{9,13},{13,9},{2,6},{6,2},{1... | collective-permute-start | bytes 786440 | tf_op jit(solution)/shard_map/ppermute | solution.py:434
  86.2 2.6 %collective-permute-start.23 = (bf16[4,128,256]{2,1,0:T(8,128)(2,1)S(1)}, bf16[4,128,256]{2,1,0:T(8,128)(2,1)S(1)}, u32[]{:S(2)}, u32[]{:S(2)}) collective-permute-start(bf16[4,128,256]{2,1,0:T(8,128)(2,1)S(1)} %pad_maximum_fusion.5.refs_0_), channel_id=1, source_target_pairs={{0,8},{4,12},{8,0},{12,4},{1,9},{5,13},{9,1},{13,5},{2,10},{6,14},... | collective-permute-start | bytes 786440 | tf_op jit(solution)/shard_map/ppermute | solution.py:434
  89.5 4.0 %collective-permute-done.20.refs_2_ = bf16[2,128,512]{2,1,0:T(8,128)(2,1)S(1)} collective-permute-done((bf16[2,128,512]{2,1,0:T(8,128)(2,1)S(1)}, bf16[2,128,512]{2,1,0:T(8,128)(2,1)S(1)}, u32[]{:S(2)}, u32[]{:S(2)}) %collective-permute-start.20) | collective-permute-done | bytes 262176 | tf_op jit(solution)/shard_map/ppermute | solution.py:434
  93.4 3.8 %collective-permute-done.21.refs_3_ = bf16[2,128,512]{2,1,0:T(8,128)(2,1)S(1)} collective-permute-done((bf16[2,128,512]{2,1,0:T(8,128)(2,1)S(1)}, bf16[2,128,512]{2,1,0:T(8,128)(2,1)S(1)}, u32[]{:S(2)}, u32[]{:S(2)}) %collective-permute-start.21) | collective-permute-done | bytes 262176 | tf_op jit(solution)/shard_map/ppermute | solution.py:434
  97.7 4.5 %collective-permute-done.24.refs_3_ = bf16[4,128,256]{2,1,0:T(8,128)(2,1)S(1)} collective-permute-done((bf16[4,128,256]{2,1,0:T(8,128)(2,1)S(1)}, bf16[4,128,256]{2,1,0:T(8,128)(2,1)S(1)}, u32[]{:S(2)}, u32[]{:S(2)}) %collective-permute-start.24) | collective-permute-done | bytes 262176 | tf_op jit(solution)/shard_map/ppermute | solution.py:434
  102.2 0.7 choose.1
  102.9 0.6 assemble.1.near_ref
  103.5 2.3 %collective-permute-start.28 = (bf16[2,128,2048]{2,1,0:T(8,128)(2,1)S(1)}, bf16[2,128,2048]{2,1,0:T(8,128)(2,1)S(1)}, u32[]{:S(2)}, u32[]{:S(2)}) collective-permute-start(bf16[2,128,2048]{2,1,0:T(8,128)(2,1)S(1)} %assemble.1.near_ref), channel_id=1, source_target_pairs={{0,16},{16,0},{1,17},{17,1},{2,18},{18,2},{3,19},{19,3},{4,20},{20... | collective-permute-start | bytes 3145736 | tf_op jit(solution)/shard_map/ppermute | solution.py:434
  105.8 0.7 collective-permute-start.25
  106.9 1.5 %collective-permute-start.27 = (bf16[128,256]{1,0:T(8,128)(2,1)S(1)}, bf16[128,256]{1,0:T(8,128)(2,1)S(1)}, u32[]{:S(2)}, u32[]{:S(2)}) collective-permute-start(bf16[128,256]{1,0:T(8,128)(2,1)S(1)} %get-tuple-element.89), channel_id=1, source_target_pairs={{0,3},{1,2},{2,1},{3,0},{4,7},{5,6},{6,5},{7,4},{8,11},{9,10},{10,... | collective-permute-start | bytes 196616 | tf_op jit(solution)/shard_map/ppermute | solution.py:434
  108.5 1.0 collective-permute-done.25.q1
  109.4 1.1 collective-permute-done.26.q2
  110.5 4.3 %collective-permute-done.27.q3 = bf16[128,256]{1,0:T(8,128)(2,1)S(1)} collective-permute-done((bf16[128,256]{1,0:T(8,128)(2,1)S(1)}, bf16[128,256]{1,0:T(8,128)(2,1)S(1)}, u32[]{:S(2)}, u32[]{:S(2)}) %collective-permute-start.27) | collective-permute-done | bytes 65568 | tf_op jit(solution)/shard_map/ppermute | solution.py:434
  114.9 11.4 %attention.1 = bf16[512,256]{1,0:T(8,128)(2,1)} custom-call(s32[16]{0:T(128)S(1)} %concatenate.9.tab, bf16[128,256]{1,0:T(8,128)(2,1)S(1)} %get-tuple-element.86.q0, bf16[128,256]{1,0:T(8,128)(2,1)S(1)} %collective-permute-done.25.q1, bf16[128,256]{1,0:T(8,128)(2,1)S(1)} %collective-permute-done.26.q2, bf16[128,256]{1,0:T(8,128)(2,1)S(1)} %collective-permute-done.27.q3, ...), custom_call_target="tpu_custom_call" | custom-call | tf_op jit(solution)/shard_map/attention/pallas_call | solution.py:407
  (81 shorter events, 6.3 us)
Async XLA Ops:
  0.0 9.9 %copy-start = (bf16[4,512,256]{2,1,0:T(8,128)(2,1)S(1)}, bf16[4,512,256]{2,1,0:T(8,128)(2,1)}, u32[]{:S(2)}) copy-start(bf16[4,512,256]{2,1,0:T(8,128)(2,1)} %param.13) | copy-start | bytes 3145732
  0.0 23.5 %collective-permute-start = (bf16[512,256]{1,0:T(8,128)(2,1)}, bf16[512,256]{1,0:T(8,128)(2,1)S(1)}, u32[]{:S(2)}, u32[]{:S(2)}) collective-permute-start(bf16[512,256]{1,0:T(8,128)(2,1)} %bitcast.21), channel_id=1, source_target_pairs={{0,128},{128,0},{1,129},{129,1},{2,130},{130,2},{3,131},{131,3},{4... | collective-permute-start | bytes 786440 | tf_op jit(solution)/shard_map/ppermute | solution.py:434
  6.0 17.5 %collective-permute-start.2 = (bf16[512,256]{1,0:T(8,128)(2,1)}, bf16[512,256]{1,0:T(8,128)(2,1)S(1)}, u32[]{:S(2)}, u32[]{:S(2)}) collective-permute-start(bf16[512,256]{1,0:T(8,128)(2,1)} %bitcast.22), channel_id=1, source_target_pairs={{0,32},{32,0},{64,96},{96,64},{1,33},{33,1},{65,97},{97,65},{2,34}... | collective-permute-start | bytes 786440 | tf_op jit(solution)/shard_map/ppermute | solution.py:434
  6.6 17.0 %collective-permute-start.3 = (bf16[512,256]{1,0:T(8,128)(2,1)}, bf16[512,256]{1,0:T(8,128)(2,1)S(1)}, u32[]{:S(2)}, u32[]{:S(2)}) collective-permute-start(bf16[512,256]{1,0:T(8,128)(2,1)} %bitcast.23), channel_id=1, source_target_pairs={{0,64},{32,96},{64,0},{96,32},{1,65},{33,97},{65,1},{97,33},{2,66}... | collective-permute-start | bytes 786440 | tf_op jit(solution)/shard_map/ppermute | solution.py:434
  7.4 16.2 %collective-permute-start.4 = (bf16[512,256]{1,0:T(8,128)(2,1)}, bf16[512,256]{1,0:T(8,128)(2,1)S(1)}, u32[]{:S(2)}, u32[]{:S(2)}) collective-permute-start(bf16[512,256]{1,0:T(8,128)(2,1)} %bitcast.24), channel_id=1, source_target_pairs={{0,96},{32,64},{64,32},{96,0},{1,97},{33,65},{65,33},{97,1},{2,98}... | collective-permute-start | bytes 786440 | tf_op jit(solution)/shard_map/ppermute | solution.py:434
  10.0 13.5 %collective-permute-start.1 = (bf16[512,128]{1,0:T(8,128)(2,1)S(1)}, bf16[512,128]{1,0:T(8,128)(2,1)S(1)}, u32[]{:S(2)}, u32[]{:S(2)}) collective-permute-start(bf16[512,128]{1,0:T(8,128)(2,1)S(1)} %fusion.15), channel_id=1, source_target_pairs={{0,128},{128,0},{1,129},{129,1},{2,130},{130,2},{3,131},{131,3},{4... | collective-permute-start | bytes 393224 | tf_op jit(solution)/shard_map/ppermute | solution.py:434
  23.5 18.5 %copy-start.4 = (bf16[2,512,128]{2,1,0:T(8,128)(2,1)}, bf16[2,512,128]{2,1,0:T(8,128)(2,1)S(1)}, u32[]{:S(2)}) copy-start(bf16[2,512,128]{2,1,0:T(8,128)(2,1)S(1)} %pad_maximum_fusion.2.refs_0_) | copy-start | bytes 786436
  23.5 18.5 %copy-start.5 = (bf16[512,256]{1,0:T(8,128)(2,1)}, bf16[512,256]{1,0:T(8,128)(2,1)S(1)}, u32[]{:S(2)}) copy-start(bf16[512,256]{1,0:T(8,128)(2,1)S(1)} %collective-permute-done.refs_0_) | copy-start | bytes 786436
  23.5 13.3 %copy-start.6 = (bf16[512,256]{1,0:T(8,128)(2,1)}, bf16[512,256]{1,0:T(8,128)(2,1)S(1)}, u32[]{:S(2)}) copy-start(bf16[512,256]{1,0:T(8,128)(2,1)S(1)} %collective-permute-done.2.refs_1_) | copy-start | bytes 786436
  23.6 13.3 %copy-start.7 = (bf16[512,256]{1,0:T(8,128)(2,1)}, bf16[512,256]{1,0:T(8,128)(2,1)S(1)}, u32[]{:S(2)}) copy-start(bf16[512,256]{1,0:T(8,128)(2,1)S(1)} %collective-permute-done.3.refs_2_) | copy-start | bytes 786436
  23.6 13.3 %copy-start.8 = (bf16[512,256]{1,0:T(8,128)(2,1)}, bf16[512,256]{1,0:T(8,128)(2,1)S(1)}, u32[]{:S(2)}) copy-start(bf16[512,256]{1,0:T(8,128)(2,1)S(1)} %collective-permute-done.4.refs_3_) | copy-start | bytes 786436
  23.6 11.2 %collective-permute-start.5 = (bf16[8,512,512]{2,1,0:T(8,128)(2,1)}, bf16[8,512,512]{2,1,0:T(8,128)(2,1)}, u32[]{:S(2)}, u32[]{:S(2)}) collective-permute-start(bf16[8,512,512]{2,1,0:T(8,128)(2,1)} %get-tuple-element.53), channel_id=1, source_target_pairs={{0,16},{16,0},{1,17},{17,1},{2,18},{18,2},{3,19},{19,3},{4,20},{20... | collective-permute-start | bytes 12582920 | tf_op jit(solution)/shard_map/ppermute | solution.py:434
  25.0 8.0 %collective-permute-start.6 = (bf16[2,512,128]{2,1,0:T(8,128)(2,1)S(1)}, bf16[2,512,128]{2,1,0:T(8,128)(2,1)S(1)}, u32[]{:S(2)}, u32[]{:S(2)}) collective-permute-start(bf16[2,512,128]{2,1,0:T(8,128)(2,1)S(1)} %pad_maximum_fusion.2.refs_0_), channel_id=1, source_target_pairs={{0,32},{32,0},{64,96},{96,64},{1,33},{33,1},{65,97},{97,65},{2,34}... | collective-permute-start | bytes 786440 | tf_op jit(solution)/shard_map/ppermute | solution.py:434
  25.6 16.5 %collective-permute-start.7 = (bf16[2,512,128]{2,1,0:T(8,128)(2,1)S(1)}, bf16[2,512,128]{2,1,0:T(8,128)(2,1)}, u32[]{:S(2)}, u32[]{:S(2)}) collective-permute-start(bf16[2,512,128]{2,1,0:T(8,128)(2,1)S(1)} %pad_maximum_fusion.2.refs_0_), channel_id=1, source_target_pairs={{0,64},{32,96},{64,0},{96,32},{1,65},{33,97},{65,1},{97,33},{2,66}... | collective-permute-start | bytes 786440 | tf_op jit(solution)/shard_map/ppermute | solution.py:434
  26.8 15.3 %collective-permute-start.8 = (bf16[2,512,128]{2,1,0:T(8,128)(2,1)S(1)}, bf16[2,512,128]{2,1,0:T(8,128)(2,1)}, u32[]{:S(2)}, u32[]{:S(2)}) collective-permute-start(bf16[2,512,128]{2,1,0:T(8,128)(2,1)S(1)} %pad_maximum_fusion.2.refs_0_), channel_id=1, source_target_pairs={{0,96},{32,64},{64,32},{96,0},{1,97},{33,65},{65,33},{97,1},{2,98}... | collective-permute-start | bytes 786440 | tf_op jit(solution)/shard_map/ppermute | solution.py:434
  33.0 9.1 %copy-start.12 = (bf16[2,512,128]{2,1,0:T(8,128)(2,1)}, bf16[2,512,128]{2,1,0:T(8,128)(2,1)S(1)}, u32[]{:S(2)}) copy-start(bf16[2,512,128]{2,1,0:T(8,128)(2,1)S(1)} %collective-permute-done.6.refs_1_) | copy-start | bytes 786436
  33.0 19.7 %collective-permute-start.9 = (bf16[512,256]{1,0:T(8,128)(2,1)S(1)}, bf16[512,256]{1,0:T(8,128)(2,1)S(1)}, u32[]{:S(2)}, u32[]{:S(2)}) collective-permute-start(bf16[512,256]{1,0:T(8,128)(2,1)S(1)} %collective-permute-done.refs_0_), channel_id=1, source_target_pairs={{0,32},{32,0},{64,96},{96,64},{1,33},{33,1},{65,97},{97,65},{2,34}... | collective-permute-start | bytes 786440 | tf_op jit(solution)/shard_map/ppermute | solution.py:434
  33.5 19.1 %collective-permute-start.10 = (bf16[512,256]{1,0:T(8,128)(2,1)S(1)}, bf16[512,256]{1,0:T(8,128)(2,1)S(1)}, u32[]{:S(2)}, u32[]{:S(2)}) collective-permute-start(bf16[512,256]{1,0:T(8,128)(2,1)S(1)} %collective-permute-done.refs_0_), channel_id=1, source_target_pairs={{0,64},{32,96},{64,0},{96,32},{1,65},{33,97},{65,1},{97,33},{2,66}... | collective-permute-start | bytes 786440 | tf_op jit(solution)/shard_map/ppermute | solution.py:434
  34.8 17.9 %collective-permute-start.11 = (bf16[512,256]{1,0:T(8,128)(2,1)S(1)}, bf16[512,256]{1,0:T(8,128)(2,1)S(1)}, u32[]{:S(2)}, u32[]{:S(2)}) collective-permute-start(bf16[512,256]{1,0:T(8,128)(2,1)S(1)} %collective-permute-done.refs_0_), channel_id=1, source_target_pairs={{0,96},{32,64},{64,32},{96,0},{1,97},{33,65},{65,33},{97,1},{2,98}... | collective-permute-start | bytes 786440 | tf_op jit(solution)/shard_map/ppermute | solution.py:434
  42.1 6.8 %copy-start.13 = (s32[2,17]{1,0:T(2,128)S(1)}, s32[2,17]{1,0:T(2,128)}, u32[]{:S(2)}) copy-start(s32[2,17]{1,0:T(2,128)} %param.16) | copy-start | bytes 412
  52.7 10.3 %copy-start.9 = (bf16[512,256]{1,0:T(8,128)(2,1)}, bf16[512,256]{1,0:T(8,128)(2,1)S(1)}, u32[]{:S(2)}) copy-start(bf16[512,256]{1,0:T(8,128)(2,1)S(1)} %collective-permute-done.9.refs_1_) | copy-start | bytes 786436
  52.7 10.3 %copy-start.10 = (bf16[512,256]{1,0:T(8,128)(2,1)}, bf16[512,256]{1,0:T(8,128)(2,1)S(1)}, u32[]{:S(2)}) copy-start(bf16[512,256]{1,0:T(8,128)(2,1)S(1)} %collective-permute-done.10.refs_2_) | copy-start | bytes 786436
  52.7 10.3 %copy-start.11 = (bf16[512,256]{1,0:T(8,128)(2,1)}, bf16[512,256]{1,0:T(8,128)(2,1)S(1)}, u32[]{:S(2)}) copy-start(bf16[512,256]{1,0:T(8,128)(2,1)S(1)} %collective-permute-done.11.refs_3_) | copy-start | bytes 786436
  52.7 3.7 %collective-permute-start.16 = (f32[128,512]{1,0:T(8,128)}, f32[128,512]{1,0:T(8,128)S(1)}, u32[]{:S(2)}, u32[]{:S(2)}) collective-permute-start(f32[128,512]{1,0:T(8,128)} %get-tuple-element.80), channel_id=1, source_target_pairs={{0,16},{16,0},{1,17},{17,1},{2,18},{18,2},{3,19},{19,3},{4,20},{20... | collective-permute-start | bytes 786440 | tf_op jit(solution)/shard_map/ppermute | solution.py:434
  56.5 1.0 copy-start.2
  57.6 11.8 %collective-permute-start.17 = (bf16[128,512]{1,0:T(8,128)(2,1)S(1)}, bf16[128,512]{1,0:T(8,128)(2,1)S(1)}, u32[]{:S(2)}, u32[]{:S(2)}) collective-permute-start(bf16[128,512]{1,0:T(8,128)(2,1)S(1)} %kv_finish.1), channel_id=1, source_target_pairs={{0,128},{128,0},{1,129},{129,1},{2,130},{130,2},{3,131},{131,3},{4... | collective-permute-start | bytes 393224 | tf_op jit(solution)/shard_map/ppermute | solution.py:434
  63.0 6.2 %copy-start.14 = (s32[16]{0:T(128)S(1)}, s32[16]{0:T(128)}, u32[]{:S(2)}) copy-start(s32[16]{0:T(128)} %param.17) | copy-start | bytes 196
  63.0 7.9 %copy-start.3 = (bf16[1,256]{1,0:T(2,128)(2,1)S(1)}, bf16[1,256]{1,0:T(2,128)(2,1)}, u32[]{:S(2)}) copy-start(bf16[1,256]{1,0:T(2,128)(2,1)} %bias_ref.1) | copy-start | bytes 1540
  63.0 17.7 %copy-start.15 = (s32[16]{0:T(128)S(1)}, s32[16]{0:T(128)}, u32[]{:S(2)}) copy-start(s32[16]{0:T(128)} %param.15) | copy-start | bytes 196
  68.4 2.5 %collective-permute-start.12 = (f32[512,256]{1,0:T(8,128)}, f32[512,256]{1,0:T(8,128)S(1)}, u32[]{:S(2)}, u32[]{:S(2)}) collective-permute-start(f32[512,256]{1,0:T(8,128)} %get-tuple-element.73), channel_id=1, source_target_pairs={{0,16},{16,0},{1,17},{17,1},{2,18},{18,2},{3,19},{19,3},{4,20},{20... | collective-permute-start | bytes 1572872 | tf_op jit(solution)/shard_map/ppermute | solution.py:434
  69.4 11.2 %collective-permute-start.18 = (bf16[2,128,512]{2,1,0:T(8,128)(2,1)S(1)}, bf16[2,128,512]{2,1,0:T(8,128)(2,1)S(1)}, u32[]{:S(2)}, u32[]{:S(2)}) collective-permute-start(bf16[2,128,512]{2,1,0:T(8,128)(2,1)S(1)} %pad_maximum_fusion), channel_id=1, source_target_pairs={{0,1},{1,0},{2,3},{3,2},{4,5},{5,4},{6,7},{7,6},{8,9},{9,8},{10,11... | collective-permute-start | bytes 786440 | tf_op jit(solution)/shard_map/ppermute | solution.py:434
  70.9 1.0 copy-start.1
  72.7 3.5 %collective-permute-start.15 = (bf16[128,256]{1,0:T(8,128)(2,1)S(1)}, bf16[128,256]{1,0:T(8,128)(2,1)S(1)}, u32[]{:S(2)}, u32[]{:S(2)}) collective-permute-start(bf16[128,256]{1,0:T(8,128)(2,1)S(1)} %get-tuple-element.79), channel_id=1, source_target_pairs={{0,3},{1,2},{2,1},{3,0},{4,7},{5,6},{6,5},{7,4},{8,11},{9,10},{10,... | collective-permute-start | bytes 196616 | tf_op jit(solution)/shard_map/ppermute | solution.py:434
  72.8 6.1 %collective-permute-start.14 = (bf16[128,256]{1,0:T(8,128)(2,1)S(1)}, bf16[128,256]{1,0:T(8,128)(2,1)S(1)}, u32[]{:S(2)}, u32[]{:S(2)}) collective-permute-start(bf16[128,256]{1,0:T(8,128)(2,1)S(1)} %get-tuple-element.78), channel_id=1, source_target_pairs={{0,2},{1,3},{2,0},{3,1},{4,6},{5,7},{6,4},{7,5},{8,10},{9,11},{10,... | collective-permute-start | bytes 196616 | tf_op jit(solution)/shard_map/ppermute | solution.py:434
  75.0 5.6 %collective-permute-start.13 = (bf16[128,256]{1,0:T(8,128)(2,1)S(1)}, bf16[128,256]{1,0:T(8,128)(2,1)S(1)}, u32[]{:S(2)}, u32[]{:S(2)}) collective-permute-start(bf16[128,256]{1,0:T(8,128)(2,1)S(1)} %get-tuple-element.77), channel_id=1, source_target_pairs={{0,1},{1,0},{2,3},{3,2},{4,5},{5,4},{6,7},{7,6},{8,9},{9,8},{10,11... | collective-permute-start | bytes 196616 | tf_op jit(solution)/shard_map/ppermute | solution.py:434
  80.7 8.1 %collective-permute-start.19 = (bf16[2,128,512]{2,1,0:T(8,128)(2,1)S(1)}, bf16[2,128,512]{2,1,0:T(8,128)(2,1)S(1)}, u32[]{:S(2)}, u32[]{:S(2)}) collective-permute-start(bf16[2,128,512]{2,1,0:T(8,128)(2,1)S(1)} %pad_maximum_fusion.1.refs_0_), channel_id=1, source_target_pairs={{0,32},{32,0},{64,96},{96,64},{1,33},{33,1},{65,97},{97,65},{2,34}... | collective-permute-start | bytes 786440 | tf_op jit(solution)/shard_map/ppermute | solution.py:434
  81.0 12.5 %collective-permute-start.20 = (bf16[2,128,512]{2,1,0:T(8,128)(2,1)S(1)}, bf16[2,128,512]{2,1,0:T(8,128)(2,1)S(1)}, u32[]{:S(2)}, u32[]{:S(2)}) collective-permute-start(bf16[2,128,512]{2,1,0:T(8,128)(2,1)S(1)} %pad_maximum_fusion.1.refs_0_), channel_id=1, source_target_pairs={{0,64},{32,96},{64,0},{96,32},{1,65},{33,97},{65,1},{97,33},{2,66}... | collective-permute-start | bytes 786440 | tf_op jit(solution)/shard_map/ppermute | solution.py:434
  83.7 13.5 %collective-permute-start.21 = (bf16[2,128,512]{2,1,0:T(8,128)(2,1)S(1)}, bf16[2,128,512]{2,1,0:T(8,128)(2,1)S(1)}, u32[]{:S(2)}, u32[]{:S(2)}) collective-permute-start(bf16[2,128,512]{2,1,0:T(8,128)(2,1)S(1)} %pad_maximum_fusion.1.refs_0_), channel_id=1, source_target_pairs={{0,96},{32,64},{64,32},{96,0},{1,97},{33,65},{65,33},{97,1},{2,98}... | collective-permute-start | bytes 786440 | tf_op jit(solution)/shard_map/ppermute | solution.py:434
  84.9 12.3 %collective-permute-start.22 = (bf16[4,128,256]{2,1,0:T(8,128)(2,1)S(1)}, bf16[4,128,256]{2,1,0:T(8,128)(2,1)S(1)}, u32[]{:S(2)}, u32[]{:S(2)}) collective-permute-start(bf16[4,128,256]{2,1,0:T(8,128)(2,1)S(1)} %pad_maximum_fusion.5.refs_0_), channel_id=1, source_target_pairs={{0,4},{4,0},{8,12},{12,8},{1,5},{5,1},{9,13},{13,9},{2,6},{6,2},{1... | collective-permute-start | bytes 786440 | tf_op jit(solution)/shard_map/ppermute | solution.py:434
  86.2 11.5 %collective-permute-start.23 = (bf16[4,128,256]{2,1,0:T(8,128)(2,1)S(1)}, bf16[4,128,256]{2,1,0:T(8,128)(2,1)S(1)}, u32[]{:S(2)}, u32[]{:S(2)}) collective-permute-start(bf16[4,128,256]{2,1,0:T(8,128)(2,1)S(1)} %pad_maximum_fusion.5.refs_0_), channel_id=1, source_target_pairs={{0,8},{4,12},{8,0},{12,4},{1,9},{5,13},{9,1},{13,5},{2,10},{6,14},... | collective-permute-start | bytes 786440 | tf_op jit(solution)/shard_map/ppermute | solution.py:434
  88.8 13.4 %collective-permute-start.24 = (bf16[4,128,256]{2,1,0:T(8,128)(2,1)S(1)}, bf16[4,128,256]{2,1,0:T(8,128)(2,1)S(1)}, u32[]{:S(2)}, u32[]{:S(2)}) collective-permute-start(bf16[4,128,256]{2,1,0:T(8,128)(2,1)S(1)} %pad_maximum_fusion.5.refs_0_), channel_id=1, source_target_pairs={{0,12},{4,8},{8,4},{12,0},{1,13},{5,9},{9,5},{13,1},{2,14},{6,10},... | collective-permute-start | bytes 786440 | tf_op jit(solution)/shard_map/ppermute | solution.py:434
  103.5 11.4 %collective-permute-start.28 = (bf16[2,128,2048]{2,1,0:T(8,128)(2,1)S(1)}, bf16[2,128,2048]{2,1,0:T(8,128)(2,1)S(1)}, u32[]{:S(2)}, u32[]{:S(2)}) collective-permute-start(bf16[2,128,2048]{2,1,0:T(8,128)(2,1)S(1)} %assemble.1.near_ref), channel_id=1, source_target_pairs={{0,16},{16,0},{1,17},{17,1},{2,18},{18,2},{3,19},{19,3},{4,20},{20... | collective-permute-start | bytes 3145736 | tf_op jit(solution)/shard_map/ppermute | solution.py:434
  105.8 3.7 %collective-permute-start.25 = (bf16[128,256]{1,0:T(8,128)(2,1)S(1)}, bf16[128,256]{1,0:T(8,128)(2,1)S(1)}, u32[]{:S(2)}, u32[]{:S(2)}) collective-permute-start(bf16[128,256]{1,0:T(8,128)(2,1)S(1)} %get-tuple-element.87), channel_id=1, source_target_pairs={{0,1},{1,0},{2,3},{3,2},{4,5},{5,4},{6,7},{7,6},{8,9},{9,8},{10,11... | collective-permute-start | bytes 196616 | tf_op jit(solution)/shard_map/ppermute | solution.py:434
  106.4 4.1 %collective-permute-start.26 = (bf16[128,256]{1,0:T(8,128)(2,1)S(1)}, bf16[128,256]{1,0:T(8,128)(2,1)S(1)}, u32[]{:S(2)}, u32[]{:S(2)}) collective-permute-start(bf16[128,256]{1,0:T(8,128)(2,1)S(1)} %get-tuple-element.88), channel_id=1, source_target_pairs={{0,2},{1,3},{2,0},{3,1},{4,6},{5,7},{6,4},{7,5},{8,10},{9,11},{10,... | collective-permute-start | bytes 196616 | tf_op jit(solution)/shard_map/ppermute | solution.py:434
  106.9 8.0 %collective-permute-start.27 = (bf16[128,256]{1,0:T(8,128)(2,1)S(1)}, bf16[128,256]{1,0:T(8,128)(2,1)S(1)}, u32[]{:S(2)}, u32[]{:S(2)}) collective-permute-start(bf16[128,256]{1,0:T(8,128)(2,1)S(1)} %get-tuple-element.89), channel_id=1, source_target_pairs={{0,3},{1,2},{2,1},{3,0},{4,7},{5,6},{6,5},{7,4},{8,11},{9,10},{10,... | collective-permute-start | bytes 196616 | tf_op jit(solution)/shard_map/ppermute | solution.py:434
